TPU v7x, 32 devices: a whole 2x2x4 slice. The times are simulated.
32 devices in a mesh: grp: 2 (over y), freq: 16 (over z, x, core).
Axes of the slice: x: 2, y: 2, z: 4, core: 2. Of those that a mesh axis runs over, the one named last changes fastest.
Arguments:
- source_field: bfloat16 [4, 16, 512, 256], P('grp', 'freq'), parts along dimension 0, may hold values from -6 to 6
- receiver_field: bfloat16 [4, 16, 512, 256], P('grp', 'freq'), parts along dimension 0, may hold values from -6 to 6
- slowness_slabs: bfloat16 [32, 768, 512], P(('grp', 'freq')), parts along dimension 0, may hold values from 0.3984375 to 1.1953125
- slab_map: int32 [4], P('grp'), parts along dimension 0, may hold values from 0 to 15
- reference_gaps: float32 [4, 3], P('grp'), parts along dimension 0, may hold values from 0.1 to 0.3
- reference_index: int32 [4, 512, 256], P('grp'), parts along dimension 0, may hold values from 0 to 1
- frequency_bins: int32 [16], replicated, may hold values from 10 to 120
- shot_corner: int32 [4], P('grp'), parts along dimension 0, may hold values from 0 to 256
Outputs:
- image: float32 [4, 512, 256, 256], P('grp', 'freq'), parts along dimension 0
There are 2 independent parts, one for each index of `grp`. A program takes and returns all parts, laid end to end along the dimension named above; an argument that names none is the same for every part. Nothing has to cross between parts.
All inputs are finite; a program needn't handle non-finite values.
Results may differ from a plain program's by a relative error of at most 0.014.
Values may be sent and summed in bfloat16 or wider, within the bound.
No kernel may reach another device: no remote copies, remote signals or barrier semaphores. Data moves between devices by JAX's collectives and lax.ppermute only.
A program may use at most 128 MiB of HBM per device.

v0:
```python
import math

import jax
import jax.numpy as jnp
from jax import lax
from jax.sharding import PartitionSpec as P

LAGS = 256
DEPTHS = 2


cell_width = 0.0125
layer_thick = 0.0125
bin_hertz = 0.5
period_bins = 500
slow_base = 0.3


def spread(block, axis, holder):
    block = jnp.where(lax.axis_index(axis) == holder, block, jnp.zeros_like(block))
    return lax.psum(block, axis)


def transform_table(length, forward):
    grid_steps = jnp.arange(length, dtype=jnp.int32)
    phases = jnp.mod(grid_steps[:, None] * grid_steps[None, :], length).astype(jnp.float32)
    angles = phases * (2.0 * math.pi / length)
    norm_scale = 1.0 / math.sqrt(length)
    cosine = jnp.cos(angles) * norm_scale
    sine_part = jnp.sin(angles) * norm_scale
    if forward:
        cross_term = -sine_part
    else:
        cross_term = sine_part
    return jnp.stack([jnp.stack([cosine, cross_term]), jnp.stack([-cross_term, cosine])]).astype(
        jnp.bfloat16
    )


def wave_numbers(length):
    grid_steps = jnp.arange(length, dtype=jnp.int32)
    folded = jnp.where(grid_steps < length // 2, grid_steps, grid_steps - length).astype(
        jnp.float32
    )
    return folded * (2.0 * math.pi / (length * cell_width))


def lag_table(frequency_bins, lag_count):
    offsets = jnp.arange(lag_count, dtype=jnp.int32) - lag_count // 2
    cycles = jnp.mod(frequency_bins[:, None] * offsets[None, :], period_bins).astype(jnp.float32)
    angles = cycles * (2.0 * math.pi / period_bins)
    return jnp.stack([jnp.cos(angles), -jnp.sin(angles)]).astype(jnp.bfloat16)


def phase_factors(angular, references, squares):
    radicand = (angular * references[:, None, None]) ** 2 - squares[None]
    vertical = jnp.sqrt(jnp.maximum(radicand, 0.0))
    fading = jnp.exp(-jnp.sqrt(jnp.maximum(-radicand, 0.0)) * layer_thick)
    return (fading * jnp.cos(vertical * layer_thick), fading * jnp.sin(vertical * layer_thick))


def rotate(field_pair, turn_angle):
    return jnp.stack(
        [
            jnp.cos(turn_angle) * field_pair[:, 0] - jnp.sin(turn_angle) * field_pair[:, 1],
            jnp.cos(turn_angle) * field_pair[:, 1] + jnp.sin(turn_angle) * field_pair[:, 0],
        ],
        axis=1,
    )


def extrapolate(fields, angular, slowness, references, bracket, direction, tables, squares):
    forward_x, forward_y, inverse_x, inverse_y = tables
    half_done = jnp.einsum(
        "fcxy,cdyk->fdxk", fields, forward_y, preferred_element_type=jnp.float32
    ).astype(jnp.bfloat16)
    spectrum = jnp.einsum(
        "cdxk,fcxy->fdky", forward_x, half_done, preferred_element_type=jnp.float32
    )
    cos_part, sin_part = phase_factors(angular, references, squares)
    turned = direction[:, None, None, None] * sin_part[None]
    real_new = cos_part[None] * spectrum[:, None, 0] - turned * spectrum[:, None, 1]
    imag_new = cos_part[None] * spectrum[:, None, 1] + turned * spectrum[:, None, 0]
    shifted = jnp.stack([real_new, imag_new], axis=2).astype(jnp.bfloat16)
    returned = jnp.einsum(
        "cdxk,fjcxy->fjdky", inverse_x, shifted, preferred_element_type=jnp.float32
    ).astype(jnp.bfloat16)
    refocused = jnp.einsum(
        "fjcxy,cdyk->fjdxk", returned, inverse_y, preferred_element_type=jnp.float32
    )
    lower_pair = bracket == 0
    lower_field = jnp.where(lower_pair, refocused[:, 0], refocused[:, 1])
    upper_field = jnp.where(lower_pair, refocused[:, 1], refocused[:, 2])
    slow_low = jnp.where(lower_pair, references[0], references[1])
    slow_high = jnp.where(lower_pair, references[1], references[2])
    weight = jnp.clip((slowness - slow_low) / (slow_high - slow_low), 0.0, 1.0)
    turn_low = direction[:, None, None] * angular * layer_thick * (slowness - slow_low)[None]
    turn_high = direction[:, None, None] * angular * layer_thick * (slowness - slow_high)[None]
    mixed = (1.0 - weight) * rotate(lower_field, turn_low) + weight * rotate(upper_field, turn_high)
    return mixed.astype(jnp.bfloat16)


def lag_image_depths(cross_spec, lag_weights):
    total_bins = cross_spec.shape[2]
    summed = jnp.einsum(
        "dcwab,cwl->dabl", cross_spec, lag_weights, preferred_element_type=jnp.float32
    )
    return summed * total_bins ** (-0.5)


def cross_product(wave_stack):
    values = wave_stack.astype(jnp.float32)
    real_part = values[0, 0] * values[1, 0] + values[0, 1] * values[1, 1]
    imag_part = values[0, 0] * values[1, 1] - values[0, 1] * values[1, 0]
    return jnp.stack([real_part, imag_part]).astype(jnp.bfloat16)


def shards(
    source_field,
    receiver_field,
    slowness_slabs,
    slab_map,
    reference_gaps,
    reference_index,
    frequency_bins,
    shot_corner,
):
    slots_here = source_field.shape[1]
    rows_x = source_field.shape[2]
    cols_y = source_field.shape[3]
    tables = (
        transform_table(rows_x, True),
        transform_table(cols_y, True),
        transform_table(rows_x, False),
        transform_table(cols_y, False),
    )
    wave_x = wave_numbers(rows_x)
    wave_y = wave_numbers(cols_y)
    squares = wave_x[:, None] ** 2 + wave_y[None, :] ** 2
    freq_rank = lax.axis_index("freq")
    my_bins = lax.dynamic_slice_in_dim(frequency_bins, freq_rank * slots_here, slots_here)
    omegas = my_bins.astype(jnp.float32) * (2.0 * math.pi * bin_hertz)
    lag_weights = lag_table(frequency_bins, LAGS)
    direction = jnp.array([1.0, -1.0], jnp.float32)
    wave_stack = jnp.stack([source_field, receiver_field])
    slab_count = slowness_slabs.shape[0]
    corner_x = shot_corner[0]
    corner_y = shot_corner[1]
    crosses = []
    for depth_step in range(DEPTHS):
        global_slab = slab_map[depth_step]
        owner_rank = global_slab // slab_count
        local_pick = global_slab % slab_count
        own_window = lax.dynamic_slice(
            slowness_slabs, (local_pick, corner_x, corner_y), (1, rows_x, cols_y)
        )[0]
        window = spread(own_window, "freq", owner_rank)
        slowness = window.astype(jnp.float32)
        references = slow_base + jnp.cumsum(reference_gaps[depth_step])
        bracket = reference_index[depth_step]
        stepped = [
            extrapolate(
                wave_stack[:, :, 0],
                omegas[0],
                slowness,
                references,
                bracket,
                direction,
                tables,
                squares,
            )
        ]
        wave_stack = jnp.stack(stepped, axis=2)
        crosses.append(cross_product(wave_stack))
    all_crosses = jnp.stack(crosses)
    return lag_image_depths(
        lax.all_to_all(all_crosses, "freq", split_axis=3, concat_axis=2, tiled=True), lag_weights
    )


def solution(mesh):
    placed = (
        P("grp", "freq", None, None),
        P("grp", "freq", None, None),
        P(("grp", "freq"), None, None),
        P("grp"),
        P("grp", None),
        P("grp", None, None),
        P(),
        P("grp"),
    )
    return jax.shard_map(
        shards, mesh=mesh, in_specs=placed, out_specs=P("grp", "freq", None, None), check_vma=False
    )
```

profile of v0, /device:TPU:0, one launch (start us, length us, event | category | flops | bytes accessed | tf_op | source)
XLA Modules:
  0.0 219.7 jit_solution(4472801695292932038)
XLA Ops:
  6.5 1.3 fusion.162
  14.3 2.0 select_bitcast_fusion
  16.3 4.4 %negate_convert_fusion = (bf16[1,512,512]{2,1,0:T(8,128)(2,1)S(1)}, bf16[1,512,512]{2,1,0:T(8,128)(2,1)S(1)}) fusion(), kind=kLoop, calls=%fused_computation.150 | loop fusion | flops 4980736 | bytes 1048576 | tf_op jit(solution)/shard_map/convert.25
  20.7 4.0 %fusion.115 = bf16[1,512,512]{2,1,0:T(8,128)(2,1)S(1)} fusion(), kind=kLoop, calls=%fused_computation.157 | loop fusion | flops 4194304 | bytes 524288 | tf_op jit(solution)/shard_map/convert.21
  28.5 1.8 fusion.89
  31.3 3.7 %convolution_bitcast_fusion.1 = f32[2,2,512,256]{2,3,1,0:T(8,128)S(1)} fusion(bf16[1,2,512,512]{3,2,0,1:T(8,128)(2,1)S(1)} %get-tuple-element.38, bf16[1,2,512,512]{3,2,0,1:T(8,128)(2,1)} %get-tuple-element.49, bf16[1,2,1,512,256]{4,3,1,0,2:T(8,128)(2,1)} %bitcast.250, bf16[1,2,1,512,256]{4,3,1,0,2:T(8,128)(2,1)} %bitcast.251, ...), kind=kOutput, calls=%fused_computation.63 | convolution fusion | flops 1618477056 | bytes 5767168 | tf_op jit(solution)/shard_map/cdxk,fcxy->fdky/dot_general | solution.py:77
  35.9 14.4 %fusion.59 = (f32[3,512,256]{1,2,0:T(8,128)}, f32[3,512,256]{1,2,0:T(8,128)}, f32[3,512,256]{1,2,0:T(8,128)S(1)}, f32[3,512,256]{1,2,0:T(8,128)S(1)}) fusion(f32[3]{0:T(128)S(1)} %get-tuple-element.73, f32[512,256]{0,1:T(8,128)S(1)} %broadcast_add_fusion, f32[3]{0:T(128)S(1)} %get-tuple-element.85), kind=kLoop, calls=%fused_computation.81 | loop fusion | flops 7077888 | bytes 6815768 | tf_op jit(solution)/shard_map/mul | solution.py:59
  51.5 9.4 %fusion.27 = f32[2,3,2,512,256]{3,4,1,0,2:T(8,128)} fusion(bf16[2,3,1,512,256]{3,4,2,1,0:T(8,128)(2,1)S(1)} %get-tuple-element.18, bf16[2,3,1,512,256]{3,4,2,1,0:T(8,128)(2,1)S(1)} %get-tuple-element.17, bf16[1,2,512,512]{3,2,1,0:T(8,128)(2,1)} %get-tuple-element.50, bf16[1,2,512,512]{3,2,1,0:T(8,128)(2,1)} %get-tuple-element.37, ...), kind=kOutput, calls=%fused_computation.31 | convolution fusion | flops 4844158976 | bytes 12058624 | tf_op jit(solution)/shard_map/fjcxy,cdyk->fjdxk/dot_general | solution.py:88
  61.5 47.6 %all-reduce.3.cloned.1.call-done = (bf16[512,256]{1,0:T(8,128)(2,1)}, bf16[512,256]{1,0:T(8,128)(2,1)}) async-done(((bf16[512,256]{1,0:T(8,128)(2,1)}, bf16[512,256]{1,0:T(8,128)(2,1)}), (bf16[512,256]{1,0:T(8,128)(2,1)}, bf16[512,256]{1,0:T(8,128)(2,1)})) %all-reduce.3.cloned.1.call-update) | async-done | bytes 524304 | tf_op jit(solution)/shard_map/psum | solution.py:21
  109.2 6.4 %broadcast_subtract_fusion = (f32[512,256]{1,0:T(8,128)}, pred[512,256]{1,0:T(8,128)(4,1)S(1)}, f32[512,256]{1,0:T(8,128)S(1)}, pred[512,256]{1,0:T(8,128)(4,1)S(1)}) fusion(f32[]{:T(128)} %bitcast.64, f32[]{:T(128)} %bitcast.63, f32[]{:T(128)} %bitcast.62, bf16[512,256]{1,0:T(8,128)(2,1)} %get-tuple-element.6, s32[2,512,256]{2,1,0:T(8,128)} %param.14, ...), kind=kLoop, calls=%fused_computation.202 | loop fusion | flops 2359296 | bytes 2883608 | tf_op jit(solution)/shard_map/sub | solution.py:99
  115.8 2.2 select_subtract_fusion.5
  118.2 3.1 %fusion.121 = (f32[512,256]{1,0:T(8,128)}, f32[512,256]{1,0:T(8,128)}, f32[512,256]{1,0:T(8,128)}) fusion(pred[512,256]{1,0:T(8,128)(4,1)S(1)} %get-tuple-element.8, f32[]{:T(128)} %bitcast.64, f32[]{:T(128)} %bitcast.63, f32[]{:T(128)} %bitcast.62, bf16[512,256]{1,0:T(8,128)(2,1)S(1)} %copy-done.9), kind=kLoop, calls=%fused_computation.167 | loop fusion | flops 1048576 | bytes 1966092 | tf_op jit(solution)/shard_map/jit(clip)/min | solution.py:96
  125.4 3.7 %fusion.35 = (f32[2,2,512,256]{2,3,0,1:T(8,128)S(1)}, f32[2,2,512,256]{2,3,0,1:T(8,128)S(1)}) fusion(f32[2,3,2,512,256]{3,4,1,0,2:T(8,128)} %fusion.27, pred[512,256]{0,1:T(8,128)(4,1)S(1)} %copy.57), kind=kLoop, calls=%fused_computation.45 | loop fusion | flops 1048576 | bytes 10616832 | tf_op jit(solution)/shard_map/jit(_where)/select_n | solution.py:92
  129.2 9.0 %fusion.100 = (f32[2,1,512,256]{2,3,0,1:T(8,128)S(1)}, f32[2,1,512,256]{2,3,0,1:T(8,128)S(1)}, f32[2,1,512,256]{2,3,0,1:T(8,128)S(1)}, f32[2,1,512,256]{2,3,0,1:T(8,128)}) fusion(f32[2,2,512,256]{2,3,0,1:T(8,128)S(1)} %get-tuple-element.13, f32[512,256]{0,1:T(8,128)S(1)} %copy-done, f32[2]{0:T(128)S(1)} %multiply_multiply_fusion.4, ...), kind=kLoop, calls=%fused_computation.133 | loop fusion | flops 3670016 | bytes 9437192 | tf_op jit(solution)/shard_map/sub | solution.py:65
  138.2 5.6 %convolution_bitcast_fusion = f32[2,2,512,256]{2,3,1,0:T(8,128)} fusion(bf16[1,2,512,512]{3,2,0,1:T(8,128)(2,1)} %copy-done.14, bf16[1,2,512,512]{3,2,0,1:T(8,128)(2,1)} %get-tuple-element.49, bf16[1,2,256,256]{2,3,0,1:T(8,128)(2,1)} %get-tuple-element.58, bf16[1,2,256,256]{2,3,0,1:T(8,128)(2,1)} %get-tuple-element.61, ...), kind=kOutput, calls=%fused_computation.62 | convolution fusion | flops 1619525632 | bytes 9961472 | tf_op jit(solution)/shard_map/cdxk,fcxy->fdky/dot_general | solution.py:77
  143.8 2.1 fusion.106
  151.0 3.6 %fusion.11 = bf16[2,3,2,512,256,1]{3,4,2,1,0,5:T(8,128)(2,1)S(1)} fusion(bf16[2,3,1,512,256]{3,4,2,1,0:T(8,128)(2,1)S(1)} %get-tuple-element.16, bf16[2,3,1,512,256]{3,4,2,1,0:T(8,128)(2,1)S(1)} %get-tuple-element.15, bf16[1,2,512,512]{3,2,1,0:T(8,128)(2,1)S(1)} %copy-done.13, bf16[1,2,512,512]{3,2,1,0:T(8,128)(2,1)S(1)} %copy-done.12), kind=kOutput, calls=%fused_computation.17 | convolution fusion | flops 3233284096 | bytes 8388608 | tf_op jit(solution)/shard_map/cdxk,fjcxy->fjdky/dot_general | solution.py:85
  154.6 4.5 %fusion.24 = f32[2,3,2,512,256]{3,4,0,2,1:T(8,128)} fusion(bf16[2,3,2,512,256,1]{3,4,2,1,0,5:T(8,128)(2,1)S(1)} %fusion.11, bf16[1,2,256,256]{2,3,1,0:T(8,128)(2,1)S(1)} %copy-done.11, bf16[1,2,256,256]{2,3,1,0:T(8,128)(2,1)S(1)} %get-tuple-element.57), kind=kOutput, calls=%fused_computation.30 | convolution fusion | flops 1610874880 | bytes 9961472 | tf_op jit(solution)/shard_map/fjcxy,cdyk->fjdxk/dot_general | solution.py:88
  160.6 3.7 %fusion.33 = (f32[2,2,512,256]{2,3,0,1:T(8,128)S(1)}, f32[2,2,512,256]{2,3,0,1:T(8,128)S(1)}) fusion(f32[2,3,2,512,256]{3,4,0,2,1:T(8,128)} %fusion.24, pred[512,256]{0,1:T(8,128)(4,1)S(1)} %copy.69), kind=kLoop, calls=%fused_computation.40 | loop fusion | flops 1048576 | bytes 10616832 | tf_op jit(solution)/shard_map/jit(_where)/select_n | solution.py:92
  164.3 8.0 %fusion.95 = (f32[2,1,1,512,256]{3,4,0,2,1:T(8,128)S(1)}, f32[2,1,1,512,256]{3,4,0,2,1:T(8,128)S(1)}, f32[2,1,1,512,256]{3,4,0,2,1:T(8,128)S(1)}, f32[2,1,1,512,256]{3,4,0,2,1:T(8,128)S(1)}) fusion(f32[2,2,512,256]{2,3,0,1:T(8,128)S(1)} %get-tuple-element.11, f32[512,256]{0,1:T(8,128)S(1)} %copy.68, f32[2]{0:T(128)S(1)} %multiply_multiply_fusion.4, ...), kind=kLoop, calls=%fused_computation.128 | loop fusion | flops 3670016 | bytes 9437192 | tf_op jit(solution)/shard_map/stack | solution.py:63
  174.0 2.1 copy.79
  176.1 5.3 %all-to-all-start = ((bf16[2,2,1,512,256]{4,0,2,1,3:T(2,128)(2,1)}), bf16[2,2,1,512,256]{4,0,2,1,3:T(2,128)(2,1)S(1)}, u32[]{:S(2)}, u32[]{:S(2)}) async-start(bf16[2,2,1,512,256]{4,0,2,1,3:T(2,128)(2,1)} %copy.79), calls=%async_computation | async-start | bytes 2097152 | tf_op jit(solution)/shard_map/all_to_all | solution.py:177
  181.5 22.8 %all-to-all-done = bf16[2,2,1,512,256]{4,0,2,1,3:T(2,128)(2,1)S(1)} async-done(((bf16[2,2,1,512,256]{4,0,2,1,3:T(2,128)(2,1)}), bf16[2,2,1,512,256]{4,0,2,1,3:T(2,128)(2,1)S(1)}, u32[]{:S(2)}, u32[]{:S(2)}) %all-to-all-start) | async-done | bytes 1048608 | tf_op jit(solution)/shard_map/all_to_all | solution.py:177
  204.3 8.6 %bitcast_multiply_fusion = f32[2,32,256,256]{3,2,1,0:T(8,128)} fusion(bf16[2,2,16,32,256]{4,0,1,3,2:T(2,128)(2,1)S(1)} %bitcast.249, bf16[1,16,256]{2,1,0:T(8,128)(2,1)S(1)} %get-tuple-element.64, bf16[1,16,256]{2,1,0:T(8,128)(2,1)S(1)} %get-tuple-element.63), kind=kOutput, calls=%fused_computation | convolution fusion | flops 272637952 | bytes 17842176 | tf_op jit(solution)/shard_map/dcwab,cwl->dabl/dot_general | solution.py:105
  (75 shorter events, 21.0 us)
Async XLA Ops:
  6.5 20.3 %copy-start.18 = (s32[16]{0:T(128)S(1)}, s32[16]{0:T(128)}, u32[]{:S(2)}) copy-start(s32[16]{0:T(128)} %param.15) | copy-start | bytes 196
  6.5 21.6 %copy-start.17 = (f32[2,3]{1,0:T(2,128)S(1)}, f32[2,3]{1,0:T(2,128)}, u32[]{:S(2)}) copy-start(f32[2,3]{1,0:T(2,128)} %param.13) | copy-start | bytes 76
  6.5 102.6 %all-reduce.3.cloned.1.call-start = ((), (), s32[]{:S(2)}) async-start(), calls=%async_computation.1 | async-start | bytes 1048576 | tf_op jit(solution)/shard_map/psum | solution.py:21
  30.3 4.7 %copy-start.14 = (bf16[1,2,512,512]{3,2,0,1:T(8,128)(2,1)}, bf16[1,2,512,512]{3,2,0,1:T(8,128)(2,1)S(1)}, u32[]{:S(2)}) copy-start(bf16[1,2,512,512]{3,2,0,1:T(8,128)(2,1)S(1)} %get-tuple-element.38) | copy-start | bytes 3145732
  35.9 14.4 %copy-start.16 = (f32[2]{0:T(128)S(1)}, f32[2]{0:T(128)}, u32[]{:S(2)}) copy-start(f32[2]{0:T(128)} %constant.135.clone) | copy-start | bytes 28
  109.2 6.7 %copy-start.10 = (bf16[512,256]{1,0:T(8,128)(2,1)S(1)}, bf16[512,256]{1,0:T(8,128)(2,1)}, u32[]{:S(2)}) copy-start(bf16[512,256]{1,0:T(8,128)(2,1)} %get-tuple-element.5) | copy-start | bytes 786436
  109.2 9.1 %copy-start.9 = (bf16[512,256]{1,0:T(8,128)(2,1)S(1)}, bf16[512,256]{1,0:T(8,128)(2,1)}, u32[]{:S(2)}) copy-start(bf16[512,256]{1,0:T(8,128)(2,1)} %get-tuple-element.6) | copy-start | bytes 786436
  125.4 3.7 %copy-start = (f32[512,256]{0,1:T(8,128)S(1)}, f32[512,256]{0,1:T(8,128)}, u32[]{:S(2)}) copy-start(f32[512,256]{0,1:T(8,128)} %copy.56) | copy-start | bytes 1572868
  125.4 3.8 %copy-start.1 = (f32[512,256]{0,1:T(8,128)S(1)}, f32[512,256]{0,1:T(8,128)}, u32[]{:S(2)}) copy-start(f32[512,256]{0,1:T(8,128)} %copy.66) | copy-start | bytes 1572868
  145.9 1.7 copy-start.2
  147.6 1.4 copy-start.7
  147.6 1.9 copy-start.8
  149.5 1.2 copy-start.12
  149.5 1.5 copy-start.13
  151.0 3.6 %copy-start.11 = (bf16[1,2,256,256]{2,3,1,0:T(8,128)(2,1)S(1)}, bf16[1,2,256,256]{2,3,1,0:T(8,128)(2,1)}, u32[]{:S(2)}) copy-start(bf16[1,2,256,256]{2,3,1,0:T(8,128)(2,1)} %get-tuple-element.62) | copy-start | bytes 786436
  154.6 4.5 %copy-start.6 = (f32[512,256]{1,0:T(8,128)S(1)}, f32[512,256]{1,0:T(8,128)}, u32[]{:S(2)}) copy-start(f32[512,256]{1,0:T(8,128)} %get-tuple-element.53) | copy-start | bytes 1572868
  154.6 4.7 %copy-start.5 = (f32[512,256]{1,0:T(8,128)S(1)}, f32[512,256]{1,0:T(8,128)}, u32[]{:S(2)}) copy-start(f32[512,256]{1,0:T(8,128)} %get-tuple-element.52) | copy-start | bytes 1572868
  159.2 1.0 copy-start.4
  159.2 1.2 copy-start.3
  172.9 1.0 copy-start.15
  176.1 28.2 %all-to-all-start = ((bf16[2,2,1,512,256]{4,0,2,1,3:T(2,128)(2,1)}), bf16[2,2,1,512,256]{4,0,2,1,3:T(2,128)(2,1)S(1)}, u32[]{:S(2)}, u32[]{:S(2)}) async-start(bf16[2,2,1,512,256]{4,0,2,1,3:T(2,128)(2,1)} %copy.79), calls=%async_computation | async-start | bytes 2097152 | tf_op jit(solution)/shard_map/all_to_all | solution.py:177
Sparse Core Ops, SparseCore 0:
  16.4 92.6 all-reduce.2
where the time goes:
time: 222 us; the launch traced here: 220 us
  other arithmetic  72.8 us (33%)
  waiting for transfers between devices  70.4 us (32%)
  matrix products  35.3 us (16%)
  between operations  19.5 us (9%)
  local copies, waits for them, and re-layouts  16.4 us (7%)
  starting transfers between devices  5.27 us (2%)
    psum x1, waiting for transfers between devices, spread(): return lax.psum(block, axis)  47.6 us
    all_to_all x1, waiting for transfers between devices, shards(): lax.all_to_all(all_crosses, 'freq', split_axis=3, concat_axis=2, tiled=True)  22.8 us
    another operation x11, other arithmetic  14.5 us
    mul x1, other arithmetic, phase_factors(): fading * jnp.cos(vertical * layer_thick)  14.4 us
    dot_general x2, matrix products, extrapolate(): jnp.einsum('fjcxy,cdyk->fjdxk', returned, inverse_y, preferred_element_ty...  13.9 us
    dot_general x2, matrix products, extrapolate(): jnp.einsum('cdxk,fcxy->fdky', forward_x, half_done, preferred_element_typ...  9.22 us
    sub x1, other arithmetic, rotate(): jnp.cos(turn_angle) * field_pair[:, 0]  9.01 us
    dot_general x1, matrix products, lag_image_depths(): jnp.einsum('dcwab,cwl->dabl', cross_spec, lag_weights, preferred_element_...  8.56 us
  transfers between devices with their start and end apart: 2, of which 2 were waited for; matrix products, arithmetic and copies ran while one was open for 20% of the time, Pallas kernels for 0%

commit v1 on v0

v1 whole, which is shorter than its diff:
```python
import functools
import math

import jax
import jax.numpy as jnp
import numpy as np
from jax import lax
from jax.experimental import pallas as pl
from jax.experimental.pallas import tpu as pltpu
from jax.sharding import PartitionSpec as P

LAGS = 256

cell_width = 0.0125
layer_thick = 0.0125
bin_hertz = 0.5
period_bins = 500
slow_base = 0.3

VMEM = pltpu.VMEM
SMEM = pltpu.SMEM
f32 = jnp.float32
bf16 = jnp.bfloat16


def real_table(length):
    half = length // 2
    steps = np.arange(length, dtype=np.int64)
    wave = np.concatenate([np.arange(half), [half], np.arange(1, half)])
    phases = np.mod(steps[:, None] * wave[None, :], length).astype(np.float32)
    angles = phases * np.float32(2.0 * math.pi / length)
    scale = np.float32(1.0 / math.sqrt(length))
    is_cos = np.arange(length) <= half
    table = np.where(is_cos[None, :], np.cos(angles), np.sin(angles)) * scale
    twice = np.where((wave == 0) | (wave == half), 1.0, 2.0)
    forward = jnp.asarray(table.astype(np.float32)).astype(bf16)
    inverse = (forward.astype(f32) * jnp.asarray(twice[None, :], f32)).astype(bf16)
    return forward, inverse


def sin_cos(angle):
    turns = jnp.floor(angle * (2.0 / math.pi) + 0.5)
    rest = angle - turns * 1.5707397460937500
    rest = rest - turns * 5.6580702948965924e-05
    quadrant = turns.astype(jnp.int32)
    square = rest * rest
    sine = rest + rest * square * (
        -1.6666654611e-1 + square * (8.3321608736e-3 - square * 1.9515295891e-4)
    )
    cosine = (
        1.0
        - 0.5 * square
        + square
        * square
        * (4.166664568298827e-2 + square * (-1.388731625493765e-3 + square * 2.443315711809948e-5))
    )
    odd = (quadrant & 1) == 1
    out_sin = jnp.where(odd, cosine, sine)
    out_cos = jnp.where(odd, sine, cosine)
    out_sin = jnp.where((quadrant & 2) == 2, -out_sin, out_sin)
    out_cos = jnp.where(((quadrant + 1) & 2) == 2, -out_cos, out_cos)
    return out_sin, out_cos


def references_of(gaps_ref, depth):
    first = slow_base + gaps_ref[depth, 0]
    second = first + gaps_ref[depth, 1]
    third = second + gaps_ref[depth, 2]
    return first, second, third


def angular_of(bins_ref):
    return bins_ref[lax.axis_index("freq")].astype(f32) * (2.0 * math.pi * bin_hertz)


def phase_block(reach, base_turn, squares):
    radicand = reach - squares
    root = jnp.sqrt(jnp.abs(radicand)) * layer_thick
    travelling = radicand > 0.0
    fading = jnp.where(travelling, 1.0, jnp.exp(-root))
    sine, cosine = sin_cos(jnp.where(travelling, root, 0.0) - base_turn)
    return fading * cosine, fading * sine


def make_phases(cos_ref, sin_ref, angular, reference):
    rows, cols = cos_ref.shape
    half = rows // 2
    reach = (angular * reference) * (angular * reference)
    base_turn = angular * layer_thick * reference
    step_x = 2.0 * math.pi / (rows * cell_width)
    step_y = 2.0 * math.pi / (cols * cell_width)
    lane = lax.broadcasted_iota(jnp.int32, (8, cols), 1)
    wave_y = jnp.where(lane <= cols // 2, lane, lane - cols // 2).astype(f32) * step_y
    square_y = wave_y * wave_y
    tall = 64

    def body(block, carry):
        start = pl.multiple_of(block * tall, tall)
        row = lax.broadcasted_iota(jnp.int32, (tall, cols), 0) + start
        wave_x = row.astype(f32) * step_x
        cosine, sine = phase_block(
            reach, base_turn, wave_x * wave_x + jnp.concatenate([square_y] * (tall // 8), axis=0)
        )
        cos_ref[pl.ds(start, tall), :] = cosine
        sin_ref[pl.ds(start, tall), :] = sine
        cos_ref[pl.ds(half + start, tall), :] = cosine
        sin_ref[pl.ds(half + start, tall), :] = sine
        return carry

    lax.fori_loop(0, half // tall, body, 0)
    edge = (half * step_x) ** 2
    cosine, sine = phase_block(reach, base_turn, edge + square_y)
    top = lax.broadcasted_iota(jnp.int32, (8, cols), 0) == 0
    cos_ref[half : half + 8, :] = jnp.where(top, cosine, cos_ref[half : half + 8, :])
    sin_ref[half : half + 8, :] = jnp.where(top, sine, sin_ref[half : half + 8, :])


def dot(left, right):
    return jnp.dot(left, right, preferred_element_type=f32)


def march(
    wave_ref, angular, references, tables, half_ref, spec_ref, cos_ref, sin_ref, shift_ref, out_ref
):
    forward_x, forward_y, inverse_x = tables
    for plane in range(4):
        half_ref[plane] = dot(wave_ref[plane], forward_y[...]).astype(bf16)
    for plane in range(4):
        spec_ref[plane] = dot(forward_x[...], half_ref[plane])
    for j in range(3):
        make_phases(cos_ref.at[j], sin_ref.at[j], angular, references[j])
    for j in range(3):
        for field in range(2):
            real, imag = spec_ref[2 * field], spec_ref[2 * field + 1]
            cosine, sine = cos_ref[j], sin_ref[j]
            shift_ref[j, 2 * field] = (cosine * real - sine * imag).astype(bf16)
            shift_ref[j, 2 * field + 1] = (cosine * imag + sine * real).astype(bf16)
        for plane in range(4):
            out_ref[j, plane] = dot(inverse_x[...], shift_ref[j, plane]).astype(bf16)


def blend(
    returned_ref, slow_ref, bracket_ref, depth, angular, references, inverse_y, wave_ref, cross_ref
):
    rows, cols = slow_ref.shape[1:]
    tile = cross_ref.shape[3]
    tall = max(tile, 64)
    low, mid, high = references
    ones = jnp.ones((8, cols), f32)
    slope_low = (1.0 / (ones * (mid - low)))[:1]
    slope_high = (1.0 / (ones * (high - mid)))[:1]

    def body(block, carry):
        start = pl.multiple_of(block * tall, tall)
        here = pl.ds(start, tall)
        slow = slow_ref[depth, here, :].astype(f32)
        lower = bracket_ref[depth, here, :] == 0
        weight = jnp.where(lower, (slow - low) * slope_low, (slow - mid) * slope_high)
        weight = jnp.minimum(jnp.maximum(weight, 0.0), 1.0)
        sine, cosine = sin_cos(slow * (angular * layer_thick))
        halves = []
        for plane in range(4):
            parts = [dot(returned_ref[j, plane, here, :], inverse_y[...]) for j in range(3)]
            bottom = jnp.where(lower, parts[0], parts[1])
            top = jnp.where(lower, parts[1], parts[2])
            halves.append(bottom + weight * (top - bottom))
        fresh = []
        for field in range(2):
            real, imag = halves[2 * field], halves[2 * field + 1]
            fresh.append((cosine * real - sine * imag).astype(bf16))
            fresh.append((cosine * imag + sine * real).astype(bf16))
        for plane in range(4):
            wave_ref[plane, here, :] = fresh[plane]
        s_real, s_imag, r_real, r_imag = [value.astype(f32) for value in fresh]
        cross_real = (s_real * r_real - s_imag * r_imag).astype(bf16)
        cross_imag = (s_real * r_imag + s_imag * r_real).astype(bf16)
        for part in range(tall // tile):
            spot = block * (tall // tile) + part
            cross_ref[spot, depth, 0] = cross_real[part * tile : (part + 1) * tile]
            cross_ref[spot, depth, 1] = cross_imag[part * tile : (part + 1) * tile]
        return carry

    lax.fori_loop(0, rows // tall, body, 0)


def window_kernel(map_ref, corner_ref, slab_ref, keep_ref, send_ref, turned_ref, *, slab_count):
    depth = pl.program_id(0)
    rank = lax.axis_index("freq")
    core, side = rank % 2, (rank // 2) % 2
    quarter, cols = keep_ref.shape[2:]
    wide = slab_ref.shape[2]
    turn = lax.rem(wide - corner_ref[1], wide)
    turned_ref[: slab_ref.shape[1], :] = pltpu.roll(slab_ref[0].astype(f32), turn, 1)[:, :cols]
    mine = map_ref[depth] // slab_count == rank
    above = lax.rem(corner_ref[0], 8)
    first_row = corner_ref[0] - above
    tall = quarter + 8
    for other_core in range(2):
        target = keep_ref if other_core == 0 else send_ref
        for other_side in range(2):
            spot = 2 * ((core + other_core) % 2) + (side + other_side) % 2
            block = turned_ref[pl.ds(pl.multiple_of(first_row + spot * quarter, 8), tall), :]
            block = pltpu.roll(block, lax.rem(tall - above, tall), 0)[:quarter]
            target[other_side, 0] = jnp.where(mine, block, 0.0).astype(bf16)


def first_kernel(
    bins_ref,
    gaps_ref,
    source_ref,
    receiver_ref,
    forward_x,
    forward_y,
    inverse_x,
    out_ref,
    wave_ref,
    half_ref,
    spec_ref,
    cos_ref,
    sin_ref,
    shift_ref,
):
    wave_ref[0] = source_ref[0, 0]
    wave_ref[1] = source_ref[1, 0]
    wave_ref[2] = receiver_ref[0, 0]
    wave_ref[3] = -receiver_ref[1, 0]
    march(
        wave_ref,
        angular_of(bins_ref),
        references_of(gaps_ref, 0),
        (forward_x, forward_y, inverse_x),
        half_ref,
        spec_ref,
        cos_ref,
        sin_ref,
        shift_ref,
        out_ref,
    )


def second_kernel(
    bins_ref,
    gaps_ref,
    returned_ref,
    quarter_refs,
    bracket_ref,
    forward_x,
    forward_y,
    inverse_x,
    inverse_y,
    cross_ref,
    slow_ref,
    wave_ref,
    half_ref,
    spec_ref,
    cos_ref,
    sin_ref,
    shift_ref,
    later_ref,
    *,
    depths,
):
    rank = lax.axis_index("freq")
    core, side = rank % 2, (rank // 2) % 2
    quarter = quarter_refs[0].shape[1]
    for index, (other_core, other_side) in enumerate(((0, 0), (0, 1), (1, 0), (1, 1))):
        spot = 2 * ((core + other_core) % 2) + (side + other_side) % 2
        start = pl.multiple_of(spot * quarter, quarter)
        for depth in range(depths):
            slow_ref[depth, pl.ds(start, quarter), :] = quarter_refs[index][depth]
    angular = angular_of(bins_ref)
    for depth in range(depths):
        references = references_of(gaps_ref, depth)
        if depth:
            march(
                wave_ref,
                angular,
                references,
                (forward_x, forward_y, inverse_x),
                half_ref,
                spec_ref,
                cos_ref,
                sin_ref,
                shift_ref,
                later_ref,
            )
        blend(
            later_ref if depth else returned_ref,
            slow_ref,
            bracket_ref,
            depth,
            angular,
            references,
            inverse_y,
            wave_ref,
            cross_ref,
        )


def image_kernel(cross_ref, lag_ref, out_ref, weight_ref, *, scale):
    bins, _, pair, tall, cols = cross_ref.shape
    depth_of = bins * pair * tall
    lags = lag_ref.shape[2]

    @pl.when((pl.program_id(0) == 0) & (pl.program_id(1) == 0))
    def _():
        table = jnp.broadcast_to(
            lag_ref[...].reshape(bins * pair, 1, lags), (bins * pair, tall, lags)
        ).reshape(depth_of, lags)
        place = lax.broadcasted_iota(jnp.int32, (depth_of, lags), 0) % tall
        for row in range(tall):
            weight_ref[:, row * lags : (row + 1) * lags] = jnp.where(
                place == row, table, 0.0
            ).astype(bf16)

    left = cross_ref[...].astype(f32).reshape(depth_of, cols).T.astype(bf16)
    for row in range(tall):
        out_ref[0, row] = dot(left, weight_ref[:, row * lags : (row + 1) * lags]) * scale


def plain(shape_list):
    return [pl.BlockSpec(memory_space=VMEM) for _ in range(shape_list)]


def shards(
    source_field,
    receiver_field,
    slowness_slabs,
    slab_map,
    reference_gaps,
    reference_index,
    frequency_bins,
    shot_corner,
    *,
    ranks,
):
    rows, cols = source_field.shape[2:]
    depths = slab_map.shape[0]
    slab_count = slowness_slabs.shape[0]
    quarter = rows // 4
    tile = rows // ranks
    bins = frequency_bins.shape[0]
    slab_shape = slowness_slabs.shape[1:]
    forward_x, inverse_x = real_table(rows)
    forward_x = forward_x.T
    forward_y, inverse_y = real_table(cols)
    inverse_y = inverse_y.T

    keep, send = pl.pallas_call(
        functools.partial(window_kernel, slab_count=slab_count),
        grid_spec=pltpu.PrefetchScalarGridSpec(
            num_scalar_prefetch=2,
            grid=(depths,),
            in_specs=[
                pl.BlockSpec((1,) + slab_shape, lambda d, slabs, corner: (slabs[d] % slab_count, 0, 0))
            ],
            out_specs=[
                pl.BlockSpec((2, 1, quarter, cols), lambda d, slabs, corner: (0, d, 0, 0))
            ]
            * 2,
            scratch_shapes=[VMEM((slab_shape[0] + 8, cols), f32)],
        ),
        out_shape=[jax.ShapeDtypeStruct((2, depths, quarter, cols), bf16)] * 2,
        compiler_params=pltpu.CompilerParams(vmem_limit_bytes=32 << 20),
        name="window",
    )(slab_map, shot_corner, slowness_slabs)

    def swap(value, bit):
        return lax.ppermute(value, "freq", [(i, i ^ bit) for i in range(ranks)])

    held = keep + swap(send, 1)
    quarters = held[0] + swap(held[1], 2)
    bit = 4
    while bit < ranks:
        quarters = quarters + swap(quarters, bit)
        bit *= 2
    beside = swap(quarters, 2)
    across = swap(quarters, 1)
    corner_ways = swap(beside, 1)

    march_scratch = [
        VMEM((4, rows, cols), bf16),
        VMEM((4, rows, cols), bf16),
        VMEM((4, rows, cols), f32),
        VMEM((3, rows, cols), f32),
        VMEM((3, rows, cols), f32),
        VMEM((3, 4, rows, cols), bf16),
    ]
    smem = pl.BlockSpec(memory_space=SMEM)
    flops = 2 * 4 * (1 + 3) * rows * rows * cols
    returned = pl.pallas_call(
        first_kernel,
        in_specs=[smem, smem] + plain(5),
        out_specs=pl.BlockSpec(memory_space=VMEM),
        out_shape=jax.ShapeDtypeStruct((3, 4, rows, cols), bf16),
        scratch_shapes=march_scratch,
        compiler_params=pltpu.CompilerParams(vmem_limit_bytes=40 << 20),
        cost_estimate=pl.CostEstimate(flops=4 * flops, bytes_accessed=8 << 20, transcendentals=0),
        name="first",
    )(
        frequency_bins,
        reference_gaps,
        source_field,
        receiver_field,
        forward_x,
        forward_y,
        inverse_x,
    )

    def second(bins_ref, gaps_ref, returned_ref, q0, q1, q2, q3, *rest):
        second_kernel(bins_ref, gaps_ref, returned_ref, (q0, q1, q2, q3), *rest, depths=depths)

    crosses = pl.pallas_call(
        second,
        in_specs=[smem, smem] + plain(10),
        out_specs=pl.BlockSpec(memory_space=VMEM),
        out_shape=jax.ShapeDtypeStruct((ranks, depths, 2, tile, cols), bf16),
        scratch_shapes=[VMEM((depths, rows, cols), bf16)]
        + march_scratch
        + [VMEM((3, 4, rows, cols), bf16)],
        compiler_params=pltpu.CompilerParams(vmem_limit_bytes=50 << 20),
        name="second",
    )(
        frequency_bins,
        reference_gaps,
        returned,
        quarters,
        beside,
        across,
        corner_ways,
        reference_index,
        forward_x,
        forward_y,
        inverse_x,
        inverse_y,
    )

    offsets = jnp.arange(LAGS, dtype=jnp.int32) - LAGS // 2
    cycles = jnp.mod(frequency_bins[:, None] * offsets[None, :], period_bins).astype(f32)
    angles = cycles * (2.0 * math.pi / period_bins)
    lag_weights = jnp.stack([jnp.cos(angles), jnp.sin(angles)], axis=1).astype(bf16)

    arrived = lax.all_to_all(crosses, "freq", split_axis=0, concat_axis=0, tiled=True)
    scale = bins ** (-0.5)
    tall = 8
    if tile % (2 * tall):
        summed = jnp.einsum(
            "wdcab,wcl->dabl", arrived, lag_weights, preferred_element_type=f32
        )
        return summed * scale
    return pl.pallas_call(
        functools.partial(image_kernel, scale=scale),
        grid=(depths, tile // tall),
        in_specs=[
            pl.BlockSpec((bins, 1, 2, tall, cols), lambda d, t: (0, d, 0, t, 0)),
            pl.BlockSpec((bins, 2, LAGS), lambda d, t: (0, 0, 0)),
        ],
        out_specs=pl.BlockSpec((1, tall, cols, LAGS), lambda d, t: (d, t, 0, 0)),
        out_shape=jax.ShapeDtypeStruct((depths, tile, cols, LAGS), f32),
        scratch_shapes=[VMEM((bins * 2 * tall, tall * LAGS), bf16)],
        compiler_params=pltpu.CompilerParams(vmem_limit_bytes=32 << 20),
        name="image",
    )(arrived, lag_weights.astype(f32))


def solution(mesh):
    placed = (
        P("grp", "freq", None, None),
        P("grp", "freq", None, None),
        P(("grp", "freq"), None, None),
        P("grp"),
        P("grp", None),
        P("grp", None, None),
        P(),
        P("grp"),
    )
    return jax.shard_map(
        functools.partial(shards, ranks=mesh.shape["freq"]),
        mesh=mesh,
        in_specs=placed,
        out_specs=P("grp", "freq", None, None),
        check_vma=False,
    )
```

time: 222 us -> 97.1 us (0.44)
  other arithmetic: 72.8 us -> 0.76 us
  matrix products: 35.3 us -> 0 us
  waiting for transfers between devices: 70.4 us -> 39.4 us
  Pallas kernels: 0 us -> 29.7 us
  between operations: 19.5 us -> 0.17 us
  starting transfers between devices: 5.27 us -> 14.9 us
  local copies, waits for them, and re-layouts: 16.4 us -> 10.5 us
    psum x1 -> x0, waiting for transfers between devices: 47.6 us -> none  [spread(): return lax.psum(block, axis)]
    dot_general x6 -> x0, matrix products: 35.3 us -> none  [the longest x2 13.9 us: extrapolate(): jnp.einsum('fjcxy,cdyk->fjdxk', returned, inverse_y, preferred_element_ty...]
    pallas_call x0 -> x4, Pallas kernels: none -> 29.7 us  [the longest x1 14.6 us: shards(): pl.pallas_call(second, in_specs=[smem, smem] + plain(10), out_specs=pl.Bl...]
    another operation x15 -> x1, other arithmetic: 25.4 us -> 0.48 us
    sub x4 -> x1, other arithmetic: 17.6 us -> 0.01 us  [shards(): offsets = jnp.arange(LAGS, dtype=jnp.int32) - LAGS // 2]
    ppermute x0 -> x7, waiting for transfers between devices: none -> 17.1 us  [swap(): return lax.ppermute(value, 'freq', [(i, i ^ bit) for i in range(ranks)])]
    mul x2 -> x0, other arithmetic: 14.4 us -> none  [the longest x1 14.4 us: phase_factors(): fading * jnp.cos(vertical * layer_thick)]
    select_n x3 -> x0, other arithmetic: 9.39 us -> none  [the longest x2 7.38 us: extrapolate(): lower_field = jnp.where(lower_pair, refocused[:, 0], refocused[:, 1])]
  transfers between devices with their start and end apart: 2 -> 8, of which waited for: 2 -> 6; matrix products, arithmetic and copies ran while one was open for 20% -> 1% of each run, Pallas kernels for 0% -> 5%
where the time goes in v1:
time: 97.1 us; the launch traced here: 95.5 us
  waiting for transfers between devices  39.4 us (41%)
  Pallas kernels  29.7 us (31%)
  starting transfers between devices  14.9 us (15%)
  local copies, waits for them, and re-layouts  10.5 us (11%)
    all_to_all x1, waiting for transfers between devices, shards(): lax.all_to_all(crosses, 'freq', split_axis=0, concat_axis=0, tiled=True)  22.3 us
    ppermute x7, waiting for transfers between devices, swap(): return lax.ppermute(value, 'freq', [(i, i ^ bit) for i in range(ranks)])  17.1 us
    pallas_call x1, Pallas kernels, shards(): pl.pallas_call(second, in_specs=[smem, smem] + plain(10), out_specs=pl.Bl...  14.6 us
    unnamed x36, local copies, waits for them, and re-layouts  10.5 us
    ppermute x7, starting transfers between devices, swap(): return lax.ppermute(value, 'freq', [(i, i ^ bit) for i in range(ranks)])  9.36 us
    pallas_call x1, Pallas kernels, shards(): pl.pallas_call(functools.partial(image_kernel, scale=scale), grid=(depths...  8.16 us
    all_to_all x1, starting transfers between devices, shards(): lax.all_to_all(crosses, 'freq', split_axis=0, concat_axis=0, tiled=True)  5.52 us
    pallas_call x1, Pallas kernels, shards(): pl.pallas_call(first_kernel, in_specs=[smem, smem] + plain(5), out_specs=...  5.17 us
  transfers between devices with their start and end apart: 8, of which 6 were waited for; matrix products, arithmetic and copies ran while one was open for 1% of the time, Pallas kernels for 5%

profile of v1, /device:TPU:0, one launch (start us, length us, event | category | flops | bytes accessed | tf_op | source)
XLA Modules:
  0.0 95.5 jit_solution(10400293340704358421)
XLA Ops:
  0.0 1.1 %copy-done.2 = bf16[1,768,512]{2,1,0:T(8,128)(2,1)S(1)} copy-done((bf16[1,768,512]{2,1,0:T(8,128)(2,1)S(1)}, bf16[1,768,512]{2,1,0:T(8,128)(2,1)}, u32[]{:S(2)}) %copy-start.2) | copy-done | bytes 786456
  1.8 0.7 copy-done.15
  2.4 1.8 %window.1 = (bf16[2,2,128,256]{3,2,1,0:T(8,128)(2,1)S(1)}, bf16[2,2,128,256]{3,2,1,0:T(8,128)(2,1)S(1)}) custom-call(s32[2]{0:T(128)S(1)} %copy-done.14, s32[2]{0:T(128)S(1)} %copy-done.15, bf16[1,768,512]{2,1,0:T(8,128)(2,1)S(1)} %copy-done.2), custom_call_target="tpu_custom_call" | custom-call | tf_op jit(solution)/shard_map/window/pallas_call | solution.py:349
  4.7 1.2 %collective-permute-done = bf16[2,2,128,256]{3,2,1,0:T(8,128)(2,1)S(1)} collective-permute-done((bf16[2,2,128,256]{3,2,1,0:T(8,128)(2,1)S(1)}, bf16[2,2,128,256]{3,2,1,0:T(8,128)(2,1)S(1)}, u32[]{:S(2)}, u32[]{:S(2)}) %collective-permute-start) | collective-permute-done | bytes 262176 | tf_op jit(solution)/shard_map/ppermute | solution.py:369
  6.0 2.9 %collective-permute-start.1 = (bf16[2,128,256]{2,1,0:T(8,128)(2,1)S(1)}, bf16[2,128,256]{2,1,0:T(8,128)(2,1)S(1)}, u32[]{:S(2)}, u32[]{:S(2)}) collective-permute-start(bf16[2,128,256]{2,1,0:T(8,128)(2,1)S(1)} %slice_bitcast_fusion), channel_id=1, source_target_pairs={{0,2},{1,3},{2,0},{3,1},{4,6},{5,7},{6,4},{7,5},{8,10},{9,11},{10,... | collective-permute-start | bytes 393224 | tf_op jit(solution)/shard_map/ppermute | solution.py:369
  9.0 3.8 %collective-permute-done.1 = bf16[2,128,256]{2,1,0:T(8,128)(2,1)S(1)} collective-permute-done((bf16[2,128,256]{2,1,0:T(8,128)(2,1)S(1)}, bf16[2,128,256]{2,1,0:T(8,128)(2,1)S(1)}, u32[]{:S(2)}, u32[]{:S(2)}) %collective-permute-start.1) | collective-permute-done | bytes 131104 | tf_op jit(solution)/shard_map/ppermute | solution.py:369
  12.8 1.9 %collective-permute-start.2 = (bf16[2,128,256]{2,1,0:T(8,128)(2,1)S(1)}, bf16[2,128,256]{2,1,0:T(8,128)(2,1)S(1)}, u32[]{:S(2)}, u32[]{:S(2)}) collective-permute-start(bf16[2,128,256]{2,1,0:T(8,128)(2,1)S(1)} %fusion), channel_id=1, source_target_pairs={{0,4},{1,5},{2,6},{3,7},{4,0},{5,1},{6,2},{7,3},{8,12},{9,13},{10,... | collective-permute-start | bytes 393224 | tf_op jit(solution)/shard_map/ppermute | solution.py:369
  14.7 3.2 %collective-permute-done.2 = bf16[2,128,256]{2,1,0:T(8,128)(2,1)S(1)} collective-permute-done((bf16[2,128,256]{2,1,0:T(8,128)(2,1)S(1)}, bf16[2,128,256]{2,1,0:T(8,128)(2,1)S(1)}, u32[]{:S(2)}, u32[]{:S(2)}) %collective-permute-start.2) | collective-permute-done | bytes 131104 | tf_op jit(solution)/shard_map/ppermute | solution.py:369
  17.9 2.8 %collective-permute-start.3 = (bf16[2,128,256]{2,1,0:T(8,128)(2,1)S(1)}, bf16[2,128,256]{2,1,0:T(8,128)(2,1)S(1)}, u32[]{:S(2)}, u32[]{:S(2)}) collective-permute-start(bf16[2,128,256]{2,1,0:T(8,128)(2,1)S(1)} %add.36), channel_id=1, source_target_pairs={{0,8},{1,9},{2,10},{3,11},{4,12},{5,13},{6,14},{7,15},{8,0},{9,1},... | collective-permute-start | bytes 393224 | tf_op jit(solution)/shard_map/ppermute | solution.py:369
  20.8 5.1 %collective-permute-done.3 = bf16[2,128,256]{2,1,0:T(8,128)(2,1)S(1)} collective-permute-done((bf16[2,128,256]{2,1,0:T(8,128)(2,1)S(1)}, bf16[2,128,256]{2,1,0:T(8,128)(2,1)S(1)}, u32[]{:S(2)}, u32[]{:S(2)}) %collective-permute-start.3) | collective-permute-done | bytes 131104 | tf_op jit(solution)/shard_map/ppermute | solution.py:369
  25.8 1.2 %collective-permute-start.4 = (bf16[2,128,256]{2,1,0:T(8,128)(2,1)S(1)}, bf16[2,128,256]{2,1,0:T(8,128)(2,1)S(1)}, u32[]{:S(2)}, u32[]{:S(2)}) collective-permute-start(bf16[2,128,256]{2,1,0:T(8,128)(2,1)S(1)} %add.37.q0), channel_id=1, source_target_pairs={{0,2},{1,3},{2,0},{3,1},{4,6},{5,7},{6,4},{7,5},{8,10},{9,11},{10,... | collective-permute-start | bytes 393224 | tf_op jit(solution)/shard_map/ppermute | solution.py:369
  27.0 3.9 %collective-permute-done.4.q1 = bf16[2,128,256]{2,1,0:T(8,128)(2,1)S(1)} collective-permute-done((bf16[2,128,256]{2,1,0:T(8,128)(2,1)S(1)}, bf16[2,128,256]{2,1,0:T(8,128)(2,1)S(1)}, u32[]{:S(2)}, u32[]{:S(2)}) %collective-permute-start.4) | collective-permute-done | bytes 131104 | tf_op jit(solution)/shard_map/ppermute | solution.py:369
  30.9 1.0 %copy-done.3 = bf16[512,512]{1,0:T(8,128)(2,1)S(1)} copy-done((bf16[512,512]{1,0:T(8,128)(2,1)S(1)}, bf16[512,512]{1,0:T(8,128)(2,1)}, u32[]{:S(2)}) %copy-start.3) | copy-done | bytes 524312
  31.9 1.0 %copy-done.5 = bf16[512,512]{1,0:T(8,128)(2,1)S(1)} copy-done((bf16[512,512]{1,0:T(8,128)(2,1)S(1)}, bf16[512,512]{1,0:T(8,128)(2,1)}, u32[]{:S(2)}) %copy-start.5) | copy-done | bytes 524312
  33.0 0.9 copy-done.7
  34.5 0.7 copy-done.12
  35.2 1.0 %copy-done.16 = bf16[2,1,512,256]{3,2,1,0:T(8,128)(2,1)S(1)} copy-done((bf16[2,1,512,256]{3,2,1,0:T(8,128)(2,1)S(1)}, bf16[2,1,512,256]{3,2,1,0:T(8,128)(2,1)}, u32[]{:S(2)}) %copy-start.16) | copy-done | bytes 524312
  36.3 1.0 %copy-done.17 = bf16[2,1,512,256]{3,2,1,0:T(8,128)(2,1)S(1)} copy-done((bf16[2,1,512,256]{3,2,1,0:T(8,128)(2,1)S(1)}, bf16[2,1,512,256]{3,2,1,0:T(8,128)(2,1)}, u32[]{:S(2)}) %copy-start.17) | copy-done | bytes 524312
  37.3 5.2 %first.1.returned_ref = bf16[3,4,512,256]{3,2,1,0:T(8,128)(2,1)S(1)} custom-call(s32[16]{0:T(128)S(1)} %copy-done.10, f32[2,3]{1,0:T(2,128)S(1)} %copy-done.12, bf16[2,1,512,256]{3,2,1,0:T(8,128)(2,1)S(1)} %copy-done.16, bf16[2,1,512,256]{3,2,1,0:T(8,128)(2,1)S(1)} %copy-done.17, bf16[512,512]{1,0:T(8,128)(2,1)S(1)} %copy-done.5, ...), custom_call_target="tpu_custom_call" | custom-call | flops 8589934592 | bytes 8388608 | tf_op jit(solution)/shard_map/first/pallas_call | solution.py:391
  42.5 1.7 %copy-done = bf16[3,4,512,256]{3,2,1,0:T(8,128)(2,1)} copy-done((bf16[3,4,512,256]{3,2,1,0:T(8,128)(2,1)}, bf16[3,4,512,256]{3,2,1,0:T(8,128)(2,1)S(1)}, u32[]{:S(2)}) %copy-start) | copy-done | bytes 3145752
  44.2 14.6 %second.1 = bf16[16,2,2,32,256]{4,3,2,1,0:T(8,128)(2,1)} custom-call(s32[16]{0:T(128)S(1)} %copy-done.11, f32[2,3]{1,0:T(2,128)S(1)} %copy-done.13, bf16[3,4,512,256]{3,2,1,0:T(8,128)(2,1)} %copy-done, bf16[2,128,256]{2,1,0:T(8,128)(2,1)S(1)} %add.37.q0, bf16[2,128,256]{2,1,0:T(8,128)(2,1)S(1)} %collective-permute-done.4.q1, ...), custom_call_target="tpu_custom_call" | custom-call | tf_op jit(solution)/shard_map/second/pallas_call | solution.py:413
  58.9 5.5 %all-to-all-start = ((bf16[16,2,2,32,256]{4,3,2,1,0:T(8,128)(2,1)}), bf16[16,2,2,32,256]{4,3,2,1,0:T(8,128)(2,1)S(1)}, u32[]{:S(2)}, u32[]{:S(2)}) async-start(bf16[16,2,2,32,256]{4,3,2,1,0:T(8,128)(2,1)} %second.1), calls=%async_computation | async-start | bytes 2097152 | tf_op jit(solution)/shard_map/all_to_all | solution.py:443
  65.0 22.3 %all-to-all-done.cross_ref = bf16[16,2,2,32,256]{4,3,2,1,0:T(8,128)(2,1)S(1)} async-done(((bf16[16,2,2,32,256]{4,3,2,1,0:T(8,128)(2,1)}), bf16[16,2,2,32,256]{4,3,2,1,0:T(8,128)(2,1)S(1)}, u32[]{:S(2)}, u32[]{:S(2)}) %all-to-all-start) | async-done | bytes 1048608 | tf_op jit(solution)/shard_map/all_to_all | solution.py:443
  87.3 8.2 %image.1 = f32[2,32,256,256]{3,2,1,0:T(8,128)} custom-call(bf16[16,2,2,32,256]{4,3,2,1,0:T(8,128)(2,1)S(1)} %all-to-all-done.cross_ref, f32[16,2,256]{2,1,0:T(2,128)S(1)} %maximum_convert_fusion.lag_ref), custom_call_target="tpu_custom_call" | custom-call | tf_op jit(solution)/shard_map/image/pallas_call | solution.py:451
  (41 shorter events, 2.7 us)
Async XLA Ops:
  0.0 1.1 %copy-start.2 = (bf16[1,768,512]{2,1,0:T(8,128)(2,1)S(1)}, bf16[1,768,512]{2,1,0:T(8,128)(2,1)}, u32[]{:S(2)}) copy-start(bf16[1,768,512]{2,1,0:T(8,128)(2,1)} %slab_ref.1) | copy-start | bytes 2359300
  1.1 0.7 copy-start.14
  2.4 41.7 %copy-start.9 = (bf16[256,256]{1,0:T(8,128)(2,1)S(1)}, bf16[256,256]{1,0:T(8,128)(2,1)}, u32[]{:S(2)}) copy-start(bf16[256,256]{1,0:T(8,128)(2,1)} %constant.43.rest_4_) | copy-start | bytes 393220
  4.2 1.7 %collective-permute-start = (bf16[2,2,128,256]{3,2,1,0:T(8,128)(2,1)S(1)}, bf16[2,2,128,256]{3,2,1,0:T(8,128)(2,1)S(1)}, u32[]{:S(2)}, u32[]{:S(2)}) collective-permute-start(bf16[2,2,128,256]{3,2,1,0:T(8,128)(2,1)S(1)} %get-tuple-element.8), channel_id=1, source_target_pairs={{0,1},{1,0},{2,3},{3,2},{4,5},{5,4},{6,7},{7,6},{8,9},{9,8},{10,11... | collective-permute-start | bytes 786440 | tf_op jit(solution)/shard_map/ppermute | solution.py:369
  5.9 38.3 %copy-start.8 = (bf16[256,256]{1,0:T(8,128)(2,1)S(1)}, bf16[256,256]{1,0:T(8,128)(2,1)}, u32[]{:S(2)}) copy-start(bf16[256,256]{1,0:T(8,128)(2,1)} %constant.34.forward_y.rest_2_) | copy-start | bytes 393220
  5.9 38.3 %copy-start.4 = (bf16[512,512]{1,0:T(8,128)(2,1)S(1)}, bf16[512,512]{1,0:T(8,128)(2,1)}, u32[]{:S(2)}) copy-start(bf16[512,512]{1,0:T(8,128)(2,1)} %constant.38.inverse_x.rest_3_) | copy-start | bytes 1572868
  5.9 38.3 %copy-start.6 = (bf16[512,512]{1,0:T(8,128)(2,1)S(1)}, bf16[512,512]{1,0:T(8,128)(2,1)}, u32[]{:S(2)}) copy-start(bf16[512,512]{1,0:T(8,128)(2,1)} %constant.33.forward_x.rest_1_) | copy-start | bytes 1572868
  6.0 38.2 %copy-start.1 = (s32[2,512,256]{2,1,0:T(8,128)S(1)}, s32[2,512,256]{2,1,0:T(8,128)}, u32[]{:S(2)}) copy-start(s32[2,512,256]{2,1,0:T(8,128)} %rest_0_.1) | copy-start | bytes 3145732
  6.0 38.2 %copy-start.11 = (s32[16]{0:T(128)S(1)}, s32[16]{0:T(128)}, u32[]{:S(2)}) copy-start(s32[16]{0:T(128)} %bins_ref.3) | copy-start | bytes 196
  6.0 38.2 %copy-start.13 = (f32[2,3]{1,0:T(2,128)S(1)}, f32[2,3]{1,0:T(2,128)}, u32[]{:S(2)}) copy-start(f32[2,3]{1,0:T(2,128)} %gaps_ref.3) | copy-start | bytes 76
  6.0 6.7 %collective-permute-start.1 = (bf16[2,128,256]{2,1,0:T(8,128)(2,1)S(1)}, bf16[2,128,256]{2,1,0:T(8,128)(2,1)S(1)}, u32[]{:S(2)}, u32[]{:S(2)}) collective-permute-start(bf16[2,128,256]{2,1,0:T(8,128)(2,1)S(1)} %slice_bitcast_fusion), channel_id=1, source_target_pairs={{0,2},{1,3},{2,0},{3,1},{4,6},{5,7},{6,4},{7,5},{8,10},{9,11},{10,... | collective-permute-start | bytes 393224 | tf_op jit(solution)/shard_map/ppermute | solution.py:369
  12.8 5.1 %collective-permute-start.2 = (bf16[2,128,256]{2,1,0:T(8,128)(2,1)S(1)}, bf16[2,128,256]{2,1,0:T(8,128)(2,1)S(1)}, u32[]{:S(2)}, u32[]{:S(2)}) collective-permute-start(bf16[2,128,256]{2,1,0:T(8,128)(2,1)S(1)} %fusion), channel_id=1, source_target_pairs={{0,4},{1,5},{2,6},{3,7},{4,0},{5,1},{6,2},{7,3},{8,12},{9,13},{10,... | collective-permute-start | bytes 393224 | tf_op jit(solution)/shard_map/ppermute | solution.py:369
  17.9 7.9 %collective-permute-start.3 = (bf16[2,128,256]{2,1,0:T(8,128)(2,1)S(1)}, bf16[2,128,256]{2,1,0:T(8,128)(2,1)S(1)}, u32[]{:S(2)}, u32[]{:S(2)}) collective-permute-start(bf16[2,128,256]{2,1,0:T(8,128)(2,1)S(1)} %add.36), channel_id=1, source_target_pairs={{0,8},{1,9},{2,10},{3,11},{4,12},{5,13},{6,14},{7,15},{8,0},{9,1},... | collective-permute-start | bytes 393224 | tf_op jit(solution)/shard_map/ppermute | solution.py:369
  25.8 5.0 %collective-permute-start.4 = (bf16[2,128,256]{2,1,0:T(8,128)(2,1)S(1)}, bf16[2,128,256]{2,1,0:T(8,128)(2,1)S(1)}, u32[]{:S(2)}, u32[]{:S(2)}) collective-permute-start(bf16[2,128,256]{2,1,0:T(8,128)(2,1)S(1)} %add.37.q0), channel_id=1, source_target_pairs={{0,2},{1,3},{2,0},{3,1},{4,6},{5,7},{6,4},{7,5},{8,10},{9,11},{10,... | collective-permute-start | bytes 393224 | tf_op jit(solution)/shard_map/ppermute | solution.py:369
  27.0 17.1 %collective-permute-start.5 = (bf16[2,128,256]{2,1,0:T(8,128)(2,1)S(1)}, bf16[2,128,256]{2,1,0:T(8,128)(2,1)S(1)}, u32[]{:S(2)}, u32[]{:S(2)}) collective-permute-start(bf16[2,128,256]{2,1,0:T(8,128)(2,1)S(1)} %add.37.q0), channel_id=1, source_target_pairs={{0,1},{1,0},{2,3},{3,2},{4,5},{5,4},{6,7},{7,6},{8,9},{9,8},{10,11... | collective-permute-start | bytes 393224 | tf_op jit(solution)/shard_map/ppermute | solution.py:369
  30.9 13.3 %collective-permute-start.6 = (bf16[2,128,256]{2,1,0:T(8,128)(2,1)S(1)}, bf16[2,128,256]{2,1,0:T(8,128)(2,1)S(1)}, u32[]{:S(2)}, u32[]{:S(2)}) collective-permute-start(bf16[2,128,256]{2,1,0:T(8,128)(2,1)S(1)} %collective-permute-done.4.q1), channel_id=1, source_target_pairs={{0,1},{1,0},{2,3},{3,2},{4,5},{5,4},{6,7},{7,6},{8,9},{9,8},{10,11... | collective-permute-start | bytes 393224 | tf_op jit(solution)/shard_map/ppermute | solution.py:369
  30.9 1.0 %copy-start.3 = (bf16[512,512]{1,0:T(8,128)(2,1)S(1)}, bf16[512,512]{1,0:T(8,128)(2,1)}, u32[]{:S(2)}) copy-start(bf16[512,512]{1,0:T(8,128)(2,1)} %constant.38.inverse_x.rest_3_) | copy-start | bytes 1572868
  31.9 1.0 %copy-start.5 = (bf16[512,512]{1,0:T(8,128)(2,1)S(1)}, bf16[512,512]{1,0:T(8,128)(2,1)}, u32[]{:S(2)}) copy-start(bf16[512,512]{1,0:T(8,128)(2,1)} %constant.33.forward_x.rest_1_) | copy-start | bytes 1572868
  33.0 0.9 copy-start.7
  34.5 0.7 copy-start.12
  35.2 1.0 %copy-start.16 = (bf16[2,1,512,256]{3,2,1,0:T(8,128)(2,1)S(1)}, bf16[2,1,512,256]{3,2,1,0:T(8,128)(2,1)}, u32[]{:S(2)}) copy-start(bf16[2,1,512,256]{3,2,1,0:T(8,128)(2,1)} %source_ref.1) | copy-start | bytes 1572868
  36.3 1.0 %copy-start.17 = (bf16[2,1,512,256]{3,2,1,0:T(8,128)(2,1)S(1)}, bf16[2,1,512,256]{3,2,1,0:T(8,128)(2,1)}, u32[]{:S(2)}) copy-start(bf16[2,1,512,256]{3,2,1,0:T(8,128)(2,1)} %receiver_ref.1) | copy-start | bytes 1572868
  42.5 1.7 %copy-start = (bf16[3,4,512,256]{3,2,1,0:T(8,128)(2,1)}, bf16[3,4,512,256]{3,2,1,0:T(8,128)(2,1)S(1)}, u32[]{:S(2)}) copy-start(bf16[3,4,512,256]{3,2,1,0:T(8,128)(2,1)S(1)} %first.1.returned_ref) | copy-start | bytes 9437188
  58.9 28.5 %all-to-all-start = ((bf16[16,2,2,32,256]{4,3,2,1,0:T(8,128)(2,1)}), bf16[16,2,2,32,256]{4,3,2,1,0:T(8,128)(2,1)S(1)}, u32[]{:S(2)}, u32[]{:S(2)}) async-start(bf16[16,2,2,32,256]{4,3,2,1,0:T(8,128)(2,1)} %second.1), calls=%async_computation | async-start | bytes 2097152 | tf_op jit(solution)/shard_map/all_to_all | solution.py:443
  (2 other events, 1.3 us)

commit v2 on v1

v2 whole, which is shorter than its diff:
```python
import functools
import math

import jax
import jax.numpy as jnp
import numpy as np
from jax import lax
from jax.experimental import pallas as pl
from jax.experimental.pallas import tpu as pltpu
from jax.sharding import PartitionSpec as P

LAGS = 256

cell_width = 0.0125
layer_thick = 0.0125
bin_hertz = 0.5
period_bins = 500
slow_base = 0.3

VMEM = pltpu.VMEM
SMEM = pltpu.SMEM
f32 = jnp.float32
bf16 = jnp.bfloat16


def real_table(length):
    half = length // 2
    steps = np.arange(length, dtype=np.int64)
    wave = np.concatenate([np.arange(half), [half], np.arange(1, half)])
    phases = np.mod(steps[:, None] * wave[None, :], length).astype(np.float32)
    angles = phases * np.float32(2.0 * math.pi / length)
    scale = np.float32(1.0 / math.sqrt(length))
    is_cos = np.arange(length) <= half
    table = np.where(is_cos[None, :], np.cos(angles), np.sin(angles)) * scale
    twice = np.where((wave == 0) | (wave == half), 1.0, 2.0)
    forward = jnp.asarray(table.astype(np.float32)).astype(bf16)
    inverse = (forward.astype(f32) * jnp.asarray(twice[None, :], f32)).astype(bf16)
    return forward, inverse


def sin_cos(angle):
    turns = jnp.floor(angle * (2.0 / math.pi) + 0.5)
    rest = angle - turns * 1.5707397460937500
    rest = rest - turns * 5.6580702948965924e-05
    quadrant = turns.astype(jnp.int32)
    square = rest * rest
    sine = rest + rest * square * (
        -1.6666654611e-1 + square * (8.3321608736e-3 - square * 1.9515295891e-4)
    )
    cosine = (
        1.0
        - 0.5 * square
        + square
        * square
        * (4.166664568298827e-2 + square * (-1.388731625493765e-3 + square * 2.443315711809948e-5))
    )
    odd = (quadrant & 1) == 1
    out_sin = jnp.where(odd, cosine, sine)
    out_cos = jnp.where(odd, sine, cosine)
    out_sin = jnp.where((quadrant & 2) == 2, -out_sin, out_sin)
    out_cos = jnp.where(((quadrant + 1) & 2) == 2, -out_cos, out_cos)
    return out_sin, out_cos


def references_of(gaps_ref, depth):
    first = slow_base + gaps_ref[depth, 0]
    second = first + gaps_ref[depth, 1]
    third = second + gaps_ref[depth, 2]
    return first, second, third


def scalars_of(held_ref, depth):
    rows = [held_ref[row : row + 1] for row in (0, *range(1 + 3 * depth, 4 + 3 * depth))]
    return rows[0], tuple(rows[1:])


def angular_of(bins_ref):
    return bins_ref[lax.axis_index("freq")].astype(f32) * (2.0 * math.pi * bin_hertz)


def phase_block(reach, base_turn, squares):
    radicand = reach - squares
    root = jnp.sqrt(jnp.abs(radicand)) * layer_thick
    travelling = radicand > 0.0
    fading = jnp.where(travelling, 1.0, jnp.exp(-root))
    sine, cosine = sin_cos(jnp.where(travelling, root, 0.0) - base_turn)
    return fading * cosine, fading * sine


def make_phases(cos_ref, sin_ref, angular, reference):
    rows, cols = cos_ref.shape
    half = rows // 2
    reach = (angular * reference) * (angular * reference)
    base_turn = angular * layer_thick * reference
    step_x = 2.0 * math.pi / (rows * cell_width)
    step_y = 2.0 * math.pi / (cols * cell_width)
    lane = lax.broadcasted_iota(jnp.int32, (8, cols), 1)
    wave_y = jnp.where(lane <= cols // 2, lane, lane - cols // 2).astype(f32) * step_y
    square_y = wave_y * wave_y
    tall = 64

    def body(block, carry):
        start = pl.multiple_of(block * tall, tall)
        row = lax.broadcasted_iota(jnp.int32, (tall, cols), 0) + start
        wave_x = row.astype(f32) * step_x
        cosine, sine = phase_block(
            reach, base_turn, wave_x * wave_x + jnp.concatenate([square_y] * (tall // 8), axis=0)
        )
        cos_ref[pl.ds(start, tall), :] = cosine
        sin_ref[pl.ds(start, tall), :] = sine
        cos_ref[pl.ds(half + start, tall), :] = cosine
        sin_ref[pl.ds(half + start, tall), :] = sine
        return carry

    lax.fori_loop(0, half // tall, body, 0)
    edge = (half * step_x) ** 2
    cosine, sine = phase_block(reach, base_turn, edge + square_y)
    top = lax.broadcasted_iota(jnp.int32, (8, cols), 0) == 0
    cos_ref[half : half + 8, :] = jnp.where(top, cosine, cos_ref[half : half + 8, :])
    sin_ref[half : half + 8, :] = jnp.where(top, sine, sin_ref[half : half + 8, :])


def dot(left, right):
    return jnp.dot(left, right, preferred_element_type=f32)


def march(plane_of, signs, tables, scalars, scratch, out_ref, ready=(None, None, None)):
    forward_x, forward_y, inverse_x = tables
    angular, references = scalars
    half_ref, spec_ref, cos_ref, sin_ref, shift_ref = scratch
    for j in range(3):
        make_phases(cos_ref.at[j], sin_ref.at[j], angular, references[j])
    for wait in ready[0] or ():
        wait()
    for plane in range(4):
        half = dot(plane_of(plane), forward_y[...])
        half_ref[plane] = (half if signs[plane] > 0 else -half).astype(bf16)
    for wait in ready[1] or ():
        wait()
    for plane in range(4):
        spec_ref[plane] = dot(forward_x[...], half_ref[plane])
    for wait in ready[2] or ():
        wait()
    for j in range(3):
        for field in range(2):
            real, imag = spec_ref[2 * field], spec_ref[2 * field + 1]
            cosine, sine = cos_ref[j], sin_ref[j]
            shift_ref[j, 2 * field] = (cosine * real - sine * imag).astype(bf16)
            shift_ref[j, 2 * field + 1] = (cosine * imag + sine * real).astype(bf16)
        for plane in range(4):
            out_ref[j, plane] = dot(inverse_x[...], shift_ref[j, plane]).astype(bf16)


BLEND_ROWS = 64


def blend(returned_ref, slow_of, bracket_ref, inverse_y, scalars, parts, put_wave, put_cross, starts):
    rows, cols = bracket_ref.shape
    tall = BLEND_ROWS
    chunk = 16
    angular, (low, mid, high) = scalars
    slope_low = 1.0 / (mid - low)
    slope_high = 1.0 / (high - mid)
    blocks = rows // tall

    def first_row(block):
        return pl.multiple_of(block * tall if starts is None else starts[block], tall)

    def fill(part_ref, block):
        left = returned_ref[:, :, pl.ds(first_row(block), tall), :].reshape(12 * tall, cols)
        part_ref[...] = dot(left, inverse_y[...]).reshape(12, tall, cols)

    def mix(part_ref, block):
        start = first_row(block)
        crossed = []
        for piece in range(tall // chunk):
            within = slice(piece * chunk, (piece + 1) * chunk)
            here = pl.ds(start + piece * chunk, chunk)
            slow = slow_of(block, here, within).astype(f32)
            lower = bracket_ref[here, :] == 0
            weight = jnp.where(lower, (slow - low) * slope_low, (slow - mid) * slope_high)
            weight = jnp.minimum(jnp.maximum(weight, 0.0), 1.0)
            sine, cosine = sin_cos(slow * (angular * layer_thick))
            halves = []
            for plane in range(4):
                first, second, third = [part_ref[4 * j + plane, within] for j in range(3)]
                bottom = jnp.where(lower, first, second)
                top = jnp.where(lower, second, third)
                halves.append(bottom + weight * (top - bottom))
            fresh = []
            for field in range(2):
                real, imag = halves[2 * field], halves[2 * field + 1]
                fresh.append((cosine * real - sine * imag).astype(bf16))
                fresh.append((cosine * imag + sine * real).astype(bf16))
            if put_wave is not None:
                for plane in range(4):
                    put_wave(block, here, within, plane, fresh[plane])
            s_real, s_imag, r_real, r_imag = [value.astype(f32) for value in fresh]
            crossed.append(
                (
                    (s_real * r_real - s_imag * r_imag).astype(bf16),
                    (s_real * r_imag + s_imag * r_real).astype(bf16),
                )
            )
        for side in range(2):
            put_cross(block, side, jnp.concatenate([pair[side] for pair in crossed], axis=0))

    even, odd = parts
    if starts is not None:
        fill(even, 0)
        for block in range(len(starts)):
            if block + 1 < len(starts):
                fill(odd if block % 2 == 0 else even, block + 1)
            mix(even if block % 2 == 0 else odd, block)
        return
    fill(even, 0)

    def body(step, carry):
        fill(odd, 2 * step + 1)
        mix(even, 2 * step)
        fill(even, jnp.minimum(2 * step + 2, blocks - 1))
        mix(odd, 2 * step + 1)
        return carry

    lax.fori_loop(0, blocks // 2, body, 0)


def put_tiles(cross_ref, first, side, values):
    tile = cross_ref.shape[2]
    for part in range(values.shape[0] // tile):
        cross_ref[first + part, side] = values[part * tile : (part + 1) * tile]


def spots():
    rank = lax.axis_index("freq")
    core, side = rank % 2, (rank // 2) % 2
    return [
        2 * ((core + other_core) % 2) + (side + other_side) % 2
        for other_core, other_side in ((0, 0), (0, 1), (1, 0), (1, 1))
    ]


def window_kernel(
    map_hbm, corner_hbm, slab_hbm, keep_ref, send_ref, map_ref, corner_ref, slab_ref, sems
):
    depths, quarter, cols = keep_ref.shape[1:]
    slab_count = slab_hbm.shape[0]
    tall, wide = slab_hbm.shape[1:]
    copies = [
        pltpu.make_async_copy(map_hbm, map_ref, sems.at[0]),
        pltpu.make_async_copy(corner_hbm, corner_ref, sems.at[1]),
    ]
    for copy in copies:
        copy.start()
    if slab_count == 1:
        whole = pltpu.make_async_copy(slab_hbm.at[0], slab_ref.at[0], sems.at[2])
        whole.start()
    for copy in copies:
        copy.wait()
    if slab_count == 1:
        whole.wait()
    rank = lax.axis_index("freq")
    core, side = rank % 2, (rank // 2) % 2
    rows = 4 * quarter
    first_row = jnp.minimum((corner_ref[0] // 16) * 16, tall - rows - 16)
    first_col = jnp.minimum((corner_ref[1] // 128) * 128, wide - cols - 128)
    above = corner_ref[0] - first_row
    before = corner_ref[1] - first_col
    reach = quarter + 16
    span = cols + 128
    for depth in range(depths):
        slab = map_ref[depth]
        mine = slab // slab_count == rank

        @pl.when(mine)
        def _():
            if slab_count == 1:
                here = slab_ref.at[0]
            else:
                here = slab_ref.at[0]
                copy = pltpu.make_async_copy(
                    slab_hbm.at[lax.rem(slab, slab_count)], here, sems.at[2]
                )
                copy.start()
                copy.wait()
            for other_core in range(2):
                target = send_ref if other_core else keep_ref
                for other_side in range(2):
                    spot = 2 * ((core + other_core) % 2) + (side + other_side) % 2
                    block = here[
                        pl.ds(pl.multiple_of(first_row + spot * quarter, 16), reach),
                        pl.ds(pl.multiple_of(first_col, 128), span),
                    ].astype(f32)
                    block = pltpu.roll(block, lax.rem(span - before, span), 1)[:, :cols]
                    block = pltpu.roll(block, lax.rem(reach - above, reach), 0)[:quarter]
                    target[other_side, depth] = block.astype(bf16)

        @pl.when(jnp.logical_not(mine))
        def _():
            for other_side in range(2):
                keep_ref[other_side, depth] = jnp.zeros((quarter, cols), bf16)
                send_ref[other_side, depth] = jnp.zeros((quarter, cols), bf16)


def first_kernel(
    bins_hbm,
    gaps_hbm,
    source_hbm,
    receiver_hbm,
    forward_x_hbm,
    forward_y_hbm,
    inverse_x_hbm,
    bracket_hbm,
    inverse_y_hbm,
    out_ref,
    bracket_ref,
    inverse_y,
    held_ref,
    bins_ref,
    gaps_ref,
    wave_ref,
    forward_x,
    forward_y,
    inverse_x,
    sems,
    *scratch,
):
    pairs = [
        (bins_hbm, bins_ref),
        (gaps_hbm, gaps_ref),
        (forward_y_hbm, forward_y),
        (source_hbm.at[:, 0], wave_ref.at[0:2]),
        (receiver_hbm.at[:, 0], wave_ref.at[2:4]),
        (forward_x_hbm, forward_x),
        (inverse_x_hbm, inverse_x),
        (bracket_hbm.at[0], bracket_ref),
        (inverse_y_hbm, inverse_y),
    ]
    copies = [
        pltpu.make_async_copy(source, target, sems.at[index])
        for index, (source, target) in enumerate(pairs)
    ]
    for copy in copies:
        copy.start()
    copies[0].wait()
    copies[1].wait()
    angular = angular_of(bins_ref)
    held_ref[0:1] = jnp.full((1, held_ref.shape[1]), angular, f32)
    for depth in range(gaps_ref.shape[0]):
        for j, reference in enumerate(references_of(gaps_ref, depth)):
            row = 1 + 3 * depth + j
            held_ref[row : row + 1] = jnp.full((1, held_ref.shape[1]), reference, f32)
    march(
        lambda plane: wave_ref[plane],
        (1, 1, 1, -1),
        (forward_x, forward_y, inverse_x),
        (angular, references_of(gaps_ref, 0)),
        scratch,
        out_ref,
        ready=([copy.wait for copy in copies[2:5]], [copies[5].wait], [copies[6].wait]),
    )
    for copy in copies[7:]:
        copy.wait()


def mix_starts(which):
    quarter_spots = spots()
    return lambda quarter: [
        quarter_spots[index] * quarter + offset
        for index in which
        for offset in range(0, quarter, BLEND_ROWS)
    ]


def near_kernel(
    held_ref, returned_ref, q0, q2, bracket_ref, inverse_y, wave_ref, cross_ref, even, odd
):
    quarter = q0.shape[1]
    each = quarter // BLEND_ROWS
    tile = cross_ref.shape[2]
    own = (q0, q2)

    def put_wave(block, here, within, plane, values):
        part = slice((block % each) * BLEND_ROWS + within.start, (block % each) * BLEND_ROWS + within.stop)
        wave_ref[block // each, plane, part] = values

    blend(
        returned_ref,
        lambda block, here, within: own[block // each][
            0, (block % each) * BLEND_ROWS + within.start : (block % each) * BLEND_ROWS + within.stop
        ],
        bracket_ref,
        inverse_y,
        scalars_of(held_ref, 0),
        (even, odd),
        put_wave,
        lambda block, side, values: put_tiles(cross_ref, block * BLEND_ROWS // tile, side, values),
        mix_starts((0, 2))(quarter),
    )


def far_kernel(
    held_ref,
    returned_ref,
    q1,
    q3,
    bracket_ref,
    inverse_y,
    near_wave,
    near_cross,
    wave_ref,
    cross_ref,
    even,
    odd,
):
    quarter = q1.shape[1]
    each = quarter // BLEND_ROWS
    tile = cross_ref.shape[2]
    tiles = quarter // tile
    quarter_spots = spots()
    for index, spot in enumerate((quarter_spots[0], quarter_spots[2])):
        start = pl.multiple_of(spot * quarter, quarter)
        wave_ref[:, pl.ds(start, quarter), :] = near_wave[index]
        cross_ref[pl.ds(spot * tiles, tiles)] = near_cross[index * tiles : (index + 1) * tiles]
    own = (q1, q3)
    starts = mix_starts((1, 3))(quarter)

    def put_wave(block, here, within, plane, values):
        wave_ref[plane, here, :] = values

    def put_cross(block, side, values):
        put_tiles(cross_ref, starts[block] // tile, side, values)

    blend(
        returned_ref,
        lambda block, here, within: own[block // each][
            0, (block % each) * BLEND_ROWS + within.start : (block % each) * BLEND_ROWS + within.stop
        ],
        bracket_ref,
        inverse_y,
        scalars_of(held_ref, 0),
        (even, odd),
        put_wave,
        put_cross,
        starts,
    )


def later_kernel(
    held_ref,
    wave_ref,
    q0,
    q1,
    q2,
    q3,
    bracket_hbm,
    forward_x_hbm,
    forward_y_hbm,
    inverse_x_hbm,
    inverse_y,
    *rest,
    depth,
    last,
):
    if last:
        fresh_ref = None
    else:
        fresh_ref, rest = rest[0], rest[1:]
    cross_ref, bracket_ref, forward_x, forward_y, inverse_x, sems = rest[:6]
    slow_ref, returned_ref, even, odd = rest[6:10]
    pairs = [
        (forward_y_hbm, forward_y),
        (forward_x_hbm, forward_x),
        (inverse_x_hbm, inverse_x),
        (bracket_hbm.at[depth], bracket_ref),
    ]
    copies = [
        pltpu.make_async_copy(source, target, sems.at[index])
        for index, (source, target) in enumerate(pairs)
    ]
    for copy in copies:
        copy.start()
    scalars = scalars_of(held_ref, depth)
    quarter = q0.shape[1]
    for spot, value in zip(spots(), (q0, q1, q2, q3)):
        slow_ref[pl.ds(pl.multiple_of(spot * quarter, quarter), quarter), :] = value[depth]
    march(
        lambda plane: wave_ref[plane],
        (1, 1, 1, 1),
        (forward_x, forward_y, inverse_x),
        scalars,
        rest[10:],
        returned_ref,
        ready=tuple([copy.wait] for copy in copies[:3]),
    )
    copies[3].wait()
    tile = cross_ref.shape[2]

    def put_wave(block, here, within, plane, values):
        fresh_ref[plane, here, :] = values

    blend(
        returned_ref,
        lambda block, here, within: slow_ref[here, :],
        bracket_ref,
        inverse_y,
        scalars,
        (even, odd),
        None if last else put_wave,
        lambda block, side, values: put_tiles(
            cross_ref, block * (BLEND_ROWS // tile), side, values
        ),
        None,
    )


IMAGE_ROWS = 8


def lag_kernel(lag_ref, weight_ref):
    bins, pair, lags = lag_ref.shape
    height = bins * pair * IMAGE_ROWS
    table = jnp.broadcast_to(
        lag_ref[...].reshape(bins * pair, 1, lags), (bins * pair, IMAGE_ROWS, lags)
    ).reshape(height, lags)
    place = lax.broadcasted_iota(jnp.int32, (height, lags), 0) % IMAGE_ROWS
    for row in range(IMAGE_ROWS):
        weight_ref[:, row * lags : (row + 1) * lags] = jnp.where(place == row, table, 0.0).astype(
            bf16
        )


def image_kernel(*refs, scale, depth, aliased):
    cross_ref, weight_ref = refs[:2]
    out_hbm, made_ref, sems = refs[2 + aliased :]
    bins, pair, tile, cols = cross_ref.shape
    lags = made_ref.shape[2]
    copies = []
    for group in range(tile // IMAGE_ROWS):
        rows = cross_ref[:, :, group * IMAGE_ROWS : (group + 1) * IMAGE_ROWS, :].astype(f32)
        left = rows.reshape(bins * pair * IMAGE_ROWS, cols).T.astype(bf16)
        for row in range(IMAGE_ROWS):
            place = group * IMAGE_ROWS + row
            made_ref[place] = dot(left, weight_ref[:, row * lags : (row + 1) * lags]) * scale
            copies.append(
                pltpu.make_async_copy(
                    made_ref.at[place], out_hbm.at[depth, place], sems.at[place]
                )
            )
            copies[-1].start()
    for copy in copies:
        copy.wait()


def pin(value):
    return pltpu.with_memory_space_constraint(value, pltpu.HBM)


def shards(
    source_field,
    receiver_field,
    slowness_slabs,
    slab_map,
    reference_gaps,
    reference_index,
    frequency_bins,
    shot_corner,
    *,
    ranks,
):
    rows, cols = source_field.shape[2:]
    depths = slab_map.shape[0]
    slab_count = slowness_slabs.shape[0]
    quarter = rows // 4
    tile = rows // ranks
    bins = frequency_bins.shape[0]
    slab_shape = slowness_slabs.shape[1:]
    forward_x, inverse_x = real_table(rows)
    forward_x = forward_x.T
    forward_y, inverse_y = real_table(cols)
    inverse_y = inverse_y.T

    hbm = pl.BlockSpec(memory_space=pltpu.HBM)
    vmem = pl.BlockSpec(memory_space=VMEM)
    dma = pltpu.SemaphoreType.DMA

    keep, send = pl.pallas_call(
        window_kernel,
        in_specs=[hbm] * 3,
        out_specs=[vmem] * 2,
        out_shape=[jax.ShapeDtypeStruct((2, depths, quarter, cols), bf16)] * 2,
        scratch_shapes=[
            SMEM(slab_map.shape, jnp.int32),
            SMEM(shot_corner.shape, jnp.int32),
            VMEM((1,) + slab_shape, bf16),
            dma((3,)),
        ],
        compiler_params=pltpu.CompilerParams(vmem_limit_bytes=16 << 20),
        name="window",
    )(pin(slab_map), pin(shot_corner), pin(slowness_slabs))

    def swap(value, bit, odd_bit=None):
        odd_bit = bit if odd_bit is None else odd_bit
        return lax.ppermute(
            value, "freq", [(i, i ^ (odd_bit if i & 1 else bit)) for i in range(ranks)]
        )

    held = keep + swap(send, 1)
    quarters = held[0] + swap(held[1], 2)
    bits = [1 << k for k in range(2, ranks.bit_length() - 1)]
    hops = list(zip(bits, bits[::-1]))
    for hop in hops[:-1]:
        quarters = quarters + swap(quarters, *hop)
    early_bins, quarters = lax.optimization_barrier((frequency_bins, quarters))

    march_scratch = [
        VMEM((4, rows, cols), bf16),
        VMEM((4, rows, cols), f32),
        VMEM((3, rows, cols), f32),
        VMEM((3, rows, cols), f32),
        VMEM((3, 4, rows, cols), bf16),
    ]
    flops = 2 * 4 * (1 + 3) * rows * rows * cols
    returned, bracket, kept_inverse, held_scalars = pl.pallas_call(
        first_kernel,
        in_specs=[hbm] * 9,
        out_specs=[vmem] * 4,
        out_shape=[
            jax.ShapeDtypeStruct((3, 4, rows, cols), bf16),
            jax.ShapeDtypeStruct((rows, cols), jnp.int32),
            jax.ShapeDtypeStruct((cols, cols), bf16),
            jax.ShapeDtypeStruct((8 * pl.cdiv(1 + 3 * depths, 8), cols), f32),
        ],
        scratch_shapes=[
            SMEM(frequency_bins.shape, jnp.int32),
            SMEM(reference_gaps.shape, f32),
            VMEM((4, rows, cols), bf16),
            VMEM((rows, rows), bf16),
            VMEM((cols, cols), bf16),
            VMEM((rows, rows), bf16),
            dma((9,)),
        ]
        + march_scratch,
        compiler_params=pltpu.CompilerParams(vmem_limit_bytes=28 << 20),
        cost_estimate=pl.CostEstimate(flops=flops, bytes_accessed=8 << 20, transcendentals=0),
        name="first",
    )(
        *[
            pin(value)
            for value in (
                early_bins,
                reference_gaps,
                source_field,
                receiver_field,
                forward_x,
                forward_y,
                inverse_x,
                reference_index,
                inverse_y,
            )
        ]
    )

    if hops:
        quarters = quarters + swap(quarters, *hops[-1])
    quarters, returned = lax.optimization_barrier((quarters, returned))

    across = swap(quarters, 1)
    beside = swap(quarters, 2)

    blend_scratch = [VMEM((12, BLEND_ROWS, cols), f32)] * 2
    wave_shape = jax.ShapeDtypeStruct((4, rows, cols), bf16)
    cross_shape = jax.ShapeDtypeStruct((ranks, 2, tile, cols), bf16)
    near_wave, near_cross = pl.pallas_call(
        near_kernel,
        in_specs=[vmem] * 6,
        out_specs=[vmem] * 2,
        out_shape=[
            jax.ShapeDtypeStruct((2, 4, quarter, cols), bf16),
            jax.ShapeDtypeStruct((ranks // 2, 2, tile, cols), bf16),
        ],
        scratch_shapes=blend_scratch,
        compiler_params=pltpu.CompilerParams(vmem_limit_bytes=16 << 20),
        cost_estimate=pl.CostEstimate(
            flops=flops // 4, bytes_accessed=1 << 20, transcendentals=0
        ),
        name="near",
    )(held_scalars, returned, quarters, across, bracket, kept_inverse)
    beside, near_wave, near_cross = lax.optimization_barrier((beside, near_wave, near_cross))
    corner_ways = swap(beside, 1)
    wave, cross = pl.pallas_call(
        far_kernel,
        in_specs=[vmem] * 8,
        out_specs=[vmem] * 2,
        out_shape=[wave_shape, cross_shape],
        scratch_shapes=blend_scratch,
        compiler_params=pltpu.CompilerParams(vmem_limit_bytes=20 << 20),
        cost_estimate=pl.CostEstimate(
            flops=flops // 4, bytes_accessed=1 << 20, transcendentals=0
        ),
        name="far",
    )(
        held_scalars,
        returned,
        beside,
        corner_ways,
        bracket,
        kept_inverse,
        near_wave,
        near_cross,
    )
    crosses = [cross]
    for depth in range(1, depths):
        last = depth == depths - 1
        got = pl.pallas_call(
            functools.partial(later_kernel, depth=depth, last=last),
            in_specs=[vmem] * 6 + [hbm] * 4 + [vmem],
            out_specs=[vmem] * (2 - last),
            out_shape=[wave_shape] * (1 - last) + [cross_shape],
            scratch_shapes=[
                VMEM((rows, cols), jnp.int32),
                VMEM((rows, rows), bf16),
                VMEM((cols, cols), bf16),
                VMEM((rows, rows), bf16),
                dma((4,)),
                VMEM((rows, cols), bf16),
                VMEM((3, 4, rows, cols), bf16),
            ]
            + blend_scratch
            + march_scratch,
            compiler_params=pltpu.CompilerParams(vmem_limit_bytes=32 << 20),
            cost_estimate=pl.CostEstimate(
                flops=2 * flops, bytes_accessed=8 << 20, transcendentals=0
            ),
            name="later",
        )(
            held_scalars,
            wave,
            quarters,
            beside,
            across,
            corner_ways,
            pin(reference_index),
            pin(forward_x),
            pin(forward_y),
            pin(inverse_x),
            kept_inverse,
        )
        if not last:
            wave = got[0]
        crosses.append(got[-1])

    offsets = jnp.arange(LAGS, dtype=jnp.int32) - LAGS // 2
    cycles = jnp.mod(frequency_bins[:, None] * offsets[None, :], period_bins).astype(f32)
    angles = cycles * (2.0 * math.pi / period_bins)
    lag_weights = jnp.stack([jnp.cos(angles), jnp.sin(angles)], axis=1).astype(bf16)

    scale = bins ** (-0.5)
    arrivals = [
        lax.all_to_all(cross, "freq", split_axis=0, concat_axis=0, tiled=True) for cross in crosses
    ]
    if tile % (2 * IMAGE_ROWS):
        summed = jnp.einsum(
            "dwcab,wcl->dabl", jnp.stack(arrivals), lag_weights, preferred_element_type=f32
        )
        return summed * scale
    height = bins * 2 * IMAGE_ROWS
    weights = pl.pallas_call(
        lag_kernel,
        in_specs=[vmem],
        out_specs=vmem,
        out_shape=jax.ShapeDtypeStruct((height, IMAGE_ROWS * LAGS), bf16),
        compiler_params=pltpu.CompilerParams(vmem_limit_bytes=16 << 20),
        name="lag",
    )(lag_weights.astype(f32))
    image = None
    for depth, arrived in enumerate(arrivals):
        aliased = image is not None
        image = pl.pallas_call(
            functools.partial(image_kernel, scale=scale, depth=depth, aliased=aliased),
            in_specs=[vmem, vmem] + [hbm] * aliased,
            out_specs=hbm,
            out_shape=jax.ShapeDtypeStruct((depths, tile, cols, LAGS), f32),
            scratch_shapes=[VMEM((tile, cols, LAGS), f32), dma((tile,))],
            input_output_aliases={2: 0} if aliased else {},
            compiler_params=pltpu.CompilerParams(vmem_limit_bytes=28 << 20),
            name="image",
        )(arrived, weights, *([image] if aliased else []))
    return image


def solution(mesh):
    placed = (
        P("grp", "freq", None, None),
        P("grp", "freq", None, None),
        P(("grp", "freq"), None, None),
        P("grp"),
        P("grp", None),
        P("grp", None, None),
        P(),
        P("grp"),
    )
    return jax.shard_map(
        functools.partial(shards, ranks=mesh.shape["freq"]),
        mesh=mesh,
        in_specs=placed,
        out_specs=P("grp", "freq", None, None),
        check_vma=False,
    )
```

time: 97.1 us -> 75.4 us (0.78); the launches traced: 95.5 us -> 75.2 us
  local copies, waits for them, and re-layouts: 10.5 us -> 0.02 us
  waiting for transfers between devices: 39.4 us -> 29 us
  starting transfers between devices: 14.9 us -> 18.1 us
  Pallas kernels: 29.7 us -> 27 us
    unnamed x36 -> x2, local copies, waits for them, and re-layouts: 10.5 us -> 0.01 us
    all_to_all x1 -> x2, waiting for transfers between devices: 22.3 us -> 15.4 us  [shards(): lax.all_to_all(cross, 'freq', split_axis=0, concat_axis=0, tiled=True)]
    all_to_all x1 -> x2, starting transfers between devices: 5.52 us -> 9.07 us  [shards(): lax.all_to_all(cross, 'freq', split_axis=0, concat_axis=0, tiled=True)]
    ppermute x7, waiting for transfers between devices: 17.1 us -> 13.5 us  [swap(): lax.ppermute(value, 'freq', [(i, i ^ (odd_bit if i & 1 else bit)) for i i...]
    pallas_call x4 -> x8, Pallas kernels: 29.7 us -> 27 us  [the longest x1 8.86 us: shards(): pl.pallas_call(functools.partial(later_kernel, depth=depth, last=last), i...]
  transfers between devices with their start and end apart: 8 -> 9, of which waited for: 6 -> 7; matrix products, arithmetic and copies ran while one was open for 1% -> 1% of each run, Pallas kernels for 5% -> 26%
where the time goes in v2:
time: 75.4 us; the launch traced here: 75.2 us
  waiting for transfers between devices  29 us (38%)
  Pallas kernels  27 us (36%)
  starting transfers between devices  18.1 us (24%)
  other arithmetic  0.76 us (1%)
    all_to_all x2, waiting for transfers between devices, shards(): lax.all_to_all(cross, 'freq', split_axis=0, concat_axis=0, tiled=True)  15.4 us
    ppermute x7, waiting for transfers between devices, swap(): lax.ppermute(value, 'freq', [(i, i ^ (odd_bit if i & 1 else bit)) for i i...  13.5 us
    all_to_all x2, starting transfers between devices, shards(): lax.all_to_all(cross, 'freq', split_axis=0, concat_axis=0, tiled=True)  9.07 us
    ppermute x7, starting transfers between devices, swap(): lax.ppermute(value, 'freq', [(i, i ^ (odd_bit if i & 1 else bit)) for i i...  8.99 us
    pallas_call x1, Pallas kernels, shards(): pl.pallas_call(functools.partial(later_kernel, depth=depth, last=last), i...  8.86 us
    pallas_call x2, Pallas kernels, shards(): pl.pallas_call(functools.partial(image_kernel, scale=scale, depth=depth,...  7.63 us
    pallas_call x1, Pallas kernels, shards(): pl.pallas_call(first_kernel, in_specs=[hbm] * 9, out_specs=[vmem] * 4, ou...  5.62 us
    pallas_call x1, Pallas kernels, shards(): pl.pallas_call(far_kernel, in_specs=[vmem] * 8, out_specs=[vmem] * 2, out...  2.03 us
  transfers between devices with their start and end apart: 9, of which 7 were waited for; matrix products, arithmetic and copies ran while one was open for 1% of the time, Pallas kernels for 26%

profile of v2, /device:TPU:0, one launch (start us, length us, event | category | flops | bytes accessed | tf_op | source)
XLA Modules:
  0.0 75.2 jit_solution(9216137436084188036)
XLA Ops:
  0.0 1.6 %window.1 = (bf16[2,2,128,256]{3,2,1,0:T(8,128)(2,1)S(1)}, bf16[2,2,128,256]{3,2,1,0:T(8,128)(2,1)S(1)}) custom-call(s32[2]{0:T(128)} %map_hbm.1, s32[2]{0:T(128)} %corner_hbm.1, bf16[1,768,512]{2,1,0:T(8,128)(2,1)} %slab_hbm.1), custom_call_target="tpu_custom_call" | custom-call | tf_op jit(solution)/shard_map/window/pallas_call | solution.py:587
  1.6 0.2 collective-permute-start
  1.7 1.4 %collective-permute-done = bf16[2,2,128,256]{3,2,1,0:T(8,128)(2,1)S(1)} collective-permute-done((bf16[2,2,128,256]{3,2,1,0:T(8,128)(2,1)S(1)}, bf16[2,2,128,256]{3,2,1,0:T(8,128)(2,1)S(1)}, u32[]{:S(2)}, u32[]{:S(2)}) %collective-permute-start) | collective-permute-done | bytes 262176 | tf_op jit(solution)/shard_map/ppermute | solution.py:604
  3.3 2.6 %collective-permute-start.1 = (bf16[2,128,256]{2,1,0:T(8,128)(2,1)S(1)}, bf16[2,128,256]{2,1,0:T(8,128)(2,1)S(1)}, u32[]{:S(2)}, u32[]{:S(2)}) collective-permute-start(bf16[2,128,256]{2,1,0:T(8,128)(2,1)S(1)} %slice_bitcast_fusion), channel_id=1, source_target_pairs={{0,2},{1,3},{2,0},{3,1},{4,6},{5,7},{6,4},{7,5},{8,10},{9,11},{10,... | collective-permute-start | bytes 393224 | tf_op jit(solution)/shard_map/ppermute | solution.py:604
  5.9 3.8 %collective-permute-done.1 = bf16[2,128,256]{2,1,0:T(8,128)(2,1)S(1)} collective-permute-done((bf16[2,128,256]{2,1,0:T(8,128)(2,1)S(1)}, bf16[2,128,256]{2,1,0:T(8,128)(2,1)S(1)}, u32[]{:S(2)}, u32[]{:S(2)}) %collective-permute-start.1) | collective-permute-done | bytes 131104 | tf_op jit(solution)/shard_map/ppermute | solution.py:604
  9.7 1.9 %collective-permute-start.2 = (bf16[2,128,256]{2,1,0:T(8,128)(2,1)S(1)}, bf16[2,128,256]{2,1,0:T(8,128)(2,1)S(1)}, u32[]{:S(2)}, u32[]{:S(2)}) collective-permute-start(bf16[2,128,256]{2,1,0:T(8,128)(2,1)S(1)} %fusion), channel_id=1, source_target_pairs={{0,4},{1,9},{2,6},{3,11},{4,0},{5,13},{6,2},{7,15},{8,12},{9,1},{1... | collective-permute-start | bytes 393224 | tf_op jit(solution)/shard_map/ppermute | solution.py:604
  11.6 3.9 %collective-permute-done.2 = bf16[2,128,256]{2,1,0:T(8,128)(2,1)S(1)} collective-permute-done((bf16[2,128,256]{2,1,0:T(8,128)(2,1)S(1)}, bf16[2,128,256]{2,1,0:T(8,128)(2,1)S(1)}, u32[]{:S(2)}, u32[]{:S(2)}) %collective-permute-start.2) | collective-permute-done | bytes 131104 | tf_op jit(solution)/shard_map/ppermute | solution.py:604
  15.6 2.5 %collective-permute-start.3 = (bf16[2,128,256]{2,1,0:T(8,128)(2,1)S(1)}, bf16[2,128,256]{2,1,0:T(8,128)(2,1)S(1)}, u32[]{:S(2)}, u32[]{:S(2)}) collective-permute-start(bf16[2,128,256]{2,1,0:T(8,128)(2,1)S(1)} %add.36), channel_id=1, source_target_pairs={{0,8},{1,5},{2,10},{3,7},{4,12},{5,1},{6,14},{7,3},{8,0},{9,13},{1... | collective-permute-start | bytes 393224 | tf_op jit(solution)/shard_map/ppermute | solution.py:604
  18.1 5.6 %first.1 = (bf16[3,4,512,256]{3,2,1,0:T(8,128)(2,1)S(1)}, s32[512,256]{1,0:T(8,128)S(1)}, bf16[256,256]{1,0:T(8,128)(2,1)S(1)}, f32[8,256]{1,0:T(8,128)S(1)}) custom-call(s32[16]{0:T(128)} %bins_hbm, f32[2,3]{1,0:T(2,128)} %gaps_hbm.1, bf16[2,1,512,256]{3,2,1,0:T(8,128)(2,1)} %source_hbm.1, bf16[2,1,512,256]{3,2,1,0:T(8,128)(2,1)} %receiver_hbm.1, ...), custom_call_target="tpu_custom_call" | custom-call | flops 2147483648 | bytes 8388608 | tf_op jit(solution)/shard_map/first/pallas_call | solution.py:624
  23.9 1.7 %collective-permute-start.4 = (bf16[2,128,256]{2,1,0:T(8,128)(2,1)S(1)}, bf16[2,128,256]{2,1,0:T(8,128)(2,1)S(1)}, u32[]{:S(2)}, u32[]{:S(2)}) collective-permute-start(bf16[2,128,256]{2,1,0:T(8,128)(2,1)S(1)} %add.37.q0), channel_id=1, source_target_pairs={{0,2},{1,3},{2,0},{3,1},{4,6},{5,7},{6,4},{7,5},{8,10},{9,11},{10,... | collective-permute-start | bytes 393224 | tf_op jit(solution)/shard_map/ppermute | solution.py:604
  25.6 1.2 %near.1 = (bf16[2,4,128,256]{3,2,1,0:T(8,128)(2,1)S(1)}, bf16[8,2,32,256]{3,2,1,0:T(8,128)(2,1)S(1)}) custom-call(f32[8,256]{1,0:T(8,128)S(1)} %get-tuple-element.25.held_ref, bf16[3,4,512,256]{3,2,1,0:T(8,128)(2,1)S(1)} %get-tuple-element.28.returned_ref, bf16[2,128,256]{2,1,0:T(8,128)(2,1)S(1)} %add.37.q0, ...), custom_call_target="tpu_custom_call" | custom-call | flops 536870912 | bytes 1048576 | tf_op jit(solution)/shard_map/near/pallas_call | solution.py:674
  26.7 3.0 %collective-permute-done.4.q1 = bf16[2,128,256]{2,1,0:T(8,128)(2,1)S(1)} collective-permute-done((bf16[2,128,256]{2,1,0:T(8,128)(2,1)S(1)}, bf16[2,128,256]{2,1,0:T(8,128)(2,1)S(1)}, u32[]{:S(2)}, u32[]{:S(2)}) %collective-permute-start.4) | collective-permute-done | bytes 131104 | tf_op jit(solution)/shard_map/ppermute | solution.py:604
  29.8 1.3 %collective-permute-done.6.q3 = bf16[2,128,256]{2,1,0:T(8,128)(2,1)S(1)} collective-permute-done((bf16[2,128,256]{2,1,0:T(8,128)(2,1)S(1)}, bf16[2,128,256]{2,1,0:T(8,128)(2,1)S(1)}, u32[]{:S(2)}, u32[]{:S(2)}) %collective-permute-start.6) | collective-permute-done | bytes 131104 | tf_op jit(solution)/shard_map/ppermute | solution.py:604
  31.1 2.0 %far.1 = (bf16[4,512,256]{2,1,0:T(8,128)(2,1)S(1)}, bf16[16,2,32,256]{3,2,1,0:T(8,128)(2,1)}) custom-call(f32[8,256]{1,0:T(8,128)S(1)} %get-tuple-element.25.held_ref, bf16[3,4,512,256]{3,2,1,0:T(8,128)(2,1)S(1)} %get-tuple-element.28.returned_ref, bf16[2,128,256]{2,1,0:T(8,128)(2,1)S(1)} %collective-permute-done.4.q1, ...), custom_call_target="tpu_custom_call" | custom-call | flops 536870912 | bytes 1048576 | tf_op jit(solution)/shard_map/far/pallas_call | solution.py:691
  33.2 5.0 %all-to-all-start.1 = ((bf16[16,2,32,256]{3,2,1,0:T(8,128)(2,1)}), bf16[16,2,32,256]{3,2,1,0:T(8,128)(2,1)S(1)}, u32[]{:S(2)}, u32[]{:S(2)}) async-start(bf16[16,2,32,256]{3,2,1,0:T(8,128)(2,1)} %get-tuple-element.38), calls=%async_computation.1 | async-start | bytes 1048576 | tf_op jit(solution)/shard_map/all_to_all | solution.py:760
  38.1 8.9 %later.1 = bf16[16,2,32,256]{3,2,1,0:T(8,128)(2,1)} custom-call(f32[8,256]{1,0:T(8,128)S(1)} %get-tuple-element.25.held_ref, bf16[4,512,256]{2,1,0:T(8,128)(2,1)S(1)} %get-tuple-element.37.wave_ref, bf16[2,128,256]{2,1,0:T(8,128)(2,1)S(1)} %add.37.q0, bf16[2,128,256]{2,1,0:T(8,128)(2,1)S(1)} %collective-permute-done.4.q1, ...), custom_call_target="tpu_custom_call" | custom-call | flops 4294967296 | bytes 8388608 | tf_op jit(solution)/shard_map/later/pallas_call | solution.py:715
  47.0 5.6 %all-to-all-done.1.refs_0_ = bf16[16,2,32,256]{3,2,1,0:T(8,128)(2,1)S(1)} async-done(((bf16[16,2,32,256]{3,2,1,0:T(8,128)(2,1)}), bf16[16,2,32,256]{3,2,1,0:T(8,128)(2,1)S(1)}, u32[]{:S(2)}, u32[]{:S(2)}) %all-to-all-start.1) | async-done | bytes 524320 | tf_op jit(solution)/shard_map/all_to_all | solution.py:760
  52.6 4.1 %all-to-all-start = ((bf16[16,2,32,256]{3,2,1,0:T(8,128)(2,1)}), bf16[16,2,32,256]{3,2,1,0:T(8,128)(2,1)S(1)}, u32[]{:S(2)}, u32[]{:S(2)}) async-start(bf16[16,2,32,256]{3,2,1,0:T(8,128)(2,1)} %later.1), calls=%async_computation | async-start | bytes 1048576 | tf_op jit(solution)/shard_map/all_to_all | solution.py:760
  56.7 0.1 fusion.1
  56.8 0.5 cosine_convert_fusion
  57.4 0.2 lag.1.refs_1_
  57.6 3.8 %image.2.refs_2_ = f32[2,32,256,256]{3,2,1,0:T(8,128)} custom-call(bf16[16,2,32,256]{3,2,1,0:T(8,128)(2,1)S(1)} %all-to-all-done.1.refs_0_, bf16[256,2048]{1,0:T(8,128)(2,1)S(1)} %lag.1.refs_1_), custom_call_target="tpu_custom_call" | custom-call | tf_op jit(solution)/shard_map/image/pallas_call | solution.py:779
  61.4 9.8 %all-to-all-done.refs_0_ = bf16[16,2,32,256]{3,2,1,0:T(8,128)(2,1)S(1)} async-done(((bf16[16,2,32,256]{3,2,1,0:T(8,128)(2,1)}), bf16[16,2,32,256]{3,2,1,0:T(8,128)(2,1)S(1)}, u32[]{:S(2)}, u32[]{:S(2)}) %all-to-all-start) | async-done | bytes 524320 | tf_op jit(solution)/shard_map/all_to_all | solution.py:760
  71.2 3.8 %image.3 = f32[2,32,256,256]{3,2,1,0:T(8,128)} custom-call(bf16[16,2,32,256]{3,2,1,0:T(8,128)(2,1)S(1)} %all-to-all-done.refs_0_, bf16[256,2048]{1,0:T(8,128)(2,1)S(1)} %lag.1.refs_1_, f32[2,32,256,256]{3,2,1,0:T(8,128)} %image.2.refs_2_), custom_call_target="tpu_custom_call", output_to_operand_aliasing={{}: (2, {})} | custom-call | tf_op jit(solution)/shard_map/image/pallas_call | solution.py:779
  (13 shorter events, 0.3 us)
Async XLA Ops:
  1.6 1.6 %collective-permute-start = (bf16[2,2,128,256]{3,2,1,0:T(8,128)(2,1)S(1)}, bf16[2,2,128,256]{3,2,1,0:T(8,128)(2,1)S(1)}, u32[]{:S(2)}, u32[]{:S(2)}) collective-permute-start(bf16[2,2,128,256]{3,2,1,0:T(8,128)(2,1)S(1)} %get-tuple-element.23), channel_id=1, source_target_pairs={{0,1},{1,0},{2,3},{3,2},{4,5},{5,4},{6,7},{7,6},{8,9},{9,8},{10,11... | collective-permute-start | bytes 786440 | tf_op jit(solution)/shard_map/ppermute | solution.py:604
  3.3 6.4 %collective-permute-start.1 = (bf16[2,128,256]{2,1,0:T(8,128)(2,1)S(1)}, bf16[2,128,256]{2,1,0:T(8,128)(2,1)S(1)}, u32[]{:S(2)}, u32[]{:S(2)}) collective-permute-start(bf16[2,128,256]{2,1,0:T(8,128)(2,1)S(1)} %slice_bitcast_fusion), channel_id=1, source_target_pairs={{0,2},{1,3},{2,0},{3,1},{4,6},{5,7},{6,4},{7,5},{8,10},{9,11},{10,... | collective-permute-start | bytes 393224 | tf_op jit(solution)/shard_map/ppermute | solution.py:604
  9.7 5.8 %collective-permute-start.2 = (bf16[2,128,256]{2,1,0:T(8,128)(2,1)S(1)}, bf16[2,128,256]{2,1,0:T(8,128)(2,1)S(1)}, u32[]{:S(2)}, u32[]{:S(2)}) collective-permute-start(bf16[2,128,256]{2,1,0:T(8,128)(2,1)S(1)} %fusion), channel_id=1, source_target_pairs={{0,4},{1,9},{2,6},{3,11},{4,0},{5,13},{6,2},{7,15},{8,12},{9,1},{1... | collective-permute-start | bytes 393224 | tf_op jit(solution)/shard_map/ppermute | solution.py:604
  15.6 41.2 %copy-start = (s32[16]{0:T(128)S(1)}, s32[16]{0:T(128)}, u32[]{:S(2)}) copy-start(s32[16]{0:T(128)} %bins_hbm) | copy-start | bytes 196
  15.6 8.2 %collective-permute-start.3 = (bf16[2,128,256]{2,1,0:T(8,128)(2,1)S(1)}, bf16[2,128,256]{2,1,0:T(8,128)(2,1)S(1)}, u32[]{:S(2)}, u32[]{:S(2)}) collective-permute-start(bf16[2,128,256]{2,1,0:T(8,128)(2,1)S(1)} %add.36), channel_id=1, source_target_pairs={{0,8},{1,5},{2,10},{3,7},{4,12},{5,1},{6,14},{7,3},{8,0},{9,13},{1... | collective-permute-start | bytes 393224 | tf_op jit(solution)/shard_map/ppermute | solution.py:604
  23.8 1.8 %collective-permute-start.5 = (bf16[2,128,256]{2,1,0:T(8,128)(2,1)S(1)}, bf16[2,128,256]{2,1,0:T(8,128)(2,1)S(1)}, u32[]{:S(2)}, u32[]{:S(2)}) collective-permute-start(bf16[2,128,256]{2,1,0:T(8,128)(2,1)S(1)} %add.37.q0), channel_id=1, source_target_pairs={{0,1},{1,0},{2,3},{3,2},{4,5},{5,4},{6,7},{7,6},{8,9},{9,8},{10,11... | collective-permute-start | bytes 393224 | tf_op jit(solution)/shard_map/ppermute | solution.py:604
  23.9 5.9 %collective-permute-start.4 = (bf16[2,128,256]{2,1,0:T(8,128)(2,1)S(1)}, bf16[2,128,256]{2,1,0:T(8,128)(2,1)S(1)}, u32[]{:S(2)}, u32[]{:S(2)}) collective-permute-start(bf16[2,128,256]{2,1,0:T(8,128)(2,1)S(1)} %add.37.q0), channel_id=1, source_target_pairs={{0,2},{1,3},{2,0},{3,1},{4,6},{5,7},{6,4},{7,5},{8,10},{9,11},{10,... | collective-permute-start | bytes 393224 | tf_op jit(solution)/shard_map/ppermute | solution.py:604
  29.8 1.3 %collective-permute-start.6 = (bf16[2,128,256]{2,1,0:T(8,128)(2,1)S(1)}, bf16[2,128,256]{2,1,0:T(8,128)(2,1)S(1)}, u32[]{:S(2)}, u32[]{:S(2)}) collective-permute-start(bf16[2,128,256]{2,1,0:T(8,128)(2,1)S(1)} %collective-permute-done.4.q1), channel_id=1, source_target_pairs={{0,1},{1,0},{2,3},{3,2},{4,5},{5,4},{6,7},{7,6},{8,9},{9,8},{10,11... | collective-permute-start | bytes 393224 | tf_op jit(solution)/shard_map/ppermute | solution.py:604
  33.2 19.4 %all-to-all-start.1 = ((bf16[16,2,32,256]{3,2,1,0:T(8,128)(2,1)}), bf16[16,2,32,256]{3,2,1,0:T(8,128)(2,1)S(1)}, u32[]{:S(2)}, u32[]{:S(2)}) async-start(bf16[16,2,32,256]{3,2,1,0:T(8,128)(2,1)} %get-tuple-element.38), calls=%async_computation.1 | async-start | bytes 1048576 | tf_op jit(solution)/shard_map/all_to_all | solution.py:760
  52.6 18.6 %all-to-all-start = ((bf16[16,2,32,256]{3,2,1,0:T(8,128)(2,1)}), bf16[16,2,32,256]{3,2,1,0:T(8,128)(2,1)S(1)}, u32[]{:S(2)}, u32[]{:S(2)}) async-start(bf16[16,2,32,256]{3,2,1,0:T(8,128)(2,1)} %later.1), calls=%async_computation | async-start | bytes 1048576 | tf_op jit(solution)/shard_map/all_to_all | solution.py:760

commit v3 on v2

v3 whole, which is shorter than its diff:
```python
import functools
import math

import jax
import jax.numpy as jnp
import numpy as np
from jax import lax
from jax.experimental import pallas as pl
from jax.experimental.pallas import tpu as pltpu
from jax.sharding import PartitionSpec as P

LAGS = 256

cell_width = 0.0125
layer_thick = 0.0125
bin_hertz = 0.5
period_bins = 500
slow_base = 0.3

VMEM = pltpu.VMEM
SMEM = pltpu.SMEM
f32 = jnp.float32
bf16 = jnp.bfloat16


def real_table(length):
    half = length // 2
    steps = np.arange(length, dtype=np.int64)
    wave = np.concatenate([np.arange(half), [half], np.arange(1, half)])
    phases = np.mod(steps[:, None] * wave[None, :], length).astype(np.float32)
    angles = phases * np.float32(2.0 * math.pi / length)
    scale = np.float32(1.0 / math.sqrt(length))
    is_cos = np.arange(length) <= half
    table = np.where(is_cos[None, :], np.cos(angles), np.sin(angles)) * scale
    twice = np.where((wave == 0) | (wave == half), 1.0, 2.0)
    forward = jnp.asarray(table.astype(np.float32)).astype(bf16)
    inverse = (forward.astype(f32) * jnp.asarray(twice[None, :], f32)).astype(bf16)
    return forward, inverse


def sin_cos(angle):
    turns = jnp.floor(angle * (2.0 / math.pi) + 0.5)
    rest = angle - turns * 1.5707397460937500
    rest = rest - turns * 5.6580702948965924e-05
    quadrant = turns.astype(jnp.int32)
    square = rest * rest
    sine = rest + rest * square * (
        -1.6666654611e-1 + square * (8.3321608736e-3 - square * 1.9515295891e-4)
    )
    cosine = (
        1.0
        - 0.5 * square
        + square
        * square
        * (4.166664568298827e-2 + square * (-1.388731625493765e-3 + square * 2.443315711809948e-5))
    )
    odd = (quadrant & 1) == 1
    out_sin = jnp.where(odd, cosine, sine)
    out_cos = jnp.where(odd, sine, cosine)
    out_sin = jnp.where((quadrant & 2) == 2, -out_sin, out_sin)
    out_cos = jnp.where(((quadrant + 1) & 2) == 2, -out_cos, out_cos)
    return out_sin, out_cos


def references_of(gaps_ref, depth):
    first = slow_base + gaps_ref[depth, 0]
    second = first + gaps_ref[depth, 1]
    third = second + gaps_ref[depth, 2]
    return first, second, third


def scalars_of(held_ref, depth):
    rows = [held_ref[row : row + 1] for row in (0, *range(1 + 3 * depth, 4 + 3 * depth))]
    return rows[0], tuple(rows[1:])


def angular_of(bins_ref):
    return bins_ref[lax.axis_index("freq")].astype(f32) * (2.0 * math.pi * bin_hertz)


def phase_block(reach, base_turn, squares):
    radicand = reach - squares
    root = jnp.sqrt(jnp.abs(radicand)) * layer_thick
    travelling = radicand > 0.0
    fading = jnp.where(travelling, 1.0, jnp.exp(-root))
    sine, cosine = sin_cos(jnp.where(travelling, root, 0.0) - base_turn)
    return fading * cosine, fading * sine


def make_phases(cos_ref, sin_ref, angular, reference):
    rows, cols = cos_ref.shape
    half = rows // 2
    reach = (angular * reference) * (angular * reference)
    base_turn = angular * layer_thick * reference
    step_x = 2.0 * math.pi / (rows * cell_width)
    step_y = 2.0 * math.pi / (cols * cell_width)
    lane = lax.broadcasted_iota(jnp.int32, (8, cols), 1)
    wave_y = jnp.where(lane <= cols // 2, lane, lane - cols // 2).astype(f32) * step_y
    square_y = wave_y * wave_y
    tall = 64

    def body(block, carry):
        start = pl.multiple_of(block * tall, tall)
        row = lax.broadcasted_iota(jnp.int32, (tall, cols), 0) + start
        wave_x = row.astype(f32) * step_x
        cosine, sine = phase_block(
            reach, base_turn, wave_x * wave_x + jnp.concatenate([square_y] * (tall // 8), axis=0)
        )
        cos_ref[pl.ds(start, tall), :] = cosine
        sin_ref[pl.ds(start, tall), :] = sine
        cos_ref[pl.ds(half + start, tall), :] = cosine
        sin_ref[pl.ds(half + start, tall), :] = sine
        return carry

    lax.fori_loop(0, half // tall, body, 0)
    edge = (half * step_x) ** 2
    cosine, sine = phase_block(reach, base_turn, edge + square_y)
    top = lax.broadcasted_iota(jnp.int32, (8, cols), 0) == 0
    cos_ref[half : half + 8, :] = jnp.where(top, cosine, cos_ref[half : half + 8, :])
    sin_ref[half : half + 8, :] = jnp.where(top, sine, sin_ref[half : half + 8, :])


def dot(left, right):
    return jnp.dot(left, right, preferred_element_type=f32)


def march_out(fill_half, forward_x, scalars, half_ref, spectrum, ready=((), ())):
    angular, references = scalars
    spec_ref, cos_ref, sin_ref = spectrum
    for j in range(3):
        make_phases(cos_ref.at[j], sin_ref.at[j], angular, references[j])
    for wait in ready[0]:
        wait()
    for plane in range(4):
        fill_half(plane)
    for wait in ready[1]:
        wait()
    for plane in range(4):
        spec_ref[plane] = dot(forward_x[...], half_ref[plane])


def march_back(spectrum, inverse_x, shift_ref, out_ref, ready=()):
    spec_ref, cos_ref, sin_ref = spectrum
    for j in range(3):
        for field in range(2):
            real, imag = spec_ref[2 * field], spec_ref[2 * field + 1]
            cosine, sine = cos_ref[j], sin_ref[j]
            shift_ref[j, 2 * field] = (cosine * real - sine * imag).astype(bf16)
            shift_ref[j, 2 * field + 1] = (cosine * imag + sine * real).astype(bf16)
        if j == 0:
            for wait in ready:
                wait()
        for plane in range(4):
            out_ref[j, plane] = dot(inverse_x[...], shift_ref[j, plane]).astype(bf16)


def blend(returned_ref, slow_ref, bracket_ref, inverse_y, scalars, parts, put_wave, put_cross, starts):
    tall, cols = slow_ref.shape[1:]
    chunk = 16
    angular, (low, mid, high) = scalars
    slope_low = 1.0 / (mid - low)
    slope_high = 1.0 / (high - mid)
    def first_row(block):
        return pl.multiple_of(starts[block], tall)

    def fill(part_ref, block):
        left = returned_ref[:, :, pl.ds(first_row(block), tall), :].reshape(12 * tall, cols)
        part_ref[...] = dot(left, inverse_y[...]).reshape(12, tall, cols)

    def mix(part_ref, block):
        start = first_row(block)
        crossed = []
        for piece in range(tall // chunk):
            within = slice(piece * chunk, (piece + 1) * chunk)
            here = pl.ds(start + piece * chunk, chunk)
            slow = slow_ref[block, within].astype(f32)
            lower = bracket_ref[here, :] == 0
            weight = jnp.where(lower, (slow - low) * slope_low, (slow - mid) * slope_high)
            weight = jnp.minimum(jnp.maximum(weight, 0.0), 1.0)
            sine, cosine = sin_cos(slow * (angular * layer_thick))
            halves = []
            for plane in range(4):
                first, second, third = [part_ref[4 * j + plane, within] for j in range(3)]
                bottom = jnp.where(lower, first, second)
                top = jnp.where(lower, second, third)
                halves.append(bottom + weight * (top - bottom))
            fresh = []
            for field in range(2):
                real, imag = halves[2 * field], halves[2 * field + 1]
                fresh.append((cosine * real - sine * imag).astype(bf16))
                fresh.append((cosine * imag + sine * real).astype(bf16))
            if put_wave is not None:
                for plane in range(4):
                    put_wave(block, within, plane, fresh[plane])
            s_real, s_imag, r_real, r_imag = [value.astype(f32) for value in fresh]
            crossed.append(
                (
                    (s_real * r_real - s_imag * r_imag).astype(bf16),
                    (s_real * r_imag + s_imag * r_real).astype(bf16),
                )
            )
        for side in range(2):
            put_cross(block, side, jnp.concatenate([pair[side] for pair in crossed], axis=0))

    even, odd = parts
    fill(even, 0)
    for block in range(len(starts)):
        here, other = (even, odd) if block % 2 == 0 else (odd, even)
        if block + 1 < len(starts):
            fill(other, block + 1)
        mix(here, block)


def put_tiles(cross_ref, first, side, values):
    tile = cross_ref.shape[2]
    for part in range(values.shape[0] // tile):
        cross_ref[first + part, side] = values[part * tile : (part + 1) * tile]


PIECES = 4


def piece_starts(piece):
    rank = lax.axis_index("freq")
    core, place = rank % 2, (rank // 2) % PIECES
    return [
        [(side * PIECES + (place ^ step)) * piece for step in range(PIECES)]
        for side in (core, 1 - core)
    ]


def window_kernel(
    map_hbm, corner_hbm, slab_hbm, keep_ref, send_ref, map_ref, corner_ref, slab_ref, sems
):
    depths, piece, cols = keep_ref.shape[1:]
    slab_count = slab_hbm.shape[0]
    tall, wide = slab_hbm.shape[1:]
    copies = [
        pltpu.make_async_copy(map_hbm, map_ref, sems.at[0]),
        pltpu.make_async_copy(corner_hbm, corner_ref, sems.at[1]),
    ]
    for copy in copies:
        copy.start()
    if slab_count == 1:
        whole = pltpu.make_async_copy(slab_hbm.at[0], slab_ref.at[0], sems.at[2])
        whole.start()
    for copy in copies:
        copy.wait()
    if slab_count == 1:
        whole.wait()
    rank = lax.axis_index("freq")
    rows = 2 * PIECES * piece
    first_row = jnp.minimum((corner_ref[0] // 16) * 16, tall - rows - 16)
    first_col = jnp.minimum((corner_ref[1] // 128) * 128, wide - cols - 128)
    above = corner_ref[0] - first_row
    before = corner_ref[1] - first_col
    reach = piece + 16
    span = cols + 128
    for depth in range(depths):
        slab = map_ref[depth]
        mine = slab // slab_count == rank

        @pl.when(mine)
        def _():
            if slab_count == 1:
                here = slab_ref.at[0]
            else:
                here = slab_ref.at[0]
                copy = pltpu.make_async_copy(
                    slab_hbm.at[lax.rem(slab, slab_count)], here, sems.at[2]
                )
                copy.start()
                copy.wait()
            for target, starts in zip((keep_ref, send_ref), piece_starts(piece)):
                for step, start in enumerate(starts):
                    block = here[
                        pl.ds(pl.multiple_of(first_row + start, 16), reach),
                        pl.ds(pl.multiple_of(first_col, 128), span),
                    ].astype(f32)
                    block = pltpu.roll(block, lax.rem(span - before, span), 1)[:, :cols]
                    block = pltpu.roll(block, lax.rem(reach - above, reach), 0)[:piece]
                    target[step, depth] = block.astype(bf16)

        @pl.when(jnp.logical_not(mine))
        def _():
            for target in (keep_ref, send_ref):
                target[:, depth] = jnp.zeros((PIECES, piece, cols), bf16)


def fetch(pairs, sems):
    copies = [
        pltpu.make_async_copy(source, target, sems.at[index])
        for index, (source, target) in enumerate(pairs)
    ]
    for copy in copies:
        copy.start()
    return [copy.wait for copy in copies]


def out_kernel(
    bins_hbm,
    gaps_hbm,
    source_hbm,
    receiver_hbm,
    forward_x_hbm,
    forward_y_hbm,
    spec_ref,
    cos_ref,
    sin_ref,
    held_ref,
    bins_ref,
    gaps_ref,
    wave_ref,
    forward_x,
    forward_y,
    half_ref,
    sems,
):
    waits = fetch(
        [
            (bins_hbm, bins_ref),
            (gaps_hbm, gaps_ref),
            (forward_y_hbm, forward_y),
            (source_hbm.at[:, 0], wave_ref.at[0:2]),
            (receiver_hbm.at[:, 0], wave_ref.at[2:4]),
            (forward_x_hbm, forward_x),
        ],
        sems,
    )
    waits[0]()
    waits[1]()
    angular = angular_of(bins_ref)
    held_ref[0:1] = jnp.full((1, held_ref.shape[1]), angular, f32)
    for depth in range(gaps_ref.shape[0]):
        for j, reference in enumerate(references_of(gaps_ref, depth)):
            row = 1 + 3 * depth + j
            held_ref[row : row + 1] = jnp.full((1, held_ref.shape[1]), reference, f32)

    def fill_half(plane):
        half = dot(wave_ref[plane], forward_y[...])
        half_ref[plane] = (half if plane < 3 else -half).astype(bf16)

    march_out(
        fill_half,
        forward_x,
        (angular, references_of(gaps_ref, 0)),
        half_ref,
        (spec_ref, cos_ref, sin_ref),
        ready=(waits[2:5], waits[5:]),
    )


def back_kernel(
    spec_ref,
    cos_ref,
    sin_ref,
    inverse_x_hbm,
    bracket_hbm,
    inverse_y_hbm,
    out_ref,
    bracket_ref,
    inverse_y,
    inverse_x,
    shift_ref,
    sems,
):
    waits = fetch(
        [
            (inverse_x_hbm, inverse_x),
            (bracket_hbm.at[0], bracket_ref),
            (inverse_y_hbm, inverse_y),
        ],
        sems,
    )
    march_back((spec_ref, cos_ref, sin_ref), inverse_x, shift_ref, out_ref, waits[:1])
    for wait in waits[1:]:
        wait()


def mix_kernel(*refs, depth, far, last):
    held_ref, returned_ref, slow_ref, bracket_ref, inverse_y = refs[:5]
    rest = refs[5:]
    if far:
        near_cross, rest = rest[0], rest[1:]
    if not last:
        wave_ref, rest = rest[0], rest[1:]
    cross_ref, even, odd = rest
    piece = slow_ref.shape[2]
    tile = cross_ref.shape[2]
    tiles = piece // tile
    near_starts, far_starts = piece_starts(piece)
    starts = far_starts if far else near_starts
    if far:
        for step, start in enumerate(near_starts):
            cross_ref[pl.ds(start // tile, tiles)] = near_cross[step * tiles : (step + 1) * tiles]

    def put_wave(block, within, plane, values):
        wave_ref[plane, block * piece + within.start : block * piece + within.stop] = values

    def put_cross(block, side, values):
        put_tiles(cross_ref, starts[block] // tile if far else block * tiles, side, values)

    blend(
        returned_ref,
        slow_ref.at[:, depth],
        bracket_ref,
        inverse_y,
        scalars_of(held_ref, depth),
        (even, odd),
        None if last else put_wave,
        put_cross,
        starts,
    )


def march_kernel(
    held_ref,
    near_wave,
    far_wave,
    bracket_hbm,
    forward_x_hbm,
    forward_y_hbm,
    inverse_x_hbm,
    out_ref,
    bracket_ref,
    forward_x,
    forward_y,
    inverse_x,
    sems,
    half_ref,
    shift_ref,
    *spectrum,
    depth,
):
    waits = fetch(
        [
            (forward_y_hbm, forward_y),
            (forward_x_hbm, forward_x),
            (inverse_x_hbm, inverse_x),
            (bracket_hbm.at[depth], bracket_ref),
        ],
        sems,
    )
    piece = near_wave.shape[1] // PIECES

    def fill_half(plane):
        for starts, wave_ref in zip(piece_starts(piece), (near_wave, far_wave)):
            half = dot(wave_ref[plane], forward_y[...]).astype(bf16)
            for step, start in enumerate(starts):
                here = pl.ds(pl.multiple_of(start, piece), piece)
                half_ref[plane, here, :] = half[step * piece : (step + 1) * piece]

    march_out(
        fill_half,
        forward_x,
        scalars_of(held_ref, depth),
        half_ref,
        spectrum,
        ready=(waits[:1], waits[1:2]),
    )
    march_back(spectrum, inverse_x, shift_ref, out_ref, waits[2:3])
    waits[3]()


IMAGE_ROWS = 8


def lag_kernel(lag_ref, weight_ref):
    bins, pair, lags = lag_ref.shape
    height = bins * pair * IMAGE_ROWS
    table = jnp.broadcast_to(
        lag_ref[...].reshape(bins * pair, 1, lags), (bins * pair, IMAGE_ROWS, lags)
    ).reshape(height, lags)
    place = lax.broadcasted_iota(jnp.int32, (height, lags), 0) % IMAGE_ROWS
    for row in range(IMAGE_ROWS):
        weight_ref[:, row * lags : (row + 1) * lags] = jnp.where(place == row, table, 0.0).astype(
            bf16
        )


def image_kernel(*refs, scale, depth, aliased):
    cross_ref, weight_ref = refs[:2]
    out_hbm, made_ref, sems = refs[2 + aliased :]
    bins, pair, tile, cols = cross_ref.shape
    lags = made_ref.shape[2]
    copies = []
    for group in range(tile // IMAGE_ROWS):
        rows = cross_ref[:, :, group * IMAGE_ROWS : (group + 1) * IMAGE_ROWS, :].astype(f32)
        left = rows.reshape(bins * pair * IMAGE_ROWS, cols).T.astype(bf16)
        for row in range(IMAGE_ROWS):
            place = group * IMAGE_ROWS + row
            made_ref[place] = dot(left, weight_ref[:, row * lags : (row + 1) * lags]) * scale
            copies.append(
                pltpu.make_async_copy(
                    made_ref.at[place], out_hbm.at[depth, place], sems.at[place]
                )
            )
            copies[-1].start()
    for copy in copies:
        copy.wait()


def pin(value):
    return pltpu.with_memory_space_constraint(value, pltpu.HBM)


def shards(
    source_field,
    receiver_field,
    slowness_slabs,
    slab_map,
    reference_gaps,
    reference_index,
    frequency_bins,
    shot_corner,
    *,
    ranks,
):
    rows, cols = source_field.shape[2:]
    depths = slab_map.shape[0]
    slab_count = slowness_slabs.shape[0]
    half = rows // 2
    piece = half // PIECES
    tile = rows // ranks
    bins = frequency_bins.shape[0]
    slab_shape = slowness_slabs.shape[1:]
    forward_x, inverse_x = real_table(rows)
    forward_x = forward_x.T
    forward_y, inverse_y = real_table(cols)
    inverse_y = inverse_y.T

    hbm = pl.BlockSpec(memory_space=pltpu.HBM)
    vmem = pl.BlockSpec(memory_space=VMEM)
    dma = pltpu.SemaphoreType.DMA

    keep, send = pl.pallas_call(
        window_kernel,
        in_specs=[hbm] * 3,
        out_specs=[vmem] * 2,
        out_shape=[jax.ShapeDtypeStruct((PIECES, depths, piece, cols), bf16)] * 2,
        scratch_shapes=[
            SMEM(slab_map.shape, jnp.int32),
            SMEM(shot_corner.shape, jnp.int32),
            VMEM((1,) + slab_shape, bf16),
            dma((3,)),
        ],
        compiler_params=pltpu.CompilerParams(vmem_limit_bytes=16 << 20),
        name="window",
    )(pin(slab_map), pin(shot_corner), pin(slowness_slabs))

    def swap(value, bit):
        return lax.ppermute(value, "freq", [(i, i ^ bit) for i in range(ranks)])

    held = keep + swap(send, 1)
    early_bins, held = lax.optimization_barrier((frequency_bins, held))
    spectrum_shapes = [
        jax.ShapeDtypeStruct((4, rows, cols), f32),
        jax.ShapeDtypeStruct((3, rows, cols), f32),
        jax.ShapeDtypeStruct((3, rows, cols), f32),
    ]
    returned_shape = jax.ShapeDtypeStruct((3, 4, rows, cols), bf16)
    flops = 2 * 4 * (1 + 3) * rows * rows * cols
    *spectrum, held_scalars = pl.pallas_call(
        out_kernel,
        in_specs=[hbm] * 6,
        out_specs=[vmem] * 4,
        out_shape=spectrum_shapes
        + [jax.ShapeDtypeStruct((8 * pl.cdiv(1 + 3 * depths, 8), cols), f32)],
        scratch_shapes=[
            SMEM(frequency_bins.shape, jnp.int32),
            SMEM(reference_gaps.shape, f32),
            VMEM((4, rows, cols), bf16),
            VMEM((rows, rows), bf16),
            VMEM((cols, cols), bf16),
            VMEM((4, rows, cols), bf16),
            dma((6,)),
        ],
        compiler_params=pltpu.CompilerParams(vmem_limit_bytes=20 << 20),
        cost_estimate=pl.CostEstimate(flops=flops // 2, bytes_accessed=4 << 20, transcendentals=0),
        name="out",
    )(
        *[
            pin(value)
            for value in (
                early_bins,
                reference_gaps,
                source_field,
                receiver_field,
                forward_x,
                forward_y,
            )
        ]
    )
    own = held[0] + sum(swap(held[step], 2 * step) for step in range(1, PIECES))
    own, spectrum = lax.optimization_barrier((own, spectrum))
    returned, bracket, kept_inverse = pl.pallas_call(
        back_kernel,
        in_specs=[vmem] * 3 + [hbm] * 3,
        out_specs=[vmem] * 3,
        out_shape=[
            returned_shape,
            jax.ShapeDtypeStruct((rows, cols), jnp.int32),
            jax.ShapeDtypeStruct((cols, cols), bf16),
        ],
        scratch_shapes=[
            VMEM((rows, rows), bf16),
            VMEM((3, 4, rows, cols), bf16),
            dma((3,)),
        ],
        compiler_params=pltpu.CompilerParams(vmem_limit_bytes=24 << 20),
        cost_estimate=pl.CostEstimate(flops=flops, bytes_accessed=4 << 20, transcendentals=0),
        name="back",
    )(*spectrum, pin(inverse_x), pin(reference_index), pin(inverse_y))
    bit = 2 * PIECES
    while bit < ranks:
        own = own + swap(own, bit)
        bit *= 2
    own, returned = lax.optimization_barrier((own, returned))
    near_slow = jnp.stack([own] + [swap(own, 2 * step) for step in range(1, PIECES)])
    far_slow = swap(near_slow, 1)

    blend_scratch = [VMEM((12, piece, cols), f32)] * 2
    wave_shape = jax.ShapeDtypeStruct((4, half, cols), bf16)

    def mix(depth, far, *operands):
        last = depth == depths - 1
        tiles = ranks if far else ranks // 2
        return pl.pallas_call(
            functools.partial(mix_kernel, depth=depth, far=far, last=last),
            in_specs=[vmem] * len(operands),
            out_specs=[vmem] * (2 - last),
            out_shape=[wave_shape] * (1 - last)
            + [jax.ShapeDtypeStruct((tiles, 2, tile, cols), bf16)],
            scratch_shapes=blend_scratch,
            compiler_params=pltpu.CompilerParams(vmem_limit_bytes=16 << 20),
            cost_estimate=pl.CostEstimate(
                flops=flops // 4, bytes_accessed=1 << 20, transcendentals=0
            ),
            name="far" if far else "near",
        )(*operands)

    *near_wave, near_cross = mix(0, False, held_scalars, returned, near_slow, bracket, kept_inverse)
    *far_wave, cross = mix(
        0, True, held_scalars, returned, far_slow, bracket, kept_inverse, near_cross
    )
    crosses = [cross]
    for depth in range(1, depths):
        returned, bracket = pl.pallas_call(
            functools.partial(march_kernel, depth=depth),
            in_specs=[vmem] * 3 + [hbm] * 4,
            out_specs=[vmem] * 2,
            out_shape=[returned_shape, jax.ShapeDtypeStruct((rows, cols), jnp.int32)],
            scratch_shapes=[
                VMEM((rows, rows), bf16),
                VMEM((cols, cols), bf16),
                VMEM((rows, rows), bf16),
                dma((4,)),
                VMEM((4, rows, cols), bf16),
                VMEM((3, 4, rows, cols), bf16),
                *[VMEM(shape.shape, f32) for shape in spectrum_shapes],
            ],
            compiler_params=pltpu.CompilerParams(vmem_limit_bytes=28 << 20),
            cost_estimate=pl.CostEstimate(
                flops=3 * flops // 2, bytes_accessed=8 << 20, transcendentals=0
            ),
            name="march",
        )(
            held_scalars,
            *near_wave,
            *far_wave,
            pin(reference_index),
            pin(forward_x),
            pin(forward_y),
            pin(inverse_x),
        )
        *near_wave, near_cross = mix(
            depth, False, held_scalars, returned, near_slow, bracket, kept_inverse
        )
        *far_wave, cross = mix(
            depth, True, held_scalars, returned, far_slow, bracket, kept_inverse, near_cross
        )
        crosses.append(cross)

    offsets = jnp.arange(LAGS, dtype=jnp.int32) - LAGS // 2
    cycles = jnp.mod(frequency_bins[:, None] * offsets[None, :], period_bins).astype(f32)
    angles = cycles * (2.0 * math.pi / period_bins)
    lag_weights = jnp.stack([jnp.cos(angles), jnp.sin(angles)], axis=1).astype(bf16)

    scale = bins ** (-0.5)
    arrivals = [
        lax.all_to_all(cross, "freq", split_axis=0, concat_axis=0, tiled=True) for cross in crosses
    ]
    if tile % (2 * IMAGE_ROWS):
        summed = jnp.einsum(
            "dwcab,wcl->dabl", jnp.stack(arrivals), lag_weights, preferred_element_type=f32
        )
        return summed * scale
    height = bins * 2 * IMAGE_ROWS
    weights = pl.pallas_call(
        lag_kernel,
        in_specs=[vmem],
        out_specs=vmem,
        out_shape=jax.ShapeDtypeStruct((height, IMAGE_ROWS * LAGS), bf16),
        compiler_params=pltpu.CompilerParams(vmem_limit_bytes=16 << 20),
        name="lag",
    )(lag_weights.astype(f32))
    image = None
    for depth, arrived in enumerate(arrivals):
        aliased = image is not None
        image = pl.pallas_call(
            functools.partial(image_kernel, scale=scale, depth=depth, aliased=aliased),
            in_specs=[vmem, vmem] + [hbm] * aliased,
            out_specs=hbm,
            out_shape=jax.ShapeDtypeStruct((depths, tile, cols, LAGS), f32),
            scratch_shapes=[VMEM((tile, cols, LAGS), f32), dma((tile,))],
            input_output_aliases={2: 0} if aliased else {},
            compiler_params=pltpu.CompilerParams(vmem_limit_bytes=28 << 20),
            name="image",
        )(arrived, weights, *([image] if aliased else []))
    return image


def solution(mesh):
    placed = (
        P("grp", "freq", None, None),
        P("grp", "freq", None, None),
        P(("grp", "freq"), None, None),
        P("grp"),
        P("grp", None),
        P("grp", None, None),
        P(),
        P("grp"),
    )
    return jax.shard_map(
        functools.partial(shards, ranks=mesh.shape["freq"]),
        mesh=mesh,
        in_specs=placed,
        out_specs=P("grp", "freq", None, None),
        check_vma=False,
    )
```

time: 75.4 us -> 71.2 us (0.944)
  waiting for transfers between devices: 29 us -> 21.7 us
  starting transfers between devices: 18.1 us -> 21.1 us
    ppermute x7 -> x9, waiting for transfers between devices: 13.5 us -> 5.59 us  [swap(): return lax.ppermute(value, 'freq', [(i, i ^ bit) for i in range(ranks)])]
    ppermute x7 -> x9, starting transfers between devices: 8.99 us -> 11.7 us  [swap(): return lax.ppermute(value, 'freq', [(i, i ^ bit) for i in range(ranks)])]
    pallas_call x4 -> x7, Pallas kernels: 17.7 us -> 17.9 us  [the longest x4 6.39 us: mix(): pl.pallas_call(functools.partial(mix_kernel, depth=depth, far=far, last=l...]
  transfers between devices with their start and end apart: 9 -> 11, of which waited for: 7 -> 8; matrix products, arithmetic and copies ran while one was open for 1% -> 1% of each run, Pallas kernels for 26% -> 28%
where the time goes in v3:
time: 71.2 us; the launch traced here: 70.8 us
  Pallas kernels  26.9 us (38%)
  waiting for transfers between devices  21.7 us (30%)
  starting transfers between devices  21.1 us (30%)
  other arithmetic  0.75 us (1%)
    all_to_all x2, waiting for transfers between devices, shards(): lax.all_to_all(cross, 'freq', split_axis=0, concat_axis=0, tiled=True)  16.1 us
    ppermute x9, starting transfers between devices, swap(): return lax.ppermute(value, 'freq', [(i, i ^ bit) for i in range(ranks)])  11.7 us
    all_to_all x2, starting transfers between devices, shards(): lax.all_to_all(cross, 'freq', split_axis=0, concat_axis=0, tiled=True)  9.34 us
    pallas_call x2, Pallas kernels, shards(): pl.pallas_call(functools.partial(image_kernel, scale=scale, depth=depth,...  7.63 us
    pallas_call x4, Pallas kernels, mix(): pl.pallas_call(functools.partial(mix_kernel, depth=depth, far=far, last=l...  6.39 us
    ppermute x9, waiting for transfers between devices, swap(): return lax.ppermute(value, 'freq', [(i, i ^ bit) for i in range(ranks)])  5.59 us
    pallas_call x1, Pallas kernels, shards(): pl.pallas_call(functools.partial(march_kernel, depth=depth), in_specs=[vm...  4.93 us
    pallas_call x1, Pallas kernels, shards(): pl.pallas_call(out_kernel, in_specs=[hbm] * 6, out_specs=[vmem] * 4, out_...  3.74 us
  transfers between devices with their start and end apart: 11, of which 8 were waited for; matrix products, arithmetic and copies ran while one was open for 1% of the time, Pallas kernels for 28%

profile of v3, /device:TPU:0, one launch (start us, length us, event | category | flops | bytes accessed | tf_op | source)
XLA Modules:
  0.0 70.8 jit_solution(17692280693311795952)
XLA Ops:
  0.0 1.2 %window.1 = (bf16[4,2,64,256]{3,2,1,0:T(8,128)(2,1)S(1)}, bf16[4,2,64,256]{3,2,1,0:T(8,128)(2,1)S(1)}) custom-call(s32[2]{0:T(128)} %map_hbm.1, s32[2]{0:T(128)} %corner_hbm.1, bf16[1,768,512]{2,1,0:T(8,128)(2,1)} %slab_hbm.1), custom_call_target="tpu_custom_call" | custom-call | tf_op jit(solution)/shard_map/window/pallas_call | solution.py:536
  1.7 1.2 %collective-permute-done = bf16[4,2,64,256]{3,2,1,0:T(8,128)(2,1)S(1)} collective-permute-done((bf16[4,2,64,256]{3,2,1,0:T(8,128)(2,1)S(1)}, bf16[4,2,64,256]{3,2,1,0:T(8,128)(2,1)S(1)}, u32[]{:S(2)}, u32[]{:S(2)}) %collective-permute-start) | collective-permute-done | bytes 262176 | tf_op jit(solution)/shard_map/ppermute | solution.py:552
  3.0 3.0 %collective-permute-start.2 = (bf16[2,64,256]{2,1,0:T(8,128)(2,1)S(1)}, bf16[2,64,256]{2,1,0:T(8,128)(2,1)S(1)}, u32[]{:S(2)}, u32[]{:S(2)}) collective-permute-start(bf16[2,64,256]{2,1,0:T(8,128)(2,1)S(1)} %get-tuple-element.51), channel_id=1, source_target_pairs={{0,4},{1,5},{2,6},{3,7},{4,0},{5,1},{6,2},{7,3},{8,12},{9,13},{10,... | collective-permute-start | bytes 196616 | tf_op jit(solution)/shard_map/ppermute | solution.py:552
  6.0 1.4 %collective-permute-start.3 = (bf16[2,64,256]{2,1,0:T(8,128)(2,1)S(1)}, bf16[2,64,256]{2,1,0:T(8,128)(2,1)S(1)}, u32[]{:S(2)}, u32[]{:S(2)}) collective-permute-start(bf16[2,64,256]{2,1,0:T(8,128)(2,1)S(1)} %get-tuple-element.52), channel_id=1, source_target_pairs={{0,6},{1,7},{2,4},{3,5},{4,2},{5,3},{6,0},{7,1},{8,14},{9,15},{10,... | collective-permute-start | bytes 196616 | tf_op jit(solution)/shard_map/ppermute | solution.py:552
  7.8 3.7 %out.1 = (f32[4,512,256]{2,1,0:T(8,128)S(1)}, f32[3,512,256]{2,1,0:T(8,128)S(1)}, f32[3,512,256]{2,1,0:T(8,128)S(1)}, f32[8,256]{1,0:T(8,128)S(1)}) custom-call(s32[16]{0:T(128)} %bins_hbm, f32[2,3]{1,0:T(2,128)} %gaps_hbm.1, bf16[2,1,512,256]{3,2,1,0:T(8,128)(2,1)} %source_hbm.1, bf16[2,1,512,256]{3,2,1,0:T(8,128)(2,1)} %receiver_hbm.1, ...), custom_call_target="tpu_custom_call" | custom-call | flops 1073741824 | bytes 4194304 | tf_op jit(solution)/shard_map/out/pallas_call | solution.py:563
  12.3 2.7 %collective-permute-start.4 = (bf16[2,64,256]{2,1,0:T(8,128)(2,1)S(1)}, bf16[2,64,256]{2,1,0:T(8,128)(2,1)S(1)}, u32[]{:S(2)}, u32[]{:S(2)}) collective-permute-start(bf16[2,64,256]{2,1,0:T(8,128)(2,1)S(1)} %bitcast_add_fusion), channel_id=1, source_target_pairs={{0,8},{1,9},{2,10},{3,11},{4,12},{5,13},{6,14},{7,15},{8,0},{9,1},... | collective-permute-start | bytes 196616 | tf_op jit(solution)/shard_map/ppermute | solution.py:552
  15.1 2.9 %back.1 = (bf16[3,4,512,256]{3,2,1,0:T(8,128)(2,1)S(1)}, s32[512,256]{1,0:T(8,128)S(1)}, bf16[256,256]{1,0:T(8,128)(2,1)S(1)}) custom-call(f32[4,512,256]{2,1,0:T(8,128)S(1)} %get-tuple-element.37.spec_ref, f32[3,512,256]{2,1,0:T(8,128)S(1)} %get-tuple-element.38.cos_ref, f32[3,512,256]{2,1,0:T(8,128)S(1)} %get-tuple-element.39.sin_ref, ...), custom_call_target="tpu_custom_call" | custom-call | flops 2147483648 | bytes 4194304 | tf_op jit(solution)/shard_map/back/pallas_call | solution.py:596
  18.0 1.8 %collective-permute-start.7 = (bf16[2,64,256]{2,1,0:T(8,128)(2,1)S(1)}, bf16[2,64,256]{2,1,0:T(8,128)(2,1)S(1)}, u32[]{:S(2)}, u32[]{:S(2)}) collective-permute-start(bf16[2,64,256]{2,1,0:T(8,128)(2,1)S(1)} %add.41), channel_id=1, source_target_pairs={{0,6},{1,7},{2,4},{3,5},{4,2},{5,3},{6,0},{7,1},{8,14},{9,15},{10,... | collective-permute-start | bytes 196616 | tf_op jit(solution)/shard_map/ppermute | solution.py:552
  19.9 0.8 %collective-permute-start.6 = (bf16[2,64,256]{2,1,0:T(8,128)(2,1)S(1)}, bf16[2,64,256]{2,1,0:T(8,128)(2,1)S(1)}, u32[]{:S(2)}, u32[]{:S(2)}) collective-permute-start(bf16[2,64,256]{2,1,0:T(8,128)(2,1)S(1)} %add.41), channel_id=1, source_target_pairs={{0,4},{1,5},{2,6},{3,7},{4,0},{5,1},{6,2},{7,3},{8,12},{9,13},{10,... | collective-permute-start | bytes 196616 | tf_op jit(solution)/shard_map/ppermute | solution.py:552
  20.7 0.9 %collective-permute-start.5 = (bf16[2,64,256]{2,1,0:T(8,128)(2,1)S(1)}, bf16[2,64,256]{2,1,0:T(8,128)(2,1)S(1)}, u32[]{:S(2)}, u32[]{:S(2)}) collective-permute-start(bf16[2,64,256]{2,1,0:T(8,128)(2,1)S(1)} %add.41), channel_id=1, source_target_pairs={{0,2},{1,3},{2,0},{3,1},{4,6},{5,7},{6,4},{7,5},{8,10},{9,11},{10,... | collective-permute-start | bytes 196616 | tf_op jit(solution)/shard_map/ppermute | solution.py:552
  21.6 1.7 %collective-permute-done.7 = bf16[2,64,256]{2,1,0:T(8,128)(2,1)S(1)} collective-permute-done((bf16[2,64,256]{2,1,0:T(8,128)(2,1)S(1)}, bf16[2,64,256]{2,1,0:T(8,128)(2,1)S(1)}, u32[]{:S(2)}, u32[]{:S(2)}) %collective-permute-start.7) | collective-permute-done | bytes 65568 | tf_op jit(solution)/shard_map/ppermute | solution.py:552
  23.3 0.9 %collective-permute-done.6 = bf16[2,64,256]{2,1,0:T(8,128)(2,1)S(1)} collective-permute-done((bf16[2,64,256]{2,1,0:T(8,128)(2,1)S(1)}, bf16[2,64,256]{2,1,0:T(8,128)(2,1)S(1)}, u32[]{:S(2)}, u32[]{:S(2)}) %collective-permute-start.6) | collective-permute-done | bytes 65568 | tf_op jit(solution)/shard_map/ppermute | solution.py:552
  24.1 0.8 %collective-permute-done.5 = bf16[2,64,256]{2,1,0:T(8,128)(2,1)S(1)} collective-permute-done((bf16[2,64,256]{2,1,0:T(8,128)(2,1)S(1)}, bf16[2,64,256]{2,1,0:T(8,128)(2,1)S(1)}, u32[]{:S(2)}, u32[]{:S(2)}) %collective-permute-start.5) | collective-permute-done | bytes 65568 | tf_op jit(solution)/shard_map/ppermute | solution.py:552
  25.0 1.2 %near.2 = (bf16[4,256,256]{2,1,0:T(8,128)(2,1)S(1)}, bf16[8,2,32,256]{3,2,1,0:T(8,128)(2,1)S(1)}) custom-call(f32[8,256]{1,0:T(8,128)S(1)} %get-tuple-element.31.refs_0_.held_ref, bf16[3,4,512,256]{3,2,1,0:T(8,128)(2,1)S(1)} %get-tuple-element.41.refs_1_, bf16[4,2,64,256]{3,2,1,0:T(8,128)(2,1)S(1)} %pad_maximum_fusion.refs_2_, ...), custom_call_target="tpu_custom_call" | custom-call | flops 536870912 | bytes 1048576 | tf_op jit(solution)/shard_map/near/pallas_call | solution.py:628
  26.6 2.0 %far.2 = (bf16[4,256,256]{2,1,0:T(8,128)(2,1)S(1)}, bf16[16,2,32,256]{3,2,1,0:T(8,128)(2,1)}) custom-call(f32[8,256]{1,0:T(8,128)S(1)} %get-tuple-element.31.refs_0_.held_ref, bf16[3,4,512,256]{3,2,1,0:T(8,128)(2,1)S(1)} %get-tuple-element.41.refs_1_, bf16[4,2,64,256]{3,2,1,0:T(8,128)(2,1)S(1)} %collective-permute-done.8.refs_2_, ...), custom_call_target="tpu_custom_call" | custom-call | flops 536870912 | bytes 1048576 | tf_op jit(solution)/shard_map/far/pallas_call | solution.py:628
  28.5 5.2 %all-to-all-start.1 = ((bf16[16,2,32,256]{3,2,1,0:T(8,128)(2,1)}), bf16[16,2,32,256]{3,2,1,0:T(8,128)(2,1)S(1)}, u32[]{:S(2)}, u32[]{:S(2)}) async-start(bf16[16,2,32,256]{3,2,1,0:T(8,128)(2,1)} %get-tuple-element.50), calls=%async_computation.1 | async-start | bytes 1048576 | tf_op jit(solution)/shard_map/all_to_all | solution.py:691
  33.8 4.9 %march.1 = (bf16[3,4,512,256]{3,2,1,0:T(8,128)(2,1)S(1)}, s32[512,256]{1,0:T(8,128)S(1)}) custom-call(f32[8,256]{1,0:T(8,128)S(1)} %get-tuple-element.31.refs_0_.held_ref, bf16[4,256,256]{2,1,0:T(8,128)(2,1)S(1)} %get-tuple-element.45.near_wave, bf16[4,256,256]{2,1,0:T(8,128)(2,1)S(1)} %get-tuple-element.47.far_wave, s32[2,512,256]{2,1,0:T(8,128)} %bracket_hbm.3, ...), custom_call_target="tpu_custom_call" | custom-call | flops 3221225472 | bytes 8388608 | tf_op jit(solution)/shard_map/march/pallas_call | solution.py:648
  38.7 1.2 %near.3.refs_5_ = bf16[8,2,32,256]{3,2,1,0:T(8,128)(2,1)S(1)} custom-call(f32[8,256]{1,0:T(8,128)S(1)} %get-tuple-element.31.refs_0_.held_ref, bf16[3,4,512,256]{3,2,1,0:T(8,128)(2,1)S(1)} %get-tuple-element.48.refs_1_, bf16[4,2,64,256]{3,2,1,0:T(8,128)(2,1)S(1)} %pad_maximum_fusion.refs_2_, s32[512,256]{1,0:T(8,128)S(1)} %get-tuple-element.49.refs_3_, ...), custom_call_target="tpu_custom_call" | custom-call | flops 536870912 | bytes 1048576 | tf_op jit(solution)/shard_map/near/pallas_call | solution.py:628
  40.0 2.0 %far.3 = bf16[16,2,32,256]{3,2,1,0:T(8,128)(2,1)} custom-call(f32[8,256]{1,0:T(8,128)S(1)} %get-tuple-element.31.refs_0_.held_ref, bf16[3,4,512,256]{3,2,1,0:T(8,128)(2,1)S(1)} %get-tuple-element.48.refs_1_, bf16[4,2,64,256]{3,2,1,0:T(8,128)(2,1)S(1)} %collective-permute-done.8.refs_2_, s32[512,256]{1,0:T(8,128)S(1)} %get-tuple-element.49.refs_3_, ...), custom_call_target="tpu_custom_call" | custom-call | flops 536870912 | bytes 1048576 | tf_op jit(solution)/shard_map/far/pallas_call | solution.py:628
  42.0 6.3 %all-to-all-done.1.refs_0_ = bf16[16,2,32,256]{3,2,1,0:T(8,128)(2,1)S(1)} async-done(((bf16[16,2,32,256]{3,2,1,0:T(8,128)(2,1)}), bf16[16,2,32,256]{3,2,1,0:T(8,128)(2,1)S(1)}, u32[]{:S(2)}, u32[]{:S(2)}) %all-to-all-start.1) | async-done | bytes 524320 | tf_op jit(solution)/shard_map/all_to_all | solution.py:691
  48.3 4.1 %all-to-all-start = ((bf16[16,2,32,256]{3,2,1,0:T(8,128)(2,1)}), bf16[16,2,32,256]{3,2,1,0:T(8,128)(2,1)S(1)}, u32[]{:S(2)}, u32[]{:S(2)}) async-start(bf16[16,2,32,256]{3,2,1,0:T(8,128)(2,1)} %far.3), calls=%async_computation | async-start | bytes 1048576 | tf_op jit(solution)/shard_map/all_to_all | solution.py:691
  53.2 3.8 %image.2.refs_2_ = f32[2,32,256,256]{3,2,1,0:T(8,128)} custom-call(bf16[16,2,32,256]{3,2,1,0:T(8,128)(2,1)S(1)} %all-to-all-done.1.refs_0_, bf16[256,2048]{1,0:T(8,128)(2,1)S(1)} %lag.1.refs_1_), custom_call_target="tpu_custom_call" | custom-call | tf_op jit(solution)/shard_map/image/pallas_call | solution.py:710
  57.0 9.8 %all-to-all-done.refs_0_ = bf16[16,2,32,256]{3,2,1,0:T(8,128)(2,1)S(1)} async-done(((bf16[16,2,32,256]{3,2,1,0:T(8,128)(2,1)}), bf16[16,2,32,256]{3,2,1,0:T(8,128)(2,1)S(1)}, u32[]{:S(2)}, u32[]{:S(2)}) %all-to-all-start) | async-done | bytes 524320 | tf_op jit(solution)/shard_map/all_to_all | solution.py:691
  66.8 3.8 %image.3 = f32[2,32,256,256]{3,2,1,0:T(8,128)} custom-call(bf16[16,2,32,256]{3,2,1,0:T(8,128)(2,1)S(1)} %all-to-all-done.refs_0_, bf16[256,2048]{1,0:T(8,128)(2,1)S(1)} %lag.1.refs_1_, f32[2,32,256,256]{3,2,1,0:T(8,128)} %image.2.refs_2_), custom_call_target="tpu_custom_call", output_to_operand_aliasing={{}: (2, {})} | custom-call | tf_op jit(solution)/shard_map/image/pallas_call | solution.py:710
  (20 shorter events, 3.1 us)
Async XLA Ops:
  1.2 1.7 %collective-permute-start = (bf16[4,2,64,256]{3,2,1,0:T(8,128)(2,1)S(1)}, bf16[4,2,64,256]{3,2,1,0:T(8,128)(2,1)S(1)}, u32[]{:S(2)}, u32[]{:S(2)}) collective-permute-start(bf16[4,2,64,256]{3,2,1,0:T(8,128)(2,1)S(1)} %get-tuple-element.29), channel_id=1, source_target_pairs={{0,1},{1,0},{2,3},{3,2},{4,5},{5,4},{6,7},{7,6},{8,9},{9,8},{10,11... | collective-permute-start | bytes 786440 | tf_op jit(solution)/shard_map/ppermute | solution.py:552
  3.0 8.6 %collective-permute-start.2 = (bf16[2,64,256]{2,1,0:T(8,128)(2,1)S(1)}, bf16[2,64,256]{2,1,0:T(8,128)(2,1)S(1)}, u32[]{:S(2)}, u32[]{:S(2)}) collective-permute-start(bf16[2,64,256]{2,1,0:T(8,128)(2,1)S(1)} %get-tuple-element.51), channel_id=1, source_target_pairs={{0,4},{1,5},{2,6},{3,7},{4,0},{5,1},{6,2},{7,3},{8,12},{9,13},{10,... | collective-permute-start | bytes 196616 | tf_op jit(solution)/shard_map/ppermute | solution.py:552
  6.0 5.6 %collective-permute-start.3 = (bf16[2,64,256]{2,1,0:T(8,128)(2,1)S(1)}, bf16[2,64,256]{2,1,0:T(8,128)(2,1)S(1)}, u32[]{:S(2)}, u32[]{:S(2)}) collective-permute-start(bf16[2,64,256]{2,1,0:T(8,128)(2,1)S(1)} %get-tuple-element.52), channel_id=1, source_target_pairs={{0,6},{1,7},{2,4},{3,5},{4,2},{5,3},{6,0},{7,1},{8,14},{9,15},{10,... | collective-permute-start | bytes 196616 | tf_op jit(solution)/shard_map/ppermute | solution.py:552
  7.4 5.0 %collective-permute-start.1 = (bf16[2,64,256]{2,1,0:T(8,128)(2,1)S(1)}, bf16[2,64,256]{2,1,0:T(8,128)(2,1)S(1)}, u32[]{:S(2)}, u32[]{:S(2)}) collective-permute-start(bf16[2,64,256]{2,1,0:T(8,128)(2,1)S(1)} %get-tuple-element.53), channel_id=1, source_target_pairs={{0,2},{1,3},{2,0},{3,1},{4,6},{5,7},{6,4},{7,5},{8,10},{9,11},{10,... | collective-permute-start | bytes 196616 | tf_op jit(solution)/shard_map/ppermute | solution.py:552
  12.3 5.6 %collective-permute-start.4 = (bf16[2,64,256]{2,1,0:T(8,128)(2,1)S(1)}, bf16[2,64,256]{2,1,0:T(8,128)(2,1)S(1)}, u32[]{:S(2)}, u32[]{:S(2)}) collective-permute-start(bf16[2,64,256]{2,1,0:T(8,128)(2,1)S(1)} %bitcast_add_fusion), channel_id=1, source_target_pairs={{0,8},{1,9},{2,10},{3,11},{4,12},{5,13},{6,14},{7,15},{8,0},{9,1},... | collective-permute-start | bytes 196616 | tf_op jit(solution)/shard_map/ppermute | solution.py:552
  18.0 5.2 %collective-permute-start.7 = (bf16[2,64,256]{2,1,0:T(8,128)(2,1)S(1)}, bf16[2,64,256]{2,1,0:T(8,128)(2,1)S(1)}, u32[]{:S(2)}, u32[]{:S(2)}) collective-permute-start(bf16[2,64,256]{2,1,0:T(8,128)(2,1)S(1)} %add.41), channel_id=1, source_target_pairs={{0,6},{1,7},{2,4},{3,5},{4,2},{5,3},{6,0},{7,1},{8,14},{9,15},{10,... | collective-permute-start | bytes 196616 | tf_op jit(solution)/shard_map/ppermute | solution.py:552
  19.9 4.3 %collective-permute-start.6 = (bf16[2,64,256]{2,1,0:T(8,128)(2,1)S(1)}, bf16[2,64,256]{2,1,0:T(8,128)(2,1)S(1)}, u32[]{:S(2)}, u32[]{:S(2)}) collective-permute-start(bf16[2,64,256]{2,1,0:T(8,128)(2,1)S(1)} %add.41), channel_id=1, source_target_pairs={{0,4},{1,5},{2,6},{3,7},{4,0},{5,1},{6,2},{7,3},{8,12},{9,13},{10,... | collective-permute-start | bytes 196616 | tf_op jit(solution)/shard_map/ppermute | solution.py:552
  20.7 4.3 %collective-permute-start.5 = (bf16[2,64,256]{2,1,0:T(8,128)(2,1)S(1)}, bf16[2,64,256]{2,1,0:T(8,128)(2,1)S(1)}, u32[]{:S(2)}, u32[]{:S(2)}) collective-permute-start(bf16[2,64,256]{2,1,0:T(8,128)(2,1)S(1)} %add.41), channel_id=1, source_target_pairs={{0,2},{1,3},{2,0},{3,1},{4,6},{5,7},{6,4},{7,5},{8,10},{9,11},{10,... | collective-permute-start | bytes 196616 | tf_op jit(solution)/shard_map/ppermute | solution.py:552
  25.0 1.6 %collective-permute-start.8 = (bf16[4,2,64,256]{3,2,1,0:T(8,128)(2,1)S(1)}, bf16[4,2,64,256]{3,2,1,0:T(8,128)(2,1)S(1)}, u32[]{:S(2)}, u32[]{:S(2)}) collective-permute-start(bf16[4,2,64,256]{3,2,1,0:T(8,128)(2,1)S(1)} %pad_maximum_fusion.refs_2_), channel_id=1, source_target_pairs={{0,1},{1,0},{2,3},{3,2},{4,5},{5,4},{6,7},{7,6},{8,9},{9,8},{10,11... | collective-permute-start | bytes 786440 | tf_op jit(solution)/shard_map/ppermute | solution.py:552
  28.5 19.7 %all-to-all-start.1 = ((bf16[16,2,32,256]{3,2,1,0:T(8,128)(2,1)}), bf16[16,2,32,256]{3,2,1,0:T(8,128)(2,1)S(1)}, u32[]{:S(2)}, u32[]{:S(2)}) async-start(bf16[16,2,32,256]{3,2,1,0:T(8,128)(2,1)} %get-tuple-element.50), calls=%async_computation.1 | async-start | bytes 1048576 | tf_op jit(solution)/shard_map/all_to_all | solution.py:691
  39.9 12.4 %copy-start = (s32[16]{0:T(128)S(1)}, s32[16]{0:T(128)}, u32[]{:S(2)}) copy-start(s32[16]{0:T(128)} %bins_hbm) | copy-start | bytes 196
  48.3 18.6 %all-to-all-start = ((bf16[16,2,32,256]{3,2,1,0:T(8,128)(2,1)}), bf16[16,2,32,256]{3,2,1,0:T(8,128)(2,1)S(1)}, u32[]{:S(2)}, u32[]{:S(2)}) async-start(bf16[16,2,32,256]{3,2,1,0:T(8,128)(2,1)} %far.3), calls=%async_computation | async-start | bytes 1048576 | tf_op jit(solution)/shard_map/all_to_all | solution.py:691

commit v4 on v3

--- a/solution.py
+++ b/solution.py
@@ -211,12 +211,6 @@
         mix(here, block)
 
 
-def put_tiles(cross_ref, first, side, values):
-    tile = cross_ref.shape[2]
-    for part in range(values.shape[0] // tile):
-        cross_ref[first + part, side] = values[part * tile : (part + 1) * tile]
-
-
 PIECES = 4
 
 
@@ -377,7 +371,12 @@
         wait()
 
 
-def mix_kernel(*refs, depth, far, last):
+def place_of(rank):
+    here = lax.axis_index("freq")
+    return (rank ^ here) % 2, (rank // 2) ^ (here // 2)
+
+
+def mix_kernel(*refs, depth, far, last, paired):
     held_ref, returned_ref, slow_ref, bracket_ref, inverse_y = refs[:5]
     rest = refs[5:]
     if far:
@@ -386,19 +385,26 @@
         wave_ref, rest = rest[0], rest[1:]
     cross_ref, even, odd = rest
     piece = slow_ref.shape[2]
-    tile = cross_ref.shape[2]
+    tile = cross_ref.shape[-2]
     tiles = piece // tile
     near_starts, far_starts = piece_starts(piece)
     starts = far_starts if far else near_starts
     if far:
         for step, start in enumerate(near_starts):
+            if paired:
+                for part in range(tiles):
+                    cross_ref[place_of(start // tile + part)] = near_cross[step * tiles + part]
+                continue
             cross_ref[pl.ds(start // tile, tiles)] = near_cross[step * tiles : (step + 1) * tiles]
 
     def put_wave(block, within, plane, values):
         wave_ref[plane, block * piece + within.start : block * piece + within.stop] = values
 
     def put_cross(block, side, values):
-        put_tiles(cross_ref, starts[block] // tile if far else block * tiles, side, values)
+        for part in range(tiles):
+            rank = starts[block] // tile + part if far else block * tiles + part
+            place = place_of(rank) if far and paired else (rank,)
+            cross_ref[*place, side] = values[part * tile : (part + 1) * tile]
 
     blend(
         returned_ref,
@@ -465,28 +471,38 @@
 IMAGE_ROWS = 8
 
 
-def lag_kernel(lag_ref, weight_ref):
+def lag_kernel(lag_ref, *weight_refs):
     bins, pair, lags = lag_ref.shape
     height = bins * pair * IMAGE_ROWS
-    table = jnp.broadcast_to(
-        lag_ref[...].reshape(bins * pair, 1, lags), (bins * pair, IMAGE_ROWS, lags)
-    ).reshape(height, lags)
-    place = lax.broadcasted_iota(jnp.int32, (height, lags), 0) % IMAGE_ROWS
-    for row in range(IMAGE_ROWS):
-        weight_ref[:, row * lags : (row + 1) * lags] = jnp.where(place == row, table, 0.0).astype(
-            bf16
+    here = lax.axis_index("freq")
+    for weight_ref, mask in zip(weight_refs, (0, here)):
+        table = jnp.concatenate(
+            [
+                jnp.broadcast_to(lag_ref[spot ^ mask][:, None], (pair, IMAGE_ROWS, lags)).reshape(
+                    pair * IMAGE_ROWS, lags
+                )
+                for spot in range(bins)
+            ],
+            axis=0,
         )
-
-
-def image_kernel(*refs, scale, depth, aliased):
-    cross_ref, weight_ref = refs[:2]
-    out_hbm, made_ref, sems = refs[2 + aliased :]
-    bins, pair, tile, cols = cross_ref.shape
-    lags = made_ref.shape[2]
+        place = lax.broadcasted_iota(jnp.int32, (height, lags), 0) % IMAGE_ROWS
+        for row in range(IMAGE_ROWS):
+            weight_ref[:, row * lags : (row + 1) * lags] = jnp.where(
+                place == row, table, 0.0
+            ).astype(bf16)
+
+
+def image_kernel(*refs, scale, depth, aliased, count):
+    cross_refs, weight_ref = refs[:count], refs[count]
+    out_hbm, made_ref, sems = refs[count + 1 + aliased :]
+    tile, cols, lags = made_ref.shape
     copies = []
     for group in range(tile // IMAGE_ROWS):
-        rows = cross_ref[:, :, group * IMAGE_ROWS : (group + 1) * IMAGE_ROWS, :].astype(f32)
-        left = rows.reshape(bins * pair * IMAGE_ROWS, cols).T.astype(bf16)
+        rows = slice(group * IMAGE_ROWS, (group + 1) * IMAGE_ROWS)
+        left = jnp.concatenate(
+            [ref[..., rows, :].astype(f32).reshape(-1, cols) for ref in cross_refs], axis=0
+        )
+        left = left.T.astype(bf16)
         for row in range(IMAGE_ROWS):
             place = group * IMAGE_ROWS + row
             made_ref[place] = dot(left, weight_ref[:, row * lags : (row + 1) * lags]) * scale
@@ -620,17 +636,20 @@
     far_slow = swap(near_slow, 1)
 
     blend_scratch = [VMEM((12, piece, cols), f32)] * 2
+    paired = ranks <= 16 and depths > 1 and tile % (2 * IMAGE_ROWS) == 0
     wave_shape = jax.ShapeDtypeStruct((4, half, cols), bf16)
 
     def mix(depth, far, *operands):
         last = depth == depths - 1
-        tiles = ranks if far else ranks // 2
+        tiles = (ranks // 2,) if not far else (2, ranks // 2) if paired and last else (ranks,)
         return pl.pallas_call(
-            functools.partial(mix_kernel, depth=depth, far=far, last=last),
+            functools.partial(
+                mix_kernel, depth=depth, far=far, last=last, paired=paired and last
+            ),
             in_specs=[vmem] * len(operands),
             out_specs=[vmem] * (2 - last),
             out_shape=[wave_shape] * (1 - last)
-            + [jax.ShapeDtypeStruct((tiles, 2, tile, cols), bf16)],
+            + [jax.ShapeDtypeStruct(tiles + (2, tile, cols), bf16)],
             scratch_shapes=blend_scratch,
             compiler_params=pltpu.CompilerParams(vmem_limit_bytes=16 << 20),
             cost_estimate=pl.CostEstimate(
@@ -687,36 +706,51 @@
     lag_weights = jnp.stack([jnp.cos(angles), jnp.sin(angles)], axis=1).astype(bf16)
 
     scale = bins ** (-0.5)
-    arrivals = [
-        lax.all_to_all(cross, "freq", split_axis=0, concat_axis=0, tiled=True) for cross in crosses
-    ]
+    def exchange(value):
+        return lax.all_to_all(value, "freq", split_axis=0, concat_axis=0, tiled=True)
+
+    if not paired:
+        arrivals = [[exchange(cross)] for cross in crosses]
+    else:
+        arrivals = [[exchange(cross)] for cross in crosses[:-1]]
+        by_core = crosses[-1]
+        by_chip = jnp.stack([by_core[0], swap(by_core[1], 1)], axis=1)
+        chips = ranks // 2
+        got = {step: swap(by_chip[step], 2 * step) for step in range(chips - 1, 0, -1)}
+        arrivals.append([by_chip[0]] + [got[step] for step in range(1, chips)])
     if tile % (2 * IMAGE_ROWS):
         summed = jnp.einsum(
-            "dwcab,wcl->dabl", jnp.stack(arrivals), lag_weights, preferred_element_type=f32
+            "dwcab,wcl->dabl",
+            jnp.stack([arrived for (arrived,) in arrivals]),
+            lag_weights,
+            preferred_element_type=f32,
         )
         return summed * scale
     height = bins * 2 * IMAGE_ROWS
     weights = pl.pallas_call(
         lag_kernel,
         in_specs=[vmem],
-        out_specs=vmem,
-        out_shape=jax.ShapeDtypeStruct((height, IMAGE_ROWS * LAGS), bf16),
+        out_specs=[vmem] * (1 + paired),
+        out_shape=[jax.ShapeDtypeStruct((height, IMAGE_ROWS * LAGS), bf16)] * (1 + paired),
         compiler_params=pltpu.CompilerParams(vmem_limit_bytes=16 << 20),
         name="lag",
     )(lag_weights.astype(f32))
     image = None
     for depth, arrived in enumerate(arrivals):
         aliased = image is not None
+        count = len(arrived)
         image = pl.pallas_call(
-            functools.partial(image_kernel, scale=scale, depth=depth, aliased=aliased),
-            in_specs=[vmem, vmem] + [hbm] * aliased,
+            functools.partial(
+                image_kernel, scale=scale, depth=depth, aliased=aliased, count=count
+            ),
+            in_specs=[vmem] * (count + 1) + [hbm] * aliased,
             out_specs=hbm,
             out_shape=jax.ShapeDtypeStruct((depths, tile, cols, LAGS), f32),
             scratch_shapes=[VMEM((tile, cols, LAGS), f32), dma((tile,))],
-            input_output_aliases={2: 0} if aliased else {},
+            input_output_aliases={count + 1: 0} if aliased else {},
             compiler_params=pltpu.CompilerParams(vmem_limit_bytes=28 << 20),
             name="image",
-        )(arrived, weights, *([image] if aliased else []))
+        )(*arrived, weights[count > 1], *([image] if aliased else []))
     return image
 
 

time: 71.2 us -> 66 us (0.927)
  waiting for transfers between devices: 21.7 us -> 8.34 us
  starting transfers between devices: 21.1 us -> 29.8 us
    all_to_all x2 -> x1, waiting for transfers between devices: 16.1 us -> 0.01 us  [exchange(): lax.all_to_all(value, 'freq', split_axis=0, concat_axis=0, tiled=True)]
    ppermute x9 -> x17, starting transfers between devices: 11.7 us -> 24.3 us  [swap(): return lax.ppermute(value, 'freq', [(i, i ^ bit) for i in range(ranks)])]
    all_to_all x2 -> x1, starting transfers between devices: 9.34 us -> 5.54 us  [exchange(): lax.all_to_all(value, 'freq', split_axis=0, concat_axis=0, tiled=True)]
    ppermute x9 -> x17, waiting for transfers between devices: 5.59 us -> 8.34 us  [swap(): return lax.ppermute(value, 'freq', [(i, i ^ bit) for i in range(ranks)])]
    pallas_call x4, Pallas kernels: 6.39 us -> 5.6 us  [mix(): pl.pallas_call(functools.partial(mix_kernel, depth=depth, far=far, last=l...]
  transfers between devices with their start and end apart: 11 -> 18, of which waited for: 8 -> 9; matrix products, arithmetic and copies ran while one was open for 1% -> 1% of each run, Pallas kernels for 28% -> 29%
where the time goes in v4:
time: 66 us; the launch traced here: 65.7 us
  starting transfers between devices  29.8 us (45%)
  Pallas kernels  26.3 us (40%)
  waiting for transfers between devices  8.34 us (13%)
  other arithmetic  0.79 us (1%)
    ppermute x17, starting transfers between devices, swap(): return lax.ppermute(value, 'freq', [(i, i ^ bit) for i in range(ranks)])  24.3 us
    ppermute x17, waiting for transfers between devices, swap(): return lax.ppermute(value, 'freq', [(i, i ^ bit) for i in range(ranks)])  8.34 us
    pallas_call x2, Pallas kernels, shards(): pl.pallas_call(functools.partial(image_kernel, scale=scale, depth=depth,...  7.63 us
    pallas_call x4, Pallas kernels, mix(): pl.pallas_call(functools.partial(mix_kernel, depth=depth, far=far, last=l...  5.6 us
    all_to_all x1, starting transfers between devices, exchange(): lax.all_to_all(value, 'freq', split_axis=0, concat_axis=0, tiled=True)  5.54 us
    pallas_call x1, Pallas kernels, shards(): pl.pallas_call(functools.partial(march_kernel, depth=depth), in_specs=[vm...  4.92 us
    pallas_call x1, Pallas kernels, shards(): pl.pallas_call(out_kernel, in_specs=[hbm] * 6, out_specs=[vmem] * 4, out_...  3.74 us
    pallas_call x1, Pallas kernels, shards(): pl.pallas_call(back_kernel, in_specs=[vmem] * 3 + [hbm] * 3, out_specs=[v...  2.88 us
  transfers between devices with their start and end apart: 18, of which 9 were waited for; matrix products, arithmetic and copies ran while one was open for 1% of the time, Pallas kernels for 29%

profile of v4, /device:TPU:0, one launch (start us, length us, event | category | flops | bytes accessed | tf_op | source)
XLA Modules:
  0.0 65.7 jit_solution(12576652467814701179)
XLA Ops:
  0.0 1.2 %window.1 = (bf16[4,2,64,256]{3,2,1,0:T(8,128)(2,1)S(1)}, bf16[4,2,64,256]{3,2,1,0:T(8,128)(2,1)S(1)}) custom-call(s32[2]{0:T(128)} %map_hbm.1, s32[2]{0:T(128)} %corner_hbm.1, bf16[1,768,512]{2,1,0:T(8,128)(2,1)} %slab_hbm.1), custom_call_target="tpu_custom_call" | custom-call | tf_op jit(solution)/shard_map/window/pallas_call | solution.py:552
  1.7 1.2 %collective-permute-done = bf16[4,2,64,256]{3,2,1,0:T(8,128)(2,1)S(1)} collective-permute-done((bf16[4,2,64,256]{3,2,1,0:T(8,128)(2,1)S(1)}, bf16[4,2,64,256]{3,2,1,0:T(8,128)(2,1)S(1)}, u32[]{:S(2)}, u32[]{:S(2)}) %collective-permute-start) | collective-permute-done | bytes 262176 | tf_op jit(solution)/shard_map/ppermute | solution.py:568
  3.0 3.0 %collective-permute-start.2 = (bf16[2,64,256]{2,1,0:T(8,128)(2,1)S(1)}, bf16[2,64,256]{2,1,0:T(8,128)(2,1)S(1)}, u32[]{:S(2)}, u32[]{:S(2)}) collective-permute-start(bf16[2,64,256]{2,1,0:T(8,128)(2,1)S(1)} %get-tuple-element.65), channel_id=1, source_target_pairs={{0,4},{1,5},{2,6},{3,7},{4,0},{5,1},{6,2},{7,3},{8,12},{9,13},{10,... | collective-permute-start | bytes 196616 | tf_op jit(solution)/shard_map/ppermute | solution.py:568
  6.0 1.4 %collective-permute-start.3 = (bf16[2,64,256]{2,1,0:T(8,128)(2,1)S(1)}, bf16[2,64,256]{2,1,0:T(8,128)(2,1)S(1)}, u32[]{:S(2)}, u32[]{:S(2)}) collective-permute-start(bf16[2,64,256]{2,1,0:T(8,128)(2,1)S(1)} %get-tuple-element.66), channel_id=1, source_target_pairs={{0,6},{1,7},{2,4},{3,5},{4,2},{5,3},{6,0},{7,1},{8,14},{9,15},{10,... | collective-permute-start | bytes 196616 | tf_op jit(solution)/shard_map/ppermute | solution.py:568
  7.8 3.7 %out.1 = (f32[4,512,256]{2,1,0:T(8,128)S(1)}, f32[3,512,256]{2,1,0:T(8,128)S(1)}, f32[3,512,256]{2,1,0:T(8,128)S(1)}, f32[8,256]{1,0:T(8,128)S(1)}) custom-call(s32[16]{0:T(128)} %bins_hbm, f32[2,3]{1,0:T(2,128)} %gaps_hbm.1, bf16[2,1,512,256]{3,2,1,0:T(8,128)(2,1)} %source_hbm.1, bf16[2,1,512,256]{3,2,1,0:T(8,128)(2,1)} %receiver_hbm.1, ...), custom_call_target="tpu_custom_call" | custom-call | flops 1073741824 | bytes 4194304 | tf_op jit(solution)/shard_map/out/pallas_call | solution.py:579
  12.3 2.5 %collective-permute-start.4 = (bf16[2,64,256]{2,1,0:T(8,128)(2,1)S(1)}, bf16[2,64,256]{2,1,0:T(8,128)(2,1)S(1)}, u32[]{:S(2)}, u32[]{:S(2)}) collective-permute-start(bf16[2,64,256]{2,1,0:T(8,128)(2,1)S(1)} %bitcast_add_fusion), channel_id=1, source_target_pairs={{0,8},{1,9},{2,10},{3,11},{4,12},{5,13},{6,14},{7,15},{8,0},{9,1},... | collective-permute-start | bytes 196616 | tf_op jit(solution)/shard_map/ppermute | solution.py:568
  14.9 2.9 %back.1 = (bf16[3,4,512,256]{3,2,1,0:T(8,128)(2,1)S(1)}, s32[512,256]{1,0:T(8,128)S(1)}, bf16[256,256]{1,0:T(8,128)(2,1)S(1)}) custom-call(f32[4,512,256]{2,1,0:T(8,128)S(1)} %get-tuple-element.39.spec_ref, f32[3,512,256]{2,1,0:T(8,128)S(1)} %get-tuple-element.40.cos_ref, f32[3,512,256]{2,1,0:T(8,128)S(1)} %get-tuple-element.41.sin_ref, ...), custom_call_target="tpu_custom_call" | custom-call | flops 2147483648 | bytes 4194304 | tf_op jit(solution)/shard_map/back/pallas_call | solution.py:612
  17.9 2.0 %collective-permute-start.7 = (bf16[2,64,256]{2,1,0:T(8,128)(2,1)S(1)}, bf16[2,64,256]{2,1,0:T(8,128)(2,1)S(1)}, u32[]{:S(2)}, u32[]{:S(2)}) collective-permute-start(bf16[2,64,256]{2,1,0:T(8,128)(2,1)S(1)} %add.41), channel_id=1, source_target_pairs={{0,6},{1,7},{2,4},{3,5},{4,2},{5,3},{6,0},{7,1},{8,14},{9,15},{10,... | collective-permute-start | bytes 196616 | tf_op jit(solution)/shard_map/ppermute | solution.py:568
  20.4 1.1 %collective-permute-start.5 = (bf16[2,64,256]{2,1,0:T(8,128)(2,1)S(1)}, bf16[2,64,256]{2,1,0:T(8,128)(2,1)S(1)}, u32[]{:S(2)}, u32[]{:S(2)}) collective-permute-start(bf16[2,64,256]{2,1,0:T(8,128)(2,1)S(1)} %add.41), channel_id=1, source_target_pairs={{0,2},{1,3},{2,0},{3,1},{4,6},{5,7},{6,4},{7,5},{8,10},{9,11},{10,... | collective-permute-start | bytes 196616 | tf_op jit(solution)/shard_map/ppermute | solution.py:568
  21.4 1.7 %collective-permute-done.7 = bf16[2,64,256]{2,1,0:T(8,128)(2,1)S(1)} collective-permute-done((bf16[2,64,256]{2,1,0:T(8,128)(2,1)S(1)}, bf16[2,64,256]{2,1,0:T(8,128)(2,1)S(1)}, u32[]{:S(2)}, u32[]{:S(2)}) %collective-permute-start.7) | collective-permute-done | bytes 65568 | tf_op jit(solution)/shard_map/ppermute | solution.py:568
  24.7 1.2 %near.2 = (bf16[4,256,256]{2,1,0:T(8,128)(2,1)S(1)}, bf16[8,2,32,256]{3,2,1,0:T(8,128)(2,1)S(1)}) custom-call(f32[8,256]{1,0:T(8,128)S(1)} %get-tuple-element.33.refs_0_.held_ref, bf16[3,4,512,256]{3,2,1,0:T(8,128)(2,1)S(1)} %get-tuple-element.43.refs_1_, bf16[4,2,64,256]{3,2,1,0:T(8,128)(2,1)S(1)} %pad_maximum_fusion.refs_2_, ...), custom_call_target="tpu_custom_call" | custom-call | flops 536870912 | bytes 1048576 | tf_op jit(solution)/shard_map/near/pallas_call | solution.py:645
  26.3 2.0 %far.2 = (bf16[4,256,256]{2,1,0:T(8,128)(2,1)S(1)}, bf16[16,2,32,256]{3,2,1,0:T(8,128)(2,1)}) custom-call(f32[8,256]{1,0:T(8,128)S(1)} %get-tuple-element.33.refs_0_.held_ref, bf16[3,4,512,256]{3,2,1,0:T(8,128)(2,1)S(1)} %get-tuple-element.43.refs_1_, bf16[4,2,64,256]{3,2,1,0:T(8,128)(2,1)S(1)} %collective-permute-done.8.refs_2_, ...), custom_call_target="tpu_custom_call" | custom-call | flops 536870912 | bytes 1048576 | tf_op jit(solution)/shard_map/far/pallas_call | solution.py:645
  28.3 5.5 %all-to-all-start = ((bf16[16,2,32,256]{3,2,1,0:T(8,128)(2,1)}), bf16[16,2,32,256]{3,2,1,0:T(8,128)(2,1)S(1)}, u32[]{:S(2)}, u32[]{:S(2)}) async-start(bf16[16,2,32,256]{3,2,1,0:T(8,128)(2,1)} %get-tuple-element.53), calls=%async_computation | async-start | bytes 1048576 | tf_op jit(solution)/shard_map/all_to_all | solution.py:710
  33.8 4.9 %march.1 = (bf16[3,4,512,256]{3,2,1,0:T(8,128)(2,1)S(1)}, s32[512,256]{1,0:T(8,128)S(1)}) custom-call(f32[8,256]{1,0:T(8,128)S(1)} %get-tuple-element.33.refs_0_.held_ref, bf16[4,256,256]{2,1,0:T(8,128)(2,1)S(1)} %get-tuple-element.47.near_wave, bf16[4,256,256]{2,1,0:T(8,128)(2,1)S(1)} %get-tuple-element.49.far_wave, s32[2,512,256]{2,1,0:T(8,128)} %bracket_hbm.3, ...), custom_call_target="tpu_custom_call" | custom-call | flops 3221225472 | bytes 8388608 | tf_op jit(solution)/shard_map/march/pallas_call | solution.py:667
  38.7 1.2 %near.3.refs_5_ = bf16[8,2,32,256]{3,2,1,0:T(8,128)(2,1)S(1)} custom-call(f32[8,256]{1,0:T(8,128)S(1)} %get-tuple-element.33.refs_0_.held_ref, bf16[3,4,512,256]{3,2,1,0:T(8,128)(2,1)S(1)} %get-tuple-element.50.refs_1_, bf16[4,2,64,256]{3,2,1,0:T(8,128)(2,1)S(1)} %pad_maximum_fusion.refs_2_, s32[512,256]{1,0:T(8,128)S(1)} %get-tuple-element.51.refs_3_, ...), custom_call_target="tpu_custom_call" | custom-call | flops 536870912 | bytes 1048576 | tf_op jit(solution)/shard_map/near/pallas_call | solution.py:645
  39.9 1.2 %far.3 = bf16[2,8,2,32,256]{4,3,2,1,0:T(8,128)(2,1)S(1)} custom-call(f32[8,256]{1,0:T(8,128)S(1)} %get-tuple-element.33.refs_0_.held_ref, bf16[3,4,512,256]{3,2,1,0:T(8,128)(2,1)S(1)} %get-tuple-element.50.refs_1_, bf16[4,2,64,256]{3,2,1,0:T(8,128)(2,1)S(1)} %collective-permute-done.8.refs_2_, s32[512,256]{1,0:T(8,128)S(1)} %get-tuple-element.51.refs_3_, ...), custom_call_target="tpu_custom_call" | custom-call | flops 536870912 | bytes 1048576 | tf_op jit(solution)/shard_map/far/pallas_call | solution.py:645
  41.8 1.1 %collective-permute-done.9 = bf16[8,2,32,256]{3,2,1,0:T(8,128)(2,1)S(1)} collective-permute-done((bf16[8,2,32,256]{3,2,1,0:T(8,128)(2,1)S(1)}, bf16[8,2,32,256]{3,2,1,0:T(8,128)(2,1)S(1)}, u32[]{:S(2)}, u32[]{:S(2)}) %collective-permute-start.9) | collective-permute-done | bytes 262176 | tf_op jit(solution)/shard_map/ppermute | solution.py:568
  42.9 4.7 %collective-permute-start.16 = (bf16[2,2,32,256]{3,2,1,0:T(8,128)(2,1)S(1)}, bf16[2,2,32,256]{3,2,1,0:T(8,128)(2,1)S(1)}, u32[]{:S(2)}, u32[]{:S(2)}) collective-permute-start(bf16[2,2,32,256]{3,2,1,0:T(8,128)(2,1)S(1)} %get-tuple-element.55), channel_id=1, source_target_pairs={{0,14},{1,15},{2,12},{3,13},{4,10},{5,11},{6,8},{7,9},{8,6},{9,7},... | collective-permute-start | bytes 196616 | tf_op jit(solution)/shard_map/ppermute | solution.py:568
  48.7 2.9 %collective-permute-start.12 = (bf16[2,2,32,256]{3,2,1,0:T(8,128)(2,1)S(1)}, bf16[2,2,32,256]{3,2,1,0:T(8,128)(2,1)S(1)}, u32[]{:S(2)}, u32[]{:S(2)}) collective-permute-start(bf16[2,2,32,256]{3,2,1,0:T(8,128)(2,1)S(1)} %get-tuple-element.59), channel_id=1, source_target_pairs={{0,6},{1,7},{2,4},{3,5},{4,2},{5,3},{6,0},{7,1},{8,14},{9,15},{10,... | collective-permute-start | bytes 196616 | tf_op jit(solution)/shard_map/ppermute | solution.py:568
  51.6 2.9 %collective-permute-start.14 = (bf16[2,2,32,256]{3,2,1,0:T(8,128)(2,1)S(1)}, bf16[2,2,32,256]{3,2,1,0:T(8,128)(2,1)S(1)}, u32[]{:S(2)}, u32[]{:S(2)}) collective-permute-start(bf16[2,2,32,256]{3,2,1,0:T(8,128)(2,1)S(1)} %get-tuple-element.61), channel_id=1, source_target_pairs={{0,10},{1,11},{2,8},{3,9},{4,14},{5,15},{6,12},{7,13},{8,2},{9,3},... | collective-permute-start | bytes 196616 | tf_op jit(solution)/shard_map/ppermute | solution.py:568
  54.5 1.2 %collective-permute-start.15 = (bf16[2,2,32,256]{3,2,1,0:T(8,128)(2,1)S(1)}, bf16[2,2,32,256]{3,2,1,0:T(8,128)(2,1)S(1)}, u32[]{:S(2)}, u32[]{:S(2)}) collective-permute-start(bf16[2,2,32,256]{3,2,1,0:T(8,128)(2,1)S(1)} %get-tuple-element.62), channel_id=1, source_target_pairs={{0,12},{1,13},{2,14},{3,15},{4,8},{5,9},{6,10},{7,11},{8,4},{9,5},... | collective-permute-start | bytes 196616 | tf_op jit(solution)/shard_map/ppermute | solution.py:568
  56.1 3.8 %image.2.refs_9_ = f32[2,32,256,256]{3,2,1,0:T(8,128)} custom-call(bf16[16,2,32,256]{3,2,1,0:T(8,128)(2,1)S(1)} %all-to-all-done.refs_0_, bf16[256,2048]{1,0:T(8,128)(2,1)S(1)} %get-tuple-element.54.refs_1_), custom_call_target="tpu_custom_call" | custom-call | tf_op jit(solution)/shard_map/image/pallas_call | solution.py:742
  60.0 1.7 %collective-permute-done.14.refs_5_ = bf16[2,2,32,256]{3,2,1,0:T(8,128)(2,1)S(1)} collective-permute-done((bf16[2,2,32,256]{3,2,1,0:T(8,128)(2,1)S(1)}, bf16[2,2,32,256]{3,2,1,0:T(8,128)(2,1)S(1)}, u32[]{:S(2)}, u32[]{:S(2)}) %collective-permute-start.14) | collective-permute-done | bytes 65568 | tf_op jit(solution)/shard_map/ppermute | solution.py:568
  61.7 3.8 %image.3 = f32[2,32,256,256]{3,2,1,0:T(8,128)} custom-call(bf16[2,2,32,256]{3,2,1,0:T(8,128)(2,1)S(1)} %get-tuple-element.56.refs_0_, bf16[2,2,32,256]{3,2,1,0:T(8,128)(2,1)S(1)} %collective-permute-done.10.refs_1_, bf16[2,2,32,256]{3,2,1,0:T(8,128)(2,1)S(1)} %collective-permute-done.11.refs_2_, ...), custom_call_target="tpu_custom_call", output_to_operand_aliasing={{}: (9, {})} | custom-call | tf_op jit(solution)/shard_map/image/pallas_call | solution.py:742
  (36 shorter events, 6.5 us)
Async XLA Ops:
  1.2 1.7 %collective-permute-start = (bf16[4,2,64,256]{3,2,1,0:T(8,128)(2,1)S(1)}, bf16[4,2,64,256]{3,2,1,0:T(8,128)(2,1)S(1)}, u32[]{:S(2)}, u32[]{:S(2)}) collective-permute-start(bf16[4,2,64,256]{3,2,1,0:T(8,128)(2,1)S(1)} %get-tuple-element.31), channel_id=1, source_target_pairs={{0,1},{1,0},{2,3},{3,2},{4,5},{5,4},{6,7},{7,6},{8,9},{9,8},{10,11... | collective-permute-start | bytes 786440 | tf_op jit(solution)/shard_map/ppermute | solution.py:568
  3.0 8.6 %collective-permute-start.2 = (bf16[2,64,256]{2,1,0:T(8,128)(2,1)S(1)}, bf16[2,64,256]{2,1,0:T(8,128)(2,1)S(1)}, u32[]{:S(2)}, u32[]{:S(2)}) collective-permute-start(bf16[2,64,256]{2,1,0:T(8,128)(2,1)S(1)} %get-tuple-element.65), channel_id=1, source_target_pairs={{0,4},{1,5},{2,6},{3,7},{4,0},{5,1},{6,2},{7,3},{8,12},{9,13},{10,... | collective-permute-start | bytes 196616 | tf_op jit(solution)/shard_map/ppermute | solution.py:568
  6.0 5.6 %collective-permute-start.3 = (bf16[2,64,256]{2,1,0:T(8,128)(2,1)S(1)}, bf16[2,64,256]{2,1,0:T(8,128)(2,1)S(1)}, u32[]{:S(2)}, u32[]{:S(2)}) collective-permute-start(bf16[2,64,256]{2,1,0:T(8,128)(2,1)S(1)} %get-tuple-element.66), channel_id=1, source_target_pairs={{0,6},{1,7},{2,4},{3,5},{4,2},{5,3},{6,0},{7,1},{8,14},{9,15},{10,... | collective-permute-start | bytes 196616 | tf_op jit(solution)/shard_map/ppermute | solution.py:568
  7.4 5.0 %collective-permute-start.1 = (bf16[2,64,256]{2,1,0:T(8,128)(2,1)S(1)}, bf16[2,64,256]{2,1,0:T(8,128)(2,1)S(1)}, u32[]{:S(2)}, u32[]{:S(2)}) collective-permute-start(bf16[2,64,256]{2,1,0:T(8,128)(2,1)S(1)} %get-tuple-element.67), channel_id=1, source_target_pairs={{0,2},{1,3},{2,0},{3,1},{4,6},{5,7},{6,4},{7,5},{8,10},{9,11},{10,... | collective-permute-start | bytes 196616 | tf_op jit(solution)/shard_map/ppermute | solution.py:568
  12.3 5.5 %collective-permute-start.4 = (bf16[2,64,256]{2,1,0:T(8,128)(2,1)S(1)}, bf16[2,64,256]{2,1,0:T(8,128)(2,1)S(1)}, u32[]{:S(2)}, u32[]{:S(2)}) collective-permute-start(bf16[2,64,256]{2,1,0:T(8,128)(2,1)S(1)} %bitcast_add_fusion), channel_id=1, source_target_pairs={{0,8},{1,9},{2,10},{3,11},{4,12},{5,13},{6,14},{7,15},{8,0},{9,1},... | collective-permute-start | bytes 196616 | tf_op jit(solution)/shard_map/ppermute | solution.py:568
  17.9 5.2 %collective-permute-start.7 = (bf16[2,64,256]{2,1,0:T(8,128)(2,1)S(1)}, bf16[2,64,256]{2,1,0:T(8,128)(2,1)S(1)}, u32[]{:S(2)}, u32[]{:S(2)}) collective-permute-start(bf16[2,64,256]{2,1,0:T(8,128)(2,1)S(1)} %add.41), channel_id=1, source_target_pairs={{0,6},{1,7},{2,4},{3,5},{4,2},{5,3},{6,0},{7,1},{8,14},{9,15},{10,... | collective-permute-start | bytes 196616 | tf_op jit(solution)/shard_map/ppermute | solution.py:568
  19.9 4.3 %collective-permute-start.6 = (bf16[2,64,256]{2,1,0:T(8,128)(2,1)S(1)}, bf16[2,64,256]{2,1,0:T(8,128)(2,1)S(1)}, u32[]{:S(2)}, u32[]{:S(2)}) collective-permute-start(bf16[2,64,256]{2,1,0:T(8,128)(2,1)S(1)} %add.41), channel_id=1, source_target_pairs={{0,4},{1,5},{2,6},{3,7},{4,0},{5,1},{6,2},{7,3},{8,12},{9,13},{10,... | collective-permute-start | bytes 196616 | tf_op jit(solution)/shard_map/ppermute | solution.py:568
  20.4 4.3 %collective-permute-start.5 = (bf16[2,64,256]{2,1,0:T(8,128)(2,1)S(1)}, bf16[2,64,256]{2,1,0:T(8,128)(2,1)S(1)}, u32[]{:S(2)}, u32[]{:S(2)}) collective-permute-start(bf16[2,64,256]{2,1,0:T(8,128)(2,1)S(1)} %add.41), channel_id=1, source_target_pairs={{0,2},{1,3},{2,0},{3,1},{4,6},{5,7},{6,4},{7,5},{8,10},{9,11},{10,... | collective-permute-start | bytes 196616 | tf_op jit(solution)/shard_map/ppermute | solution.py:568
  24.7 1.6 %collective-permute-start.8 = (bf16[4,2,64,256]{3,2,1,0:T(8,128)(2,1)S(1)}, bf16[4,2,64,256]{3,2,1,0:T(8,128)(2,1)S(1)}, u32[]{:S(2)}, u32[]{:S(2)}) collective-permute-start(bf16[4,2,64,256]{3,2,1,0:T(8,128)(2,1)S(1)} %pad_maximum_fusion.refs_2_), channel_id=1, source_target_pairs={{0,1},{1,0},{2,3},{3,2},{4,5},{5,4},{6,7},{7,6},{8,9},{9,8},{10,11... | collective-permute-start | bytes 786440 | tf_op jit(solution)/shard_map/ppermute | solution.py:568
  28.3 27.9 %all-to-all-start = ((bf16[16,2,32,256]{3,2,1,0:T(8,128)(2,1)}), bf16[16,2,32,256]{3,2,1,0:T(8,128)(2,1)S(1)}, u32[]{:S(2)}, u32[]{:S(2)}) async-start(bf16[16,2,32,256]{3,2,1,0:T(8,128)(2,1)} %get-tuple-element.53), calls=%async_computation | async-start | bytes 1048576 | tf_op jit(solution)/shard_map/all_to_all | solution.py:710
  39.9 1.8 %copy-start = (s32[16]{0:T(128)S(1)}, s32[16]{0:T(128)}, u32[]{:S(2)}) copy-start(s32[16]{0:T(128)} %bins_hbm) | copy-start | bytes 196
  41.2 1.6 %collective-permute-start.9 = (bf16[8,2,32,256]{3,2,1,0:T(8,128)(2,1)S(1)}, bf16[8,2,32,256]{3,2,1,0:T(8,128)(2,1)S(1)}, u32[]{:S(2)}, u32[]{:S(2)}) collective-permute-start(bf16[8,2,32,256]{3,2,1,0:T(8,128)(2,1)S(1)} %get-tuple-element.64), channel_id=1, source_target_pairs={{0,1},{1,0},{2,3},{3,2},{4,5},{5,4},{6,7},{7,6},{8,9},{9,8},{10,11... | collective-permute-start | bytes 786440 | tf_op jit(solution)/shard_map/ppermute | solution.py:568
  42.9 8.7 %collective-permute-start.16 = (bf16[2,2,32,256]{3,2,1,0:T(8,128)(2,1)S(1)}, bf16[2,2,32,256]{3,2,1,0:T(8,128)(2,1)S(1)}, u32[]{:S(2)}, u32[]{:S(2)}) collective-permute-start(bf16[2,2,32,256]{3,2,1,0:T(8,128)(2,1)S(1)} %get-tuple-element.55), channel_id=1, source_target_pairs={{0,14},{1,15},{2,12},{3,13},{4,10},{5,11},{6,8},{7,9},{8,6},{9,7},... | collective-permute-start | bytes 196616 | tf_op jit(solution)/shard_map/ppermute | solution.py:568
  47.6 7.0 %collective-permute-start.10 = (bf16[2,2,32,256]{3,2,1,0:T(8,128)(2,1)S(1)}, bf16[2,2,32,256]{3,2,1,0:T(8,128)(2,1)S(1)}, u32[]{:S(2)}, u32[]{:S(2)}) collective-permute-start(bf16[2,2,32,256]{3,2,1,0:T(8,128)(2,1)S(1)} %get-tuple-element.57), channel_id=1, source_target_pairs={{0,2},{1,3},{2,0},{3,1},{4,6},{5,7},{6,4},{7,5},{8,10},{9,11},{10,... | collective-permute-start | bytes 196616 | tf_op jit(solution)/shard_map/ppermute | solution.py:568
  48.6 11.3 %collective-permute-start.11 = (bf16[2,2,32,256]{3,2,1,0:T(8,128)(2,1)S(1)}, bf16[2,2,32,256]{3,2,1,0:T(8,128)(2,1)S(1)}, u32[]{:S(2)}, u32[]{:S(2)}) collective-permute-start(bf16[2,2,32,256]{3,2,1,0:T(8,128)(2,1)S(1)} %get-tuple-element.58), channel_id=1, source_target_pairs={{0,4},{1,5},{2,6},{3,7},{4,0},{5,1},{6,2},{7,3},{8,12},{9,13},{10,... | collective-permute-start | bytes 196616 | tf_op jit(solution)/shard_map/ppermute | solution.py:568
  48.7 11.3 %collective-permute-start.12 = (bf16[2,2,32,256]{3,2,1,0:T(8,128)(2,1)S(1)}, bf16[2,2,32,256]{3,2,1,0:T(8,128)(2,1)S(1)}, u32[]{:S(2)}, u32[]{:S(2)}) collective-permute-start(bf16[2,2,32,256]{3,2,1,0:T(8,128)(2,1)S(1)} %get-tuple-element.59), channel_id=1, source_target_pairs={{0,6},{1,7},{2,4},{3,5},{4,2},{5,3},{6,0},{7,1},{8,14},{9,15},{10,... | collective-permute-start | bytes 196616 | tf_op jit(solution)/shard_map/ppermute | solution.py:568
  51.6 8.4 %collective-permute-start.13 = (bf16[2,2,32,256]{3,2,1,0:T(8,128)(2,1)S(1)}, bf16[2,2,32,256]{3,2,1,0:T(8,128)(2,1)S(1)}, u32[]{:S(2)}, u32[]{:S(2)}) collective-permute-start(bf16[2,2,32,256]{3,2,1,0:T(8,128)(2,1)S(1)} %get-tuple-element.60), channel_id=1, source_target_pairs={{0,8},{1,9},{2,10},{3,11},{4,12},{5,13},{6,14},{7,15},{8,0},{9,1},... | collective-permute-start | bytes 196616 | tf_op jit(solution)/shard_map/ppermute | solution.py:568
  51.6 10.1 %collective-permute-start.14 = (bf16[2,2,32,256]{3,2,1,0:T(8,128)(2,1)S(1)}, bf16[2,2,32,256]{3,2,1,0:T(8,128)(2,1)S(1)}, u32[]{:S(2)}, u32[]{:S(2)}) collective-permute-start(bf16[2,2,32,256]{3,2,1,0:T(8,128)(2,1)S(1)} %get-tuple-element.61), channel_id=1, source_target_pairs={{0,10},{1,11},{2,8},{3,9},{4,14},{5,15},{6,12},{7,13},{8,2},{9,3},... | collective-permute-start | bytes 196616 | tf_op jit(solution)/shard_map/ppermute | solution.py:568
  54.5 7.2 %collective-permute-start.15 = (bf16[2,2,32,256]{3,2,1,0:T(8,128)(2,1)S(1)}, bf16[2,2,32,256]{3,2,1,0:T(8,128)(2,1)S(1)}, u32[]{:S(2)}, u32[]{:S(2)}) collective-permute-start(bf16[2,2,32,256]{3,2,1,0:T(8,128)(2,1)S(1)} %get-tuple-element.62), channel_id=1, source_target_pairs={{0,12},{1,13},{2,14},{3,15},{4,8},{5,9},{6,10},{7,11},{8,4},{9,5},... | collective-permute-start | bytes 196616 | tf_op jit(solution)/shard_map/ppermute | solution.py:568

commit v5 on v4

--- a/solution.py
+++ b/solution.py
@@ -172,7 +172,7 @@
         crossed = []
         for piece in range(tall // chunk):
             within = slice(piece * chunk, (piece + 1) * chunk)
-            here = pl.ds(start + piece * chunk, chunk)
+            here = pl.ds(pl.multiple_of(start + piece * chunk, chunk), chunk)
             slow = slow_ref[block, within].astype(f32)
             lower = bracket_ref[here, :] == 0
             weight = jnp.where(lower, (slow - low) * slope_low, (slow - mid) * slope_high)
@@ -180,7 +180,10 @@
             sine, cosine = sin_cos(slow * (angular * layer_thick))
             halves = []
             for plane in range(4):
-                first, second, third = [part_ref[4 * j + plane, within] for j in range(3)]
+                if inverse_y is None:
+                    first, second, third = [returned_ref[4 * j + plane, here] for j in range(3)]
+                else:
+                    first, second, third = [part_ref[4 * j + plane, within] for j in range(3)]
                 bottom = jnp.where(lower, first, second)
                 top = jnp.where(lower, second, third)
                 halves.append(bottom + weight * (top - bottom))
@@ -202,6 +205,10 @@
         for side in range(2):
             put_cross(block, side, jnp.concatenate([pair[side] for pair in crossed], axis=0))
 
+    if inverse_y is None:
+        for block in range(len(starts)):
+            mix(None, block)
+        return
     even, odd = parts
     fill(even, 0)
     for block in range(len(starts)):
@@ -371,19 +378,26 @@
         wait()
 
 
+def unfold_kernel(returned_ref, inverse_y, part_ref):
+    rows, cols = returned_ref.shape[2:]
+    for j in range(3):
+        for plane in range(4):
+            part_ref[4 * j + plane] = dot(returned_ref[j, plane], inverse_y[...])
+
+
 def place_of(rank):
     here = lax.axis_index("freq")
     return (rank ^ here) % 2, (rank // 2) ^ (here // 2)
 
 
 def mix_kernel(*refs, depth, far, last, paired):
-    held_ref, returned_ref, slow_ref, bracket_ref, inverse_y = refs[:5]
-    rest = refs[5:]
+    held_ref, returned_ref, slow_ref, bracket_ref = refs[:4]
+    inverse_y, rest = (None, refs[4:]) if depth == 0 else (refs[4], refs[5:])
     if far:
         near_cross, rest = rest[0], rest[1:]
     if not last:
         wave_ref, rest = rest[0], rest[1:]
-    cross_ref, even, odd = rest
+    cross_ref, *parts = rest
     piece = slow_ref.shape[2]
     tile = cross_ref.shape[-2]
     tiles = piece // tile
@@ -412,7 +426,7 @@
         bracket_ref,
         inverse_y,
         scalars_of(held_ref, depth),
-        (even, odd),
+        parts,
         None if last else put_wave,
         put_cross,
         starts,
@@ -469,19 +483,22 @@
 
 
 IMAGE_ROWS = 8
+PAIR_ORDER = (4, 5, 6, 7, 2, 3, 1)
 
 
 def lag_kernel(lag_ref, *weight_refs):
     bins, pair, lags = lag_ref.shape
     height = bins * pair * IMAGE_ROWS
     here = lax.axis_index("freq")
-    for weight_ref, mask in zip(weight_refs, (0, here)):
+    steps = (0, *PAIR_ORDER)
+    by_pair = [2 * steps[spot // 2] + spot % 2 for spot in range(bins)] if weight_refs[1:] else None
+    for weight_ref, spots, mask in zip(weight_refs, (range(bins), by_pair), (0, here)):
         table = jnp.concatenate(
             [
                 jnp.broadcast_to(lag_ref[spot ^ mask][:, None], (pair, IMAGE_ROWS, lags)).reshape(
                     pair * IMAGE_ROWS, lags
                 )
-                for spot in range(bins)
+                for spot in spots
             ],
             axis=0,
         )
@@ -632,11 +649,22 @@
         own = own + swap(own, bit)
         bit *= 2
     own, returned = lax.optimization_barrier((own, returned))
-    near_slow = jnp.stack([own] + [swap(own, 2 * step) for step in range(1, PIECES)])
+    pieces = [own] + [swap(own, 2 * step) for step in range(1, PIECES)]
+    part = pl.pallas_call(
+        unfold_kernel,
+        in_specs=[vmem] * 2,
+        out_specs=vmem,
+        out_shape=jax.ShapeDtypeStruct((12, rows, cols), f32),
+        compiler_params=pltpu.CompilerParams(vmem_limit_bytes=16 << 20),
+        cost_estimate=pl.CostEstimate(flops=flops // 2, bytes_accessed=1 << 20, transcendentals=0),
+        name="unfold",
+    )(returned, kept_inverse)
+    pieces, part = lax.optimization_barrier((pieces, part))
+    near_slow = jnp.stack(pieces)
     far_slow = swap(near_slow, 1)
 
     blend_scratch = [VMEM((12, piece, cols), f32)] * 2
-    paired = ranks <= 16 and depths > 1 and tile % (2 * IMAGE_ROWS) == 0
+    paired = ranks == 2 * (1 + len(PAIR_ORDER)) and depths > 1 and tile % (2 * IMAGE_ROWS) == 0
     wave_shape = jax.ShapeDtypeStruct((4, half, cols), bf16)
 
     def mix(depth, far, *operands):
@@ -650,7 +678,7 @@
             out_specs=[vmem] * (2 - last),
             out_shape=[wave_shape] * (1 - last)
             + [jax.ShapeDtypeStruct(tiles + (2, tile, cols), bf16)],
-            scratch_shapes=blend_scratch,
+            scratch_shapes=blend_scratch if depth else [],
             compiler_params=pltpu.CompilerParams(vmem_limit_bytes=16 << 20),
             cost_estimate=pl.CostEstimate(
                 flops=flops // 4, bytes_accessed=1 << 20, transcendentals=0
@@ -658,9 +686,9 @@
             name="far" if far else "near",
         )(*operands)
 
-    *near_wave, near_cross = mix(0, False, held_scalars, returned, near_slow, bracket, kept_inverse)
+    *near_wave, near_cross = mix(0, False, held_scalars, part, near_slow, bracket)
     *far_wave, cross = mix(
-        0, True, held_scalars, returned, far_slow, bracket, kept_inverse, near_cross
+        0, True, held_scalars, part, far_slow, bracket, near_cross
     )
     crosses = [cross]
     for depth in range(1, depths):
@@ -715,9 +743,7 @@
         arrivals = [[exchange(cross)] for cross in crosses[:-1]]
         by_core = crosses[-1]
         by_chip = jnp.stack([by_core[0], swap(by_core[1], 1)], axis=1)
-        chips = ranks // 2
-        got = {step: swap(by_chip[step], 2 * step) for step in range(chips - 1, 0, -1)}
-        arrivals.append([by_chip[0]] + [got[step] for step in range(1, chips)])
+        arrivals.append([by_chip[0]] + [swap(by_chip[step], 2 * step) for step in PAIR_ORDER])
     if tile % (2 * IMAGE_ROWS):
         summed = jnp.einsum(
             "dwcab,wcl->dabl",

time: 66 us -> 64.6 us (0.979)
  starting transfers between devices: 29.8 us -> 27.5 us
  waiting for transfers between devices: 8.34 us -> 9.06 us
    ppermute x17, starting transfers between devices: 24.3 us -> 21.8 us  [swap(): return lax.ppermute(value, 'freq', [(i, i ^ bit) for i in range(ranks)])]
    pallas_call x0 -> x1, Pallas kernels: none -> 0.98 us  [shards(): pl.pallas_call(unfold_kernel, in_specs=[vmem] * 2, out_specs=vmem, out_sh...]
    ppermute x17, waiting for transfers between devices: 8.34 us -> 9.05 us  [swap(): return lax.ppermute(value, 'freq', [(i, i ^ bit) for i in range(ranks)])]
    pallas_call x4, Pallas kernels: 5.6 us -> 4.93 us  [mix(): pl.pallas_call(functools.partial(mix_kernel, depth=depth, far=far, last=l...]
  transfers between devices with their start and end apart: 18 -> 18, of which waited for: 9 -> 9; matrix products, arithmetic and copies ran while one was open for 1% -> 1% of each run, Pallas kernels for 29% -> 31%
where the time goes in v5:
time: 64.6 us; the launch traced here: 64.5 us
  starting transfers between devices  27.5 us (43%)
  Pallas kernels  26.7 us (41%)
  waiting for transfers between devices  9.06 us (14%)
  other arithmetic  0.79 us (1%)
    ppermute x17, starting transfers between devices, swap(): return lax.ppermute(value, 'freq', [(i, i ^ bit) for i in range(ranks)])  21.8 us
    ppermute x17, waiting for transfers between devices, swap(): return lax.ppermute(value, 'freq', [(i, i ^ bit) for i in range(ranks)])  9.05 us
    pallas_call x2, Pallas kernels, shards(): pl.pallas_call(functools.partial(image_kernel, scale=scale, depth=depth,...  7.63 us
    all_to_all x1, starting transfers between devices, exchange(): lax.all_to_all(value, 'freq', split_axis=0, concat_axis=0, tiled=True)  5.72 us
    pallas_call x4, Pallas kernels, mix(): pl.pallas_call(functools.partial(mix_kernel, depth=depth, far=far, last=l...  4.93 us
    pallas_call x1, Pallas kernels, shards(): pl.pallas_call(functools.partial(march_kernel, depth=depth), in_specs=[vm...  4.92 us
    pallas_call x1, Pallas kernels, shards(): pl.pallas_call(out_kernel, in_specs=[hbm] * 6, out_specs=[vmem] * 4, out_...  3.74 us
    pallas_call x1, Pallas kernels, shards(): pl.pallas_call(back_kernel, in_specs=[vmem] * 3 + [hbm] * 3, out_specs=[v...  2.98 us
  transfers between devices with their start and end apart: 18, of which 9 were waited for; matrix products, arithmetic and copies ran while one was open for 1% of the time, Pallas kernels for 31%

profile of v5, /device:TPU:0, one launch (start us, length us, event | category | flops | bytes accessed | tf_op | source)
XLA Modules:
  0.0 64.5 jit_solution(15618304314774466131)
XLA Ops:
  0.0 1.2 %window.1 = (bf16[4,2,64,256]{3,2,1,0:T(8,128)(2,1)S(1)}, bf16[4,2,64,256]{3,2,1,0:T(8,128)(2,1)S(1)}) custom-call(s32[2]{0:T(128)} %map_hbm.1, s32[2]{0:T(128)} %corner_hbm.1, bf16[1,768,512]{2,1,0:T(8,128)(2,1)} %slab_hbm.1), custom_call_target="tpu_custom_call" | custom-call | tf_op jit(solution)/shard_map/window/pallas_call | solution.py:569
  1.7 1.2 %collective-permute-done = bf16[4,2,64,256]{3,2,1,0:T(8,128)(2,1)S(1)} collective-permute-done((bf16[4,2,64,256]{3,2,1,0:T(8,128)(2,1)S(1)}, bf16[4,2,64,256]{3,2,1,0:T(8,128)(2,1)S(1)}, u32[]{:S(2)}, u32[]{:S(2)}) %collective-permute-start) | collective-permute-done | bytes 262176 | tf_op jit(solution)/shard_map/ppermute | solution.py:585
  3.0 3.0 %collective-permute-start.2 = (bf16[2,64,256]{2,1,0:T(8,128)(2,1)S(1)}, bf16[2,64,256]{2,1,0:T(8,128)(2,1)S(1)}, u32[]{:S(2)}, u32[]{:S(2)}) collective-permute-start(bf16[2,64,256]{2,1,0:T(8,128)(2,1)S(1)} %get-tuple-element.75), channel_id=1, source_target_pairs={{0,4},{1,5},{2,6},{3,7},{4,0},{5,1},{6,2},{7,3},{8,12},{9,13},{10,... | collective-permute-start | bytes 196616 | tf_op jit(solution)/shard_map/ppermute | solution.py:585
  6.0 1.4 %collective-permute-start.3 = (bf16[2,64,256]{2,1,0:T(8,128)(2,1)S(1)}, bf16[2,64,256]{2,1,0:T(8,128)(2,1)S(1)}, u32[]{:S(2)}, u32[]{:S(2)}) collective-permute-start(bf16[2,64,256]{2,1,0:T(8,128)(2,1)S(1)} %get-tuple-element.76), channel_id=1, source_target_pairs={{0,6},{1,7},{2,4},{3,5},{4,2},{5,3},{6,0},{7,1},{8,14},{9,15},{10,... | collective-permute-start | bytes 196616 | tf_op jit(solution)/shard_map/ppermute | solution.py:585
  7.8 3.7 %out.1 = (f32[4,512,256]{2,1,0:T(8,128)S(1)}, f32[3,512,256]{2,1,0:T(8,128)S(1)}, f32[3,512,256]{2,1,0:T(8,128)S(1)}, f32[8,256]{1,0:T(8,128)S(1)}) custom-call(s32[16]{0:T(128)} %bins_hbm, f32[2,3]{1,0:T(2,128)} %gaps_hbm.1, bf16[2,1,512,256]{3,2,1,0:T(8,128)(2,1)} %source_hbm.1, bf16[2,1,512,256]{3,2,1,0:T(8,128)(2,1)} %receiver_hbm.1, ...), custom_call_target="tpu_custom_call" | custom-call | flops 1073741824 | bytes 4194304 | tf_op jit(solution)/shard_map/out/pallas_call | solution.py:596
  12.3 2.7 %collective-permute-start.4 = (bf16[2,64,256]{2,1,0:T(8,128)(2,1)S(1)}, bf16[2,64,256]{2,1,0:T(8,128)(2,1)S(1)}, u32[]{:S(2)}, u32[]{:S(2)}) collective-permute-start(bf16[2,64,256]{2,1,0:T(8,128)(2,1)S(1)} %bitcast_add_fusion), channel_id=1, source_target_pairs={{0,8},{1,9},{2,10},{3,11},{4,12},{5,13},{6,14},{7,15},{8,0},{9,1},... | collective-permute-start | bytes 196616 | tf_op jit(solution)/shard_map/ppermute | solution.py:585
  15.0 3.0 %back.1 = (bf16[3,4,512,256]{3,2,1,0:T(8,128)(2,1)S(1)}, s32[512,256]{1,0:T(8,128)S(1)}, bf16[256,256]{1,0:T(8,128)(2,1)S(1)}) custom-call(f32[4,512,256]{2,1,0:T(8,128)S(1)} %get-tuple-element.44.spec_ref, f32[3,512,256]{2,1,0:T(8,128)S(1)} %get-tuple-element.45.cos_ref, f32[3,512,256]{2,1,0:T(8,128)S(1)} %get-tuple-element.46.sin_ref, ...), custom_call_target="tpu_custom_call" | custom-call | flops 2147483648 | bytes 4194304 | tf_op jit(solution)/shard_map/back/pallas_call | solution.py:629
  18.0 2.3 %collective-permute-start.7 = (bf16[2,64,256]{2,1,0:T(8,128)(2,1)S(1)}, bf16[2,64,256]{2,1,0:T(8,128)(2,1)S(1)}, u32[]{:S(2)}, u32[]{:S(2)}) collective-permute-start(bf16[2,64,256]{2,1,0:T(8,128)(2,1)S(1)} %add.41), channel_id=1, source_target_pairs={{0,6},{1,7},{2,4},{3,5},{4,2},{5,3},{6,0},{7,1},{8,14},{9,15},{10,... | collective-permute-start | bytes 196616 | tf_op jit(solution)/shard_map/ppermute | solution.py:585
  20.5 1.1 %collective-permute-start.5 = (bf16[2,64,256]{2,1,0:T(8,128)(2,1)S(1)}, bf16[2,64,256]{2,1,0:T(8,128)(2,1)S(1)}, u32[]{:S(2)}, u32[]{:S(2)}) collective-permute-start(bf16[2,64,256]{2,1,0:T(8,128)(2,1)S(1)} %add.41), channel_id=1, source_target_pairs={{0,2},{1,3},{2,0},{3,1},{4,6},{5,7},{6,4},{7,5},{8,10},{9,11},{10,... | collective-permute-start | bytes 196616 | tf_op jit(solution)/shard_map/ppermute | solution.py:585
  23.5 1.0 %collective-permute-done.6 = bf16[2,64,256]{2,1,0:T(8,128)(2,1)S(1)} collective-permute-done((bf16[2,64,256]{2,1,0:T(8,128)(2,1)S(1)}, bf16[2,64,256]{2,1,0:T(8,128)(2,1)S(1)}, u32[]{:S(2)}, u32[]{:S(2)}) %collective-permute-start.6) | collective-permute-done | bytes 65568 | tf_op jit(solution)/shard_map/ppermute | solution.py:585
  26.4 1.6 %far.2 = (bf16[4,256,256]{2,1,0:T(8,128)(2,1)S(1)}, bf16[16,2,32,256]{3,2,1,0:T(8,128)(2,1)}) custom-call(f32[8,256]{1,0:T(8,128)S(1)} %get-tuple-element.38.refs_0_.held_ref, f32[12,512,256]{2,1,0:T(8,128)S(1)} %unfold.1.refs_1_, bf16[4,2,64,256]{3,2,1,0:T(8,128)(2,1)S(1)} %collective-permute-done.8.refs_2_, s32[512,256]{1,0:T(8,128)S(1)} %get-tuple-element.56.refs_3_, ...), custom_call_target="tpu_custom_call" | custom-call | flops 536870912 | bytes 1048576 | tf_op jit(solution)/shard_map/far/pallas_call | solution.py:673
  28.1 5.7 %all-to-all-start = ((bf16[16,2,32,256]{3,2,1,0:T(8,128)(2,1)}), bf16[16,2,32,256]{3,2,1,0:T(8,128)(2,1)S(1)}, u32[]{:S(2)}, u32[]{:S(2)}) async-start(bf16[16,2,32,256]{3,2,1,0:T(8,128)(2,1)} %get-tuple-element.63), calls=%async_computation | async-start | bytes 1048576 | tf_op jit(solution)/shard_map/all_to_all | solution.py:738
  33.8 4.9 %march.1 = (bf16[3,4,512,256]{3,2,1,0:T(8,128)(2,1)S(1)}, s32[512,256]{1,0:T(8,128)S(1)}) custom-call(f32[8,256]{1,0:T(8,128)S(1)} %get-tuple-element.38.refs_0_.held_ref, bf16[4,256,256]{2,1,0:T(8,128)(2,1)S(1)} %get-tuple-element.57.near_wave, bf16[4,256,256]{2,1,0:T(8,128)(2,1)S(1)} %get-tuple-element.59.far_wave, s32[2,512,256]{2,1,0:T(8,128)} %bracket_hbm.3, ...), custom_call_target="tpu_custom_call" | custom-call | flops 3221225472 | bytes 8388608 | tf_op jit(solution)/shard_map/march/pallas_call | solution.py:695
  38.7 1.2 %near.3.refs_5_ = bf16[8,2,32,256]{3,2,1,0:T(8,128)(2,1)S(1)} custom-call(f32[8,256]{1,0:T(8,128)S(1)} %get-tuple-element.38.refs_0_.held_ref, bf16[3,4,512,256]{3,2,1,0:T(8,128)(2,1)S(1)} %get-tuple-element.60.refs_1_, bf16[4,2,64,256]{3,2,1,0:T(8,128)(2,1)S(1)} %pad_maximum_fusion.refs_2_, s32[512,256]{1,0:T(8,128)S(1)} %get-tuple-element.61.refs_3_, ...), custom_call_target="tpu_custom_call" | custom-call | flops 536870912 | bytes 1048576 | tf_op jit(solution)/shard_map/near/pallas_call | solution.py:673
  39.9 1.2 %far.3 = bf16[2,8,2,32,256]{4,3,2,1,0:T(8,128)(2,1)S(1)} custom-call(f32[8,256]{1,0:T(8,128)S(1)} %get-tuple-element.38.refs_0_.held_ref, bf16[3,4,512,256]{3,2,1,0:T(8,128)(2,1)S(1)} %get-tuple-element.60.refs_1_, bf16[4,2,64,256]{3,2,1,0:T(8,128)(2,1)S(1)} %collective-permute-done.8.refs_2_, s32[512,256]{1,0:T(8,128)S(1)} %get-tuple-element.61.refs_3_, ...), custom_call_target="tpu_custom_call" | custom-call | flops 536870912 | bytes 1048576 | tf_op jit(solution)/shard_map/far/pallas_call | solution.py:673
  41.8 1.1 %collective-permute-done.9 = bf16[8,2,32,256]{3,2,1,0:T(8,128)(2,1)S(1)} collective-permute-done((bf16[8,2,32,256]{3,2,1,0:T(8,128)(2,1)S(1)}, bf16[8,2,32,256]{3,2,1,0:T(8,128)(2,1)S(1)}, u32[]{:S(2)}, u32[]{:S(2)}) %collective-permute-start.9) | collective-permute-done | bytes 262176 | tf_op jit(solution)/shard_map/ppermute | solution.py:585
  42.9 2.0 %collective-permute-start.16 = (bf16[2,2,32,256]{3,2,1,0:T(8,128)(2,1)S(1)}, bf16[2,2,32,256]{3,2,1,0:T(8,128)(2,1)S(1)}, u32[]{:S(2)}, u32[]{:S(2)}) collective-permute-start(bf16[2,2,32,256]{3,2,1,0:T(8,128)(2,1)S(1)} %get-tuple-element.65), channel_id=1, source_target_pairs={{0,2},{1,3},{2,0},{3,1},{4,6},{5,7},{6,4},{7,5},{8,10},{9,11},{10,... | collective-permute-start | bytes 196616 | tf_op jit(solution)/shard_map/ppermute | solution.py:585
  44.9 2.4 %collective-permute-start.10 = (bf16[2,2,32,256]{3,2,1,0:T(8,128)(2,1)S(1)}, bf16[2,2,32,256]{3,2,1,0:T(8,128)(2,1)S(1)}, u32[]{:S(2)}, u32[]{:S(2)}) collective-permute-start(bf16[2,2,32,256]{3,2,1,0:T(8,128)(2,1)S(1)} %get-tuple-element.67), channel_id=1, source_target_pairs={{0,8},{1,9},{2,10},{3,11},{4,12},{5,13},{6,14},{7,15},{8,0},{9,1},... | collective-permute-start | bytes 196616 | tf_op jit(solution)/shard_map/ppermute | solution.py:585
  47.9 3.7 %collective-permute-start.12 = (bf16[2,2,32,256]{3,2,1,0:T(8,128)(2,1)S(1)}, bf16[2,2,32,256]{3,2,1,0:T(8,128)(2,1)S(1)}, u32[]{:S(2)}, u32[]{:S(2)}) collective-permute-start(bf16[2,2,32,256]{3,2,1,0:T(8,128)(2,1)S(1)} %get-tuple-element.69), channel_id=1, source_target_pairs={{0,12},{1,13},{2,14},{3,15},{4,8},{5,9},{6,10},{7,11},{8,4},{9,5},... | collective-permute-start | bytes 196616 | tf_op jit(solution)/shard_map/ppermute | solution.py:585
  51.6 1.5 %collective-permute-start.13 = (bf16[2,2,32,256]{3,2,1,0:T(8,128)(2,1)S(1)}, bf16[2,2,32,256]{3,2,1,0:T(8,128)(2,1)S(1)}, u32[]{:S(2)}, u32[]{:S(2)}) collective-permute-start(bf16[2,2,32,256]{3,2,1,0:T(8,128)(2,1)S(1)} %get-tuple-element.70), channel_id=1, source_target_pairs={{0,14},{1,15},{2,12},{3,13},{4,10},{5,11},{6,8},{7,9},{8,6},{9,7},... | collective-permute-start | bytes 196616 | tf_op jit(solution)/shard_map/ppermute | solution.py:585
  53.1 2.2 %collective-permute-done.10.refs_1_ = bf16[2,2,32,256]{3,2,1,0:T(8,128)(2,1)S(1)} collective-permute-done((bf16[2,2,32,256]{3,2,1,0:T(8,128)(2,1)S(1)}, bf16[2,2,32,256]{3,2,1,0:T(8,128)(2,1)S(1)}, u32[]{:S(2)}, u32[]{:S(2)}) %collective-permute-start.10) | collective-permute-done | bytes 65568 | tf_op jit(solution)/shard_map/ppermute | solution.py:585
  55.6 3.8 %image.2.refs_9_ = f32[2,32,256,256]{3,2,1,0:T(8,128)} custom-call(bf16[16,2,32,256]{3,2,1,0:T(8,128)(2,1)S(1)} %all-to-all-done.refs_0_, bf16[256,2048]{1,0:T(8,128)(2,1)S(1)} %get-tuple-element.64.refs_1_), custom_call_target="tpu_custom_call" | custom-call | tf_op jit(solution)/shard_map/image/pallas_call | solution.py:768
  59.5 1.0 %collective-permute-done.15.refs_6_ = bf16[2,2,32,256]{3,2,1,0:T(8,128)(2,1)S(1)} collective-permute-done((bf16[2,2,32,256]{3,2,1,0:T(8,128)(2,1)S(1)}, bf16[2,2,32,256]{3,2,1,0:T(8,128)(2,1)S(1)}, u32[]{:S(2)}, u32[]{:S(2)}) %collective-permute-start.15) | collective-permute-done | bytes 65568 | tf_op jit(solution)/shard_map/ppermute | solution.py:585
  60.5 3.8 %image.3 = f32[2,32,256,256]{3,2,1,0:T(8,128)} custom-call(bf16[2,2,32,256]{3,2,1,0:T(8,128)(2,1)S(1)} %get-tuple-element.66.refs_0_, bf16[2,2,32,256]{3,2,1,0:T(8,128)(2,1)S(1)} %collective-permute-done.10.refs_1_, bf16[2,2,32,256]{3,2,1,0:T(8,128)(2,1)S(1)} %collective-permute-done.11.refs_2_, ...), custom_call_target="tpu_custom_call", output_to_operand_aliasing={{}: (9, {})} | custom-call | tf_op jit(solution)/shard_map/image/pallas_call | solution.py:768
  (37 shorter events, 7.5 us)
Async XLA Ops:
  1.2 1.7 %collective-permute-start = (bf16[4,2,64,256]{3,2,1,0:T(8,128)(2,1)S(1)}, bf16[4,2,64,256]{3,2,1,0:T(8,128)(2,1)S(1)}, u32[]{:S(2)}, u32[]{:S(2)}) collective-permute-start(bf16[4,2,64,256]{3,2,1,0:T(8,128)(2,1)S(1)} %get-tuple-element.36), channel_id=1, source_target_pairs={{0,1},{1,0},{2,3},{3,2},{4,5},{5,4},{6,7},{7,6},{8,9},{9,8},{10,11... | collective-permute-start | bytes 786440 | tf_op jit(solution)/shard_map/ppermute | solution.py:585
  3.0 8.6 %collective-permute-start.2 = (bf16[2,64,256]{2,1,0:T(8,128)(2,1)S(1)}, bf16[2,64,256]{2,1,0:T(8,128)(2,1)S(1)}, u32[]{:S(2)}, u32[]{:S(2)}) collective-permute-start(bf16[2,64,256]{2,1,0:T(8,128)(2,1)S(1)} %get-tuple-element.75), channel_id=1, source_target_pairs={{0,4},{1,5},{2,6},{3,7},{4,0},{5,1},{6,2},{7,3},{8,12},{9,13},{10,... | collective-permute-start | bytes 196616 | tf_op jit(solution)/shard_map/ppermute | solution.py:585
  6.0 5.6 %collective-permute-start.3 = (bf16[2,64,256]{2,1,0:T(8,128)(2,1)S(1)}, bf16[2,64,256]{2,1,0:T(8,128)(2,1)S(1)}, u32[]{:S(2)}, u32[]{:S(2)}) collective-permute-start(bf16[2,64,256]{2,1,0:T(8,128)(2,1)S(1)} %get-tuple-element.76), channel_id=1, source_target_pairs={{0,6},{1,7},{2,4},{3,5},{4,2},{5,3},{6,0},{7,1},{8,14},{9,15},{10,... | collective-permute-start | bytes 196616 | tf_op jit(solution)/shard_map/ppermute | solution.py:585
  7.4 5.0 %collective-permute-start.1 = (bf16[2,64,256]{2,1,0:T(8,128)(2,1)S(1)}, bf16[2,64,256]{2,1,0:T(8,128)(2,1)S(1)}, u32[]{:S(2)}, u32[]{:S(2)}) collective-permute-start(bf16[2,64,256]{2,1,0:T(8,128)(2,1)S(1)} %get-tuple-element.77), channel_id=1, source_target_pairs={{0,2},{1,3},{2,0},{3,1},{4,6},{5,7},{6,4},{7,5},{8,10},{9,11},{10,... | collective-permute-start | bytes 196616 | tf_op jit(solution)/shard_map/ppermute | solution.py:585
  12.3 5.7 %collective-permute-start.4 = (bf16[2,64,256]{2,1,0:T(8,128)(2,1)S(1)}, bf16[2,64,256]{2,1,0:T(8,128)(2,1)S(1)}, u32[]{:S(2)}, u32[]{:S(2)}) collective-permute-start(bf16[2,64,256]{2,1,0:T(8,128)(2,1)S(1)} %bitcast_add_fusion), channel_id=1, source_target_pairs={{0,8},{1,9},{2,10},{3,11},{4,12},{5,13},{6,14},{7,15},{8,0},{9,1},... | collective-permute-start | bytes 196616 | tf_op jit(solution)/shard_map/ppermute | solution.py:585
  18.0 5.5 %collective-permute-start.7 = (bf16[2,64,256]{2,1,0:T(8,128)(2,1)S(1)}, bf16[2,64,256]{2,1,0:T(8,128)(2,1)S(1)}, u32[]{:S(2)}, u32[]{:S(2)}) collective-permute-start(bf16[2,64,256]{2,1,0:T(8,128)(2,1)S(1)} %add.41), channel_id=1, source_target_pairs={{0,6},{1,7},{2,4},{3,5},{4,2},{5,3},{6,0},{7,1},{8,14},{9,15},{10,... | collective-permute-start | bytes 196616 | tf_op jit(solution)/shard_map/ppermute | solution.py:585
  20.3 4.3 %collective-permute-start.6 = (bf16[2,64,256]{2,1,0:T(8,128)(2,1)S(1)}, bf16[2,64,256]{2,1,0:T(8,128)(2,1)S(1)}, u32[]{:S(2)}, u32[]{:S(2)}) collective-permute-start(bf16[2,64,256]{2,1,0:T(8,128)(2,1)S(1)} %add.41), channel_id=1, source_target_pairs={{0,4},{1,5},{2,6},{3,7},{4,0},{5,1},{6,2},{7,3},{8,12},{9,13},{10,... | collective-permute-start | bytes 196616 | tf_op jit(solution)/shard_map/ppermute | solution.py:585
  20.5 4.3 %collective-permute-start.5 = (bf16[2,64,256]{2,1,0:T(8,128)(2,1)S(1)}, bf16[2,64,256]{2,1,0:T(8,128)(2,1)S(1)}, u32[]{:S(2)}, u32[]{:S(2)}) collective-permute-start(bf16[2,64,256]{2,1,0:T(8,128)(2,1)S(1)} %add.41), channel_id=1, source_target_pairs={{0,2},{1,3},{2,0},{3,1},{4,6},{5,7},{6,4},{7,5},{8,10},{9,11},{10,... | collective-permute-start | bytes 196616 | tf_op jit(solution)/shard_map/ppermute | solution.py:585
  24.8 1.6 %collective-permute-start.8 = (bf16[4,2,64,256]{3,2,1,0:T(8,128)(2,1)S(1)}, bf16[4,2,64,256]{3,2,1,0:T(8,128)(2,1)S(1)}, u32[]{:S(2)}, u32[]{:S(2)}) collective-permute-start(bf16[4,2,64,256]{3,2,1,0:T(8,128)(2,1)S(1)} %pad_maximum_fusion.refs_2_), channel_id=1, source_target_pairs={{0,1},{1,0},{2,3},{3,2},{4,5},{5,4},{6,7},{7,6},{8,9},{9,8},{10,11... | collective-permute-start | bytes 786440 | tf_op jit(solution)/shard_map/ppermute | solution.py:585
  28.1 27.6 %all-to-all-start = ((bf16[16,2,32,256]{3,2,1,0:T(8,128)(2,1)}), bf16[16,2,32,256]{3,2,1,0:T(8,128)(2,1)S(1)}, u32[]{:S(2)}, u32[]{:S(2)}) async-start(bf16[16,2,32,256]{3,2,1,0:T(8,128)(2,1)} %get-tuple-element.63), calls=%async_computation | async-start | bytes 1048576 | tf_op jit(solution)/shard_map/all_to_all | solution.py:738
  39.9 1.8 %copy-start = (s32[16]{0:T(128)S(1)}, s32[16]{0:T(128)}, u32[]{:S(2)}) copy-start(s32[16]{0:T(128)} %bins_hbm) | copy-start | bytes 196
  41.2 1.6 %collective-permute-start.9 = (bf16[8,2,32,256]{3,2,1,0:T(8,128)(2,1)S(1)}, bf16[8,2,32,256]{3,2,1,0:T(8,128)(2,1)S(1)}, u32[]{:S(2)}, u32[]{:S(2)}) collective-permute-start(bf16[8,2,32,256]{3,2,1,0:T(8,128)(2,1)S(1)} %get-tuple-element.74), channel_id=1, source_target_pairs={{0,1},{1,0},{2,3},{3,2},{4,5},{5,4},{6,7},{7,6},{8,9},{9,8},{10,11... | collective-permute-start | bytes 786440 | tf_op jit(solution)/shard_map/ppermute | solution.py:585
  42.9 10.2 %collective-permute-start.16 = (bf16[2,2,32,256]{3,2,1,0:T(8,128)(2,1)S(1)}, bf16[2,2,32,256]{3,2,1,0:T(8,128)(2,1)S(1)}, u32[]{:S(2)}, u32[]{:S(2)}) collective-permute-start(bf16[2,2,32,256]{3,2,1,0:T(8,128)(2,1)S(1)} %get-tuple-element.65), channel_id=1, source_target_pairs={{0,2},{1,3},{2,0},{3,1},{4,6},{5,7},{6,4},{7,5},{8,10},{9,11},{10,... | collective-permute-start | bytes 196616 | tf_op jit(solution)/shard_map/ppermute | solution.py:585
  44.9 10.4 %collective-permute-start.10 = (bf16[2,2,32,256]{3,2,1,0:T(8,128)(2,1)S(1)}, bf16[2,2,32,256]{3,2,1,0:T(8,128)(2,1)S(1)}, u32[]{:S(2)}, u32[]{:S(2)}) collective-permute-start(bf16[2,2,32,256]{3,2,1,0:T(8,128)(2,1)S(1)} %get-tuple-element.67), channel_id=1, source_target_pairs={{0,8},{1,9},{2,10},{3,11},{4,12},{5,13},{6,14},{7,15},{8,0},{9,1},... | collective-permute-start | bytes 196616 | tf_op jit(solution)/shard_map/ppermute | solution.py:585
  47.7 11.8 %collective-permute-start.11 = (bf16[2,2,32,256]{3,2,1,0:T(8,128)(2,1)S(1)}, bf16[2,2,32,256]{3,2,1,0:T(8,128)(2,1)S(1)}, u32[]{:S(2)}, u32[]{:S(2)}) collective-permute-start(bf16[2,2,32,256]{3,2,1,0:T(8,128)(2,1)S(1)} %get-tuple-element.68), channel_id=1, source_target_pairs={{0,10},{1,11},{2,8},{3,9},{4,14},{5,15},{6,12},{7,13},{8,2},{9,3},... | collective-permute-start | bytes 196616 | tf_op jit(solution)/shard_map/ppermute | solution.py:585
  47.9 11.6 %collective-permute-start.12 = (bf16[2,2,32,256]{3,2,1,0:T(8,128)(2,1)S(1)}, bf16[2,2,32,256]{3,2,1,0:T(8,128)(2,1)S(1)}, u32[]{:S(2)}, u32[]{:S(2)}) collective-permute-start(bf16[2,2,32,256]{3,2,1,0:T(8,128)(2,1)S(1)} %get-tuple-element.69), channel_id=1, source_target_pairs={{0,12},{1,13},{2,14},{3,15},{4,8},{5,9},{6,10},{7,11},{8,4},{9,5},... | collective-permute-start | bytes 196616 | tf_op jit(solution)/shard_map/ppermute | solution.py:585
  51.6 7.9 %collective-permute-start.13 = (bf16[2,2,32,256]{3,2,1,0:T(8,128)(2,1)S(1)}, bf16[2,2,32,256]{3,2,1,0:T(8,128)(2,1)S(1)}, u32[]{:S(2)}, u32[]{:S(2)}) collective-permute-start(bf16[2,2,32,256]{3,2,1,0:T(8,128)(2,1)S(1)} %get-tuple-element.70), channel_id=1, source_target_pairs={{0,14},{1,15},{2,12},{3,13},{4,10},{5,11},{6,8},{7,9},{8,6},{9,7},... | collective-permute-start | bytes 196616 | tf_op jit(solution)/shard_map/ppermute | solution.py:585
  53.1 6.4 %collective-permute-start.14 = (bf16[2,2,32,256]{3,2,1,0:T(8,128)(2,1)S(1)}, bf16[2,2,32,256]{3,2,1,0:T(8,128)(2,1)S(1)}, u32[]{:S(2)}, u32[]{:S(2)}) collective-permute-start(bf16[2,2,32,256]{3,2,1,0:T(8,128)(2,1)S(1)} %get-tuple-element.71), channel_id=1, source_target_pairs={{0,4},{1,5},{2,6},{3,7},{4,0},{5,1},{6,2},{7,3},{8,12},{9,13},{10,... | collective-permute-start | bytes 196616 | tf_op jit(solution)/shard_map/ppermute | solution.py:585
  55.2 5.3 %collective-permute-start.15 = (bf16[2,2,32,256]{3,2,1,0:T(8,128)(2,1)S(1)}, bf16[2,2,32,256]{3,2,1,0:T(8,128)(2,1)S(1)}, u32[]{:S(2)}, u32[]{:S(2)}) collective-permute-start(bf16[2,2,32,256]{3,2,1,0:T(8,128)(2,1)S(1)} %get-tuple-element.72), channel_id=1, source_target_pairs={{0,6},{1,7},{2,4},{3,5},{4,2},{5,3},{6,0},{7,1},{8,14},{9,15},{10,... | collective-permute-start | bytes 196616 | tf_op jit(solution)/shard_map/ppermute | solution.py:585

commit v6 on v5

--- a/solution.py
+++ b/solution.py
@@ -483,7 +483,7 @@
 
 
 IMAGE_ROWS = 8
-PAIR_ORDER = (4, 5, 6, 7, 2, 3, 1)
+PAIR_ORDER = (2, 4, 5, 6, 7, 3, 1)
 
 
 def lag_kernel(lag_ref, *weight_refs):
@@ -661,7 +661,12 @@
     )(returned, kept_inverse)
     pieces, part = lax.optimization_barrier((pieces, part))
     near_slow = jnp.stack(pieces)
-    far_slow = swap(near_slow, 1)
+    offsets = jnp.arange(LAGS, dtype=jnp.int32) - LAGS // 2
+    cycles = jnp.mod(frequency_bins[:, None] * offsets[None, :], period_bins).astype(f32)
+    angles = cycles * (2.0 * math.pi / period_bins)
+    lag_weights = jnp.stack([jnp.cos(angles), jnp.sin(angles)], axis=1).astype(bf16)
+
+    far_slow, lag_weights = lax.optimization_barrier((swap(near_slow, 1), lag_weights))
 
     blend_scratch = [VMEM((12, piece, cols), f32)] * 2
     paired = ranks == 2 * (1 + len(PAIR_ORDER)) and depths > 1 and tile % (2 * IMAGE_ROWS) == 0
@@ -727,11 +732,6 @@
             depth, True, held_scalars, returned, far_slow, bracket, kept_inverse, near_cross
         )
         crosses.append(cross)
-
-    offsets = jnp.arange(LAGS, dtype=jnp.int32) - LAGS // 2
-    cycles = jnp.mod(frequency_bins[:, None] * offsets[None, :], period_bins).astype(f32)
-    angles = cycles * (2.0 * math.pi / period_bins)
-    lag_weights = jnp.stack([jnp.cos(angles), jnp.sin(angles)], axis=1).astype(bf16)
 
     scale = bins ** (-0.5)
     def exchange(value):

time: 64.6 us -> 63.7 us (0.986)
  waiting for transfers between devices: 9.06 us -> 6.49 us
  starting transfers between devices: 27.5 us -> 28.4 us
  other arithmetic: 0.79 us -> 1.46 us
    ppermute x17, waiting for transfers between devices: 9.05 us -> 6.49 us  [swap(): return lax.ppermute(value, 'freq', [(i, i ^ bit) for i in range(ranks)])]
    ppermute x17, starting transfers between devices: 21.8 us -> 22.9 us  [swap(): return lax.ppermute(value, 'freq', [(i, i ^ bit) for i in range(ranks)])]
    convert_element_type x1, other arithmetic: 0.08 us -> 0.74 us  [shards(): jnp.mod(frequency_bins[:, None] * offsets[None, :], period_bins).astype(f32)]
  transfers between devices with their start and end apart: 18 -> 18, of which waited for: 9 -> 9; matrix products, arithmetic and copies ran while one was open for 1% -> 2% of each run, Pallas kernels for 31% -> 32%
where the time goes in v6:
time: 63.7 us; the launch traced here: 63.4 us
  starting transfers between devices  28.4 us (45%)
  Pallas kernels  26.7 us (42%)
  waiting for transfers between devices  6.49 us (10%)
  other arithmetic  1.46 us (2%)
    ppermute x17, starting transfers between devices, swap(): return lax.ppermute(value, 'freq', [(i, i ^ bit) for i in range(ranks)])  22.9 us
    pallas_call x2, Pallas kernels, shards(): pl.pallas_call(functools.partial(image_kernel, scale=scale, depth=depth,...  7.63 us
    ppermute x17, waiting for transfers between devices, swap(): return lax.ppermute(value, 'freq', [(i, i ^ bit) for i in range(ranks)])  6.49 us
    all_to_all x1, starting transfers between devices, exchange(): lax.all_to_all(value, 'freq', split_axis=0, concat_axis=0, tiled=True)  5.5 us
    pallas_call x4, Pallas kernels, mix(): pl.pallas_call(functools.partial(mix_kernel, depth=depth, far=far, last=l...  4.93 us
    pallas_call x1, Pallas kernels, shards(): pl.pallas_call(functools.partial(march_kernel, depth=depth), in_specs=[vm...  4.93 us
    pallas_call x1, Pallas kernels, shards(): pl.pallas_call(out_kernel, in_specs=[hbm] * 6, out_specs=[vmem] * 4, out_...  3.74 us
    pallas_call x1, Pallas kernels, shards(): pl.pallas_call(back_kernel, in_specs=[vmem] * 3 + [hbm] * 3, out_specs=[v...  2.98 us
  transfers between devices with their start and end apart: 18, of which 9 were waited for; matrix products, arithmetic and copies ran while one was open for 2% of the time, Pallas kernels for 32%

profile of v6, /device:TPU:0, one launch (start us, length us, event | category | flops | bytes accessed | tf_op | source)
XLA Modules:
  0.0 63.4 jit_solution(13369573924425469300)
XLA Ops:
  0.0 1.2 %window.1 = (bf16[4,2,64,256]{3,2,1,0:T(8,128)(2,1)S(1)}, bf16[4,2,64,256]{3,2,1,0:T(8,128)(2,1)S(1)}) custom-call(s32[2]{0:T(128)} %map_hbm.1, s32[2]{0:T(128)} %corner_hbm.1, bf16[1,768,512]{2,1,0:T(8,128)(2,1)} %slab_hbm.1), custom_call_target="tpu_custom_call" | custom-call | tf_op jit(solution)/shard_map/window/pallas_call | solution.py:569
  3.0 3.0 %collective-permute-start.2 = (bf16[2,64,256]{2,1,0:T(8,128)(2,1)S(1)}, bf16[2,64,256]{2,1,0:T(8,128)(2,1)S(1)}, u32[]{:S(2)}, u32[]{:S(2)}) collective-permute-start(bf16[2,64,256]{2,1,0:T(8,128)(2,1)S(1)} %get-tuple-element.79), channel_id=1, source_target_pairs={{0,4},{1,5},{2,6},{3,7},{4,0},{5,1},{6,2},{7,3},{8,12},{9,13},{10,... | collective-permute-start | bytes 196616 | tf_op jit(solution)/shard_map/ppermute | solution.py:585
  6.0 1.4 %collective-permute-start.3 = (bf16[2,64,256]{2,1,0:T(8,128)(2,1)S(1)}, bf16[2,64,256]{2,1,0:T(8,128)(2,1)S(1)}, u32[]{:S(2)}, u32[]{:S(2)}) collective-permute-start(bf16[2,64,256]{2,1,0:T(8,128)(2,1)S(1)} %get-tuple-element.80), channel_id=1, source_target_pairs={{0,6},{1,7},{2,4},{3,5},{4,2},{5,3},{6,0},{7,1},{8,14},{9,15},{10,... | collective-permute-start | bytes 196616 | tf_op jit(solution)/shard_map/ppermute | solution.py:585
  7.5 3.7 %out.1 = (f32[4,512,256]{2,1,0:T(8,128)S(1)}, f32[3,512,256]{2,1,0:T(8,128)S(1)}, f32[3,512,256]{2,1,0:T(8,128)S(1)}, f32[8,256]{1,0:T(8,128)S(1)}) custom-call(s32[16]{0:T(128)} %bins_hbm, f32[2,3]{1,0:T(2,128)} %gaps_hbm.1, bf16[2,1,512,256]{3,2,1,0:T(8,128)(2,1)} %source_hbm.1, bf16[2,1,512,256]{3,2,1,0:T(8,128)(2,1)} %receiver_hbm.1, ...), custom_call_target="tpu_custom_call" | custom-call | flops 1073741824 | bytes 4194304 | tf_op jit(solution)/shard_map/out/pallas_call | solution.py:596
  12.2 2.6 %collective-permute-start.4 = (bf16[2,64,256]{2,1,0:T(8,128)(2,1)S(1)}, bf16[2,64,256]{2,1,0:T(8,128)(2,1)S(1)}, u32[]{:S(2)}, u32[]{:S(2)}) collective-permute-start(bf16[2,64,256]{2,1,0:T(8,128)(2,1)S(1)} %bitcast_add_fusion), channel_id=1, source_target_pairs={{0,8},{1,9},{2,10},{3,11},{4,12},{5,13},{6,14},{7,15},{8,0},{9,1},... | collective-permute-start | bytes 196616 | tf_op jit(solution)/shard_map/ppermute | solution.py:585
  14.9 3.0 %back.1 = (bf16[3,4,512,256]{3,2,1,0:T(8,128)(2,1)S(1)}, s32[512,256]{1,0:T(8,128)S(1)}, bf16[256,256]{1,0:T(8,128)(2,1)S(1)}) custom-call(f32[4,512,256]{2,1,0:T(8,128)S(1)} %get-tuple-element.46.spec_ref, f32[3,512,256]{2,1,0:T(8,128)S(1)} %get-tuple-element.47.cos_ref, f32[3,512,256]{2,1,0:T(8,128)S(1)} %get-tuple-element.48.sin_ref, ...), custom_call_target="tpu_custom_call" | custom-call | flops 2147483648 | bytes 4194304 | tf_op jit(solution)/shard_map/back/pallas_call | solution.py:629
  17.9 2.1 %collective-permute-start.7 = (bf16[2,64,256]{2,1,0:T(8,128)(2,1)S(1)}, bf16[2,64,256]{2,1,0:T(8,128)(2,1)S(1)}, u32[]{:S(2)}, u32[]{:S(2)}) collective-permute-start(bf16[2,64,256]{2,1,0:T(8,128)(2,1)S(1)} %add.41), channel_id=1, source_target_pairs={{0,6},{1,7},{2,4},{3,5},{4,2},{5,3},{6,0},{7,1},{8,14},{9,15},{10,... | collective-permute-start | bytes 196616 | tf_op jit(solution)/shard_map/ppermute | solution.py:585
  20.4 1.1 %collective-permute-start.5 = (bf16[2,64,256]{2,1,0:T(8,128)(2,1)S(1)}, bf16[2,64,256]{2,1,0:T(8,128)(2,1)S(1)}, u32[]{:S(2)}, u32[]{:S(2)}) collective-permute-start(bf16[2,64,256]{2,1,0:T(8,128)(2,1)S(1)} %add.41), channel_id=1, source_target_pairs={{0,2},{1,3},{2,0},{3,1},{4,6},{5,7},{6,4},{7,5},{8,10},{9,11},{10,... | collective-permute-start | bytes 196616 | tf_op jit(solution)/shard_map/ppermute | solution.py:585
  21.5 1.0 %unfold.1.refs_1_ = f32[12,512,256]{2,1,0:T(8,128)S(1)} custom-call(bf16[3,4,512,256]{3,2,1,0:T(8,128)(2,1)S(1)} %get-tuple-element.51.returned_ref, bf16[256,256]{1,0:T(8,128)(2,1)S(1)} %get-tuple-element.52.inverse_y.refs_4_), custom_call_target="tpu_custom_call" | custom-call | flops 1073741824 | bytes 1048576 | tf_op jit(solution)/shard_map/unfold/pallas_call | solution.py:653
  23.2 1.0 %collective-permute-done.6 = bf16[2,64,256]{2,1,0:T(8,128)(2,1)S(1)} collective-permute-done((bf16[2,64,256]{2,1,0:T(8,128)(2,1)S(1)}, bf16[2,64,256]{2,1,0:T(8,128)(2,1)S(1)}, u32[]{:S(2)}, u32[]{:S(2)}) %collective-permute-start.6) | collective-permute-done | bytes 65568 | tf_op jit(solution)/shard_map/ppermute | solution.py:585
  26.3 1.6 %far.2 = (bf16[4,256,256]{2,1,0:T(8,128)(2,1)S(1)}, bf16[16,2,32,256]{3,2,1,0:T(8,128)(2,1)}) custom-call(f32[8,256]{1,0:T(8,128)S(1)} %get-tuple-element.40.refs_0_.held_ref, f32[12,512,256]{2,1,0:T(8,128)S(1)} %unfold.1.refs_1_, bf16[4,2,64,256]{3,2,1,0:T(8,128)(2,1)S(1)} %collective-permute-done.8.refs_2_, s32[512,256]{1,0:T(8,128)S(1)} %get-tuple-element.58.refs_3_, ...), custom_call_target="tpu_custom_call" | custom-call | flops 536870912 | bytes 1048576 | tf_op jit(solution)/shard_map/far/pallas_call | solution.py:678
  28.0 5.5 %all-to-all-start = ((bf16[16,2,32,256]{3,2,1,0:T(8,128)(2,1)}), bf16[16,2,32,256]{3,2,1,0:T(8,128)(2,1)S(1)}, u32[]{:S(2)}, u32[]{:S(2)}) async-start(bf16[16,2,32,256]{3,2,1,0:T(8,128)(2,1)} %get-tuple-element.67), calls=%async_computation | async-start | bytes 1048576 | tf_op jit(solution)/shard_map/all_to_all | solution.py:738
  33.5 4.9 %march.1 = (bf16[3,4,512,256]{3,2,1,0:T(8,128)(2,1)S(1)}, s32[512,256]{1,0:T(8,128)S(1)}) custom-call(f32[8,256]{1,0:T(8,128)S(1)} %get-tuple-element.40.refs_0_.held_ref, bf16[4,256,256]{2,1,0:T(8,128)(2,1)S(1)} %get-tuple-element.59.near_wave, bf16[4,256,256]{2,1,0:T(8,128)(2,1)S(1)} %get-tuple-element.62.far_wave, s32[2,512,256]{2,1,0:T(8,128)} %bracket_hbm.3, ...), custom_call_target="tpu_custom_call" | custom-call | flops 3221225472 | bytes 8388608 | tf_op jit(solution)/shard_map/march/pallas_call | solution.py:700
  38.4 1.2 %near.3.refs_5_ = bf16[8,2,32,256]{3,2,1,0:T(8,128)(2,1)S(1)} custom-call(f32[8,256]{1,0:T(8,128)S(1)} %get-tuple-element.40.refs_0_.held_ref, bf16[3,4,512,256]{3,2,1,0:T(8,128)(2,1)S(1)} %get-tuple-element.63.refs_1_, bf16[4,2,64,256]{3,2,1,0:T(8,128)(2,1)S(1)} %pad_maximum_fusion.refs_2_, s32[512,256]{1,0:T(8,128)S(1)} %get-tuple-element.64.refs_3_, ...), custom_call_target="tpu_custom_call" | custom-call | flops 536870912 | bytes 1048576 | tf_op jit(solution)/shard_map/near/pallas_call | solution.py:678
  39.6 1.2 %far.3 = bf16[2,8,2,32,256]{4,3,2,1,0:T(8,128)(2,1)S(1)} custom-call(f32[8,256]{1,0:T(8,128)S(1)} %get-tuple-element.40.refs_0_.held_ref, bf16[3,4,512,256]{3,2,1,0:T(8,128)(2,1)S(1)} %get-tuple-element.63.refs_1_, bf16[4,2,64,256]{3,2,1,0:T(8,128)(2,1)S(1)} %collective-permute-done.8.refs_2_, s32[512,256]{1,0:T(8,128)S(1)} %get-tuple-element.64.refs_3_, ...), custom_call_target="tpu_custom_call" | custom-call | flops 536870912 | bytes 1048576 | tf_op jit(solution)/shard_map/far/pallas_call | solution.py:678
  41.4 1.2 %collective-permute-done.9 = bf16[8,2,32,256]{3,2,1,0:T(8,128)(2,1)S(1)} collective-permute-done((bf16[8,2,32,256]{3,2,1,0:T(8,128)(2,1)S(1)}, bf16[8,2,32,256]{3,2,1,0:T(8,128)(2,1)S(1)}, u32[]{:S(2)}, u32[]{:S(2)}) %collective-permute-start.9) | collective-permute-done | bytes 262176 | tf_op jit(solution)/shard_map/ppermute | solution.py:585
  42.6 1.9 %collective-permute-start.16 = (bf16[2,2,32,256]{3,2,1,0:T(8,128)(2,1)S(1)}, bf16[2,2,32,256]{3,2,1,0:T(8,128)(2,1)S(1)}, u32[]{:S(2)}, u32[]{:S(2)}) collective-permute-start(bf16[2,2,32,256]{3,2,1,0:T(8,128)(2,1)S(1)} %get-tuple-element.69), channel_id=1, source_target_pairs={{0,2},{1,3},{2,0},{3,1},{4,6},{5,7},{6,4},{7,5},{8,10},{9,11},{10,... | collective-permute-start | bytes 196616 | tf_op jit(solution)/shard_map/ppermute | solution.py:585
  44.5 1.5 %collective-permute-start.10 = (bf16[2,2,32,256]{3,2,1,0:T(8,128)(2,1)S(1)}, bf16[2,2,32,256]{3,2,1,0:T(8,128)(2,1)S(1)}, u32[]{:S(2)}, u32[]{:S(2)}) collective-permute-start(bf16[2,2,32,256]{3,2,1,0:T(8,128)(2,1)S(1)} %get-tuple-element.71), channel_id=1, source_target_pairs={{0,4},{1,5},{2,6},{3,7},{4,0},{5,1},{6,2},{7,3},{8,12},{9,13},{10,... | collective-permute-start | bytes 196616 | tf_op jit(solution)/shard_map/ppermute | solution.py:585
  46.0 2.4 %collective-permute-start.11 = (bf16[2,2,32,256]{3,2,1,0:T(8,128)(2,1)S(1)}, bf16[2,2,32,256]{3,2,1,0:T(8,128)(2,1)S(1)}, u32[]{:S(2)}, u32[]{:S(2)}) collective-permute-start(bf16[2,2,32,256]{3,2,1,0:T(8,128)(2,1)S(1)} %get-tuple-element.72), channel_id=1, source_target_pairs={{0,8},{1,9},{2,10},{3,11},{4,12},{5,13},{6,14},{7,15},{8,0},{9,1},... | collective-permute-start | bytes 196616 | tf_op jit(solution)/shard_map/ppermute | solution.py:585
  48.9 2.4 %collective-permute-start.13 = (bf16[2,2,32,256]{3,2,1,0:T(8,128)(2,1)S(1)}, bf16[2,2,32,256]{3,2,1,0:T(8,128)(2,1)S(1)}, u32[]{:S(2)}, u32[]{:S(2)}) collective-permute-start(bf16[2,2,32,256]{3,2,1,0:T(8,128)(2,1)S(1)} %get-tuple-element.74), channel_id=1, source_target_pairs={{0,12},{1,13},{2,14},{3,15},{4,8},{5,9},{6,10},{7,11},{8,4},{9,5},... | collective-permute-start | bytes 196616 | tf_op jit(solution)/shard_map/ppermute | solution.py:585
  51.3 2.4 %collective-permute-start.14 = (bf16[2,2,32,256]{3,2,1,0:T(8,128)(2,1)S(1)}, bf16[2,2,32,256]{3,2,1,0:T(8,128)(2,1)S(1)}, u32[]{:S(2)}, u32[]{:S(2)}) collective-permute-start(bf16[2,2,32,256]{3,2,1,0:T(8,128)(2,1)S(1)} %get-tuple-element.75), channel_id=1, source_target_pairs={{0,14},{1,15},{2,12},{3,13},{4,10},{5,11},{6,8},{7,9},{8,6},{9,7},... | collective-permute-start | bytes 196616 | tf_op jit(solution)/shard_map/ppermute | solution.py:585
  54.0 3.8 %image.2.refs_9_ = f32[2,32,256,256]{3,2,1,0:T(8,128)} custom-call(bf16[16,2,32,256]{3,2,1,0:T(8,128)(2,1)S(1)} %all-to-all-done.refs_0_, bf16[256,2048]{1,0:T(8,128)(2,1)S(1)} %get-tuple-element.68.refs_1_), custom_call_target="tpu_custom_call" | custom-call | tf_op jit(solution)/shard_map/image/pallas_call | solution.py:768
  58.4 1.1 %collective-permute-done.15.refs_6_ = bf16[2,2,32,256]{3,2,1,0:T(8,128)(2,1)S(1)} collective-permute-done((bf16[2,2,32,256]{3,2,1,0:T(8,128)(2,1)S(1)}, bf16[2,2,32,256]{3,2,1,0:T(8,128)(2,1)S(1)}, u32[]{:S(2)}, u32[]{:S(2)}) %collective-permute-start.15) | collective-permute-done | bytes 65568 | tf_op jit(solution)/shard_map/ppermute | solution.py:585
  59.5 3.8 %image.3 = f32[2,32,256,256]{3,2,1,0:T(8,128)} custom-call(bf16[2,2,32,256]{3,2,1,0:T(8,128)(2,1)S(1)} %get-tuple-element.70.refs_0_, bf16[2,2,32,256]{3,2,1,0:T(8,128)(2,1)S(1)} %collective-permute-done.10.refs_1_, bf16[2,2,32,256]{3,2,1,0:T(8,128)(2,1)S(1)} %collective-permute-done.11.refs_2_, ...), custom_call_target="tpu_custom_call", output_to_operand_aliasing={{}: (9, {})} | custom-call | tf_op jit(solution)/shard_map/image/pallas_call | solution.py:768
  (36 shorter events, 8.1 us)
Async XLA Ops:
  1.2 1.7 %collective-permute-start = (bf16[4,2,64,256]{3,2,1,0:T(8,128)(2,1)S(1)}, bf16[4,2,64,256]{3,2,1,0:T(8,128)(2,1)S(1)}, u32[]{:S(2)}, u32[]{:S(2)}) collective-permute-start(bf16[4,2,64,256]{3,2,1,0:T(8,128)(2,1)S(1)} %get-tuple-element.38), channel_id=1, source_target_pairs={{0,1},{1,0},{2,3},{3,2},{4,5},{5,4},{6,7},{7,6},{8,9},{9,8},{10,11... | collective-permute-start | bytes 786440 | tf_op jit(solution)/shard_map/ppermute | solution.py:585
  3.0 8.3 %collective-permute-start.2 = (bf16[2,64,256]{2,1,0:T(8,128)(2,1)S(1)}, bf16[2,64,256]{2,1,0:T(8,128)(2,1)S(1)}, u32[]{:S(2)}, u32[]{:S(2)}) collective-permute-start(bf16[2,64,256]{2,1,0:T(8,128)(2,1)S(1)} %get-tuple-element.79), channel_id=1, source_target_pairs={{0,4},{1,5},{2,6},{3,7},{4,0},{5,1},{6,2},{7,3},{8,12},{9,13},{10,... | collective-permute-start | bytes 196616 | tf_op jit(solution)/shard_map/ppermute | solution.py:585
  6.0 5.3 %collective-permute-start.3 = (bf16[2,64,256]{2,1,0:T(8,128)(2,1)S(1)}, bf16[2,64,256]{2,1,0:T(8,128)(2,1)S(1)}, u32[]{:S(2)}, u32[]{:S(2)}) collective-permute-start(bf16[2,64,256]{2,1,0:T(8,128)(2,1)S(1)} %get-tuple-element.80), channel_id=1, source_target_pairs={{0,6},{1,7},{2,4},{3,5},{4,2},{5,3},{6,0},{7,1},{8,14},{9,15},{10,... | collective-permute-start | bytes 196616 | tf_op jit(solution)/shard_map/ppermute | solution.py:585
  7.4 4.9 %collective-permute-start.1 = (bf16[2,64,256]{2,1,0:T(8,128)(2,1)S(1)}, bf16[2,64,256]{2,1,0:T(8,128)(2,1)S(1)}, u32[]{:S(2)}, u32[]{:S(2)}) collective-permute-start(bf16[2,64,256]{2,1,0:T(8,128)(2,1)S(1)} %get-tuple-element.81), channel_id=1, source_target_pairs={{0,2},{1,3},{2,0},{3,1},{4,6},{5,7},{6,4},{7,5},{8,10},{9,11},{10,... | collective-permute-start | bytes 196616 | tf_op jit(solution)/shard_map/ppermute | solution.py:585
  12.2 5.6 %collective-permute-start.4 = (bf16[2,64,256]{2,1,0:T(8,128)(2,1)S(1)}, bf16[2,64,256]{2,1,0:T(8,128)(2,1)S(1)}, u32[]{:S(2)}, u32[]{:S(2)}) collective-permute-start(bf16[2,64,256]{2,1,0:T(8,128)(2,1)S(1)} %bitcast_add_fusion), channel_id=1, source_target_pairs={{0,8},{1,9},{2,10},{3,11},{4,12},{5,13},{6,14},{7,15},{8,0},{9,1},... | collective-permute-start | bytes 196616 | tf_op jit(solution)/shard_map/ppermute | solution.py:585
  17.9 5.3 %collective-permute-start.7 = (bf16[2,64,256]{2,1,0:T(8,128)(2,1)S(1)}, bf16[2,64,256]{2,1,0:T(8,128)(2,1)S(1)}, u32[]{:S(2)}, u32[]{:S(2)}) collective-permute-start(bf16[2,64,256]{2,1,0:T(8,128)(2,1)S(1)} %add.41), channel_id=1, source_target_pairs={{0,6},{1,7},{2,4},{3,5},{4,2},{5,3},{6,0},{7,1},{8,14},{9,15},{10,... | collective-permute-start | bytes 196616 | tf_op jit(solution)/shard_map/ppermute | solution.py:585
  20.0 4.3 %collective-permute-start.6 = (bf16[2,64,256]{2,1,0:T(8,128)(2,1)S(1)}, bf16[2,64,256]{2,1,0:T(8,128)(2,1)S(1)}, u32[]{:S(2)}, u32[]{:S(2)}) collective-permute-start(bf16[2,64,256]{2,1,0:T(8,128)(2,1)S(1)} %add.41), channel_id=1, source_target_pairs={{0,4},{1,5},{2,6},{3,7},{4,0},{5,1},{6,2},{7,3},{8,12},{9,13},{10,... | collective-permute-start | bytes 196616 | tf_op jit(solution)/shard_map/ppermute | solution.py:585
  20.4 4.3 %collective-permute-start.5 = (bf16[2,64,256]{2,1,0:T(8,128)(2,1)S(1)}, bf16[2,64,256]{2,1,0:T(8,128)(2,1)S(1)}, u32[]{:S(2)}, u32[]{:S(2)}) collective-permute-start(bf16[2,64,256]{2,1,0:T(8,128)(2,1)S(1)} %add.41), channel_id=1, source_target_pairs={{0,2},{1,3},{2,0},{3,1},{4,6},{5,7},{6,4},{7,5},{8,10},{9,11},{10,... | collective-permute-start | bytes 196616 | tf_op jit(solution)/shard_map/ppermute | solution.py:585
  24.7 1.6 %collective-permute-start.8 = (bf16[4,2,64,256]{3,2,1,0:T(8,128)(2,1)S(1)}, bf16[4,2,64,256]{3,2,1,0:T(8,128)(2,1)S(1)}, u32[]{:S(2)}, u32[]{:S(2)}) collective-permute-start(bf16[4,2,64,256]{3,2,1,0:T(8,128)(2,1)S(1)} %pad_maximum_fusion.refs_2_), channel_id=1, source_target_pairs={{0,1},{1,0},{2,3},{3,2},{4,5},{5,4},{6,7},{7,6},{8,9},{9,8},{10,11... | collective-permute-start | bytes 786440 | tf_op jit(solution)/shard_map/ppermute | solution.py:585
  28.0 26.1 %all-to-all-start = ((bf16[16,2,32,256]{3,2,1,0:T(8,128)(2,1)}), bf16[16,2,32,256]{3,2,1,0:T(8,128)(2,1)S(1)}, u32[]{:S(2)}, u32[]{:S(2)}) async-start(bf16[16,2,32,256]{3,2,1,0:T(8,128)(2,1)} %get-tuple-element.67), calls=%async_computation | async-start | bytes 1048576 | tf_op jit(solution)/shard_map/all_to_all | solution.py:738
  40.9 1.6 %collective-permute-start.9 = (bf16[8,2,32,256]{3,2,1,0:T(8,128)(2,1)S(1)}, bf16[8,2,32,256]{3,2,1,0:T(8,128)(2,1)S(1)}, u32[]{:S(2)}, u32[]{:S(2)}) collective-permute-start(bf16[8,2,32,256]{3,2,1,0:T(8,128)(2,1)S(1)} %get-tuple-element.78), channel_id=1, source_target_pairs={{0,1},{1,0},{2,3},{3,2},{4,5},{5,4},{6,7},{7,6},{8,9},{9,8},{10,11... | collective-permute-start | bytes 786440 | tf_op jit(solution)/shard_map/ppermute | solution.py:585
  42.6 8.7 %collective-permute-start.16 = (bf16[2,2,32,256]{3,2,1,0:T(8,128)(2,1)S(1)}, bf16[2,2,32,256]{3,2,1,0:T(8,128)(2,1)S(1)}, u32[]{:S(2)}, u32[]{:S(2)}) collective-permute-start(bf16[2,2,32,256]{3,2,1,0:T(8,128)(2,1)S(1)} %get-tuple-element.69), channel_id=1, source_target_pairs={{0,2},{1,3},{2,0},{3,1},{4,6},{5,7},{6,4},{7,5},{8,10},{9,11},{10,... | collective-permute-start | bytes 196616 | tf_op jit(solution)/shard_map/ppermute | solution.py:585
  44.5 9.1 %collective-permute-start.10 = (bf16[2,2,32,256]{3,2,1,0:T(8,128)(2,1)S(1)}, bf16[2,2,32,256]{3,2,1,0:T(8,128)(2,1)S(1)}, u32[]{:S(2)}, u32[]{:S(2)}) collective-permute-start(bf16[2,2,32,256]{3,2,1,0:T(8,128)(2,1)S(1)} %get-tuple-element.71), channel_id=1, source_target_pairs={{0,4},{1,5},{2,6},{3,7},{4,0},{5,1},{6,2},{7,3},{8,12},{9,13},{10,... | collective-permute-start | bytes 196616 | tf_op jit(solution)/shard_map/ppermute | solution.py:585
  46.0 11.9 %collective-permute-start.11 = (bf16[2,2,32,256]{3,2,1,0:T(8,128)(2,1)S(1)}, bf16[2,2,32,256]{3,2,1,0:T(8,128)(2,1)S(1)}, u32[]{:S(2)}, u32[]{:S(2)}) collective-permute-start(bf16[2,2,32,256]{3,2,1,0:T(8,128)(2,1)S(1)} %get-tuple-element.72), channel_id=1, source_target_pairs={{0,8},{1,9},{2,10},{3,11},{4,12},{5,13},{6,14},{7,15},{8,0},{9,1},... | collective-permute-start | bytes 196616 | tf_op jit(solution)/shard_map/ppermute | solution.py:585
  48.4 10.0 %collective-permute-start.12 = (bf16[2,2,32,256]{3,2,1,0:T(8,128)(2,1)S(1)}, bf16[2,2,32,256]{3,2,1,0:T(8,128)(2,1)S(1)}, u32[]{:S(2)}, u32[]{:S(2)}) collective-permute-start(bf16[2,2,32,256]{3,2,1,0:T(8,128)(2,1)S(1)} %get-tuple-element.73), channel_id=1, source_target_pairs={{0,10},{1,11},{2,8},{3,9},{4,14},{5,15},{6,12},{7,13},{8,2},{9,3},... | collective-permute-start | bytes 196616 | tf_op jit(solution)/shard_map/ppermute | solution.py:585
  48.9 9.5 %collective-permute-start.13 = (bf16[2,2,32,256]{3,2,1,0:T(8,128)(2,1)S(1)}, bf16[2,2,32,256]{3,2,1,0:T(8,128)(2,1)S(1)}, u32[]{:S(2)}, u32[]{:S(2)}) collective-permute-start(bf16[2,2,32,256]{3,2,1,0:T(8,128)(2,1)S(1)} %get-tuple-element.74), channel_id=1, source_target_pairs={{0,12},{1,13},{2,14},{3,15},{4,8},{5,9},{6,10},{7,11},{8,4},{9,5},... | collective-permute-start | bytes 196616 | tf_op jit(solution)/shard_map/ppermute | solution.py:585
  51.3 7.1 %collective-permute-start.14 = (bf16[2,2,32,256]{3,2,1,0:T(8,128)(2,1)S(1)}, bf16[2,2,32,256]{3,2,1,0:T(8,128)(2,1)S(1)}, u32[]{:S(2)}, u32[]{:S(2)}) collective-permute-start(bf16[2,2,32,256]{3,2,1,0:T(8,128)(2,1)S(1)} %get-tuple-element.75), channel_id=1, source_target_pairs={{0,14},{1,15},{2,12},{3,13},{4,10},{5,11},{6,8},{7,9},{8,6},{9,7},... | collective-permute-start | bytes 196616 | tf_op jit(solution)/shard_map/ppermute | solution.py:585
  53.6 5.8 %collective-permute-start.15 = (bf16[2,2,32,256]{3,2,1,0:T(8,128)(2,1)S(1)}, bf16[2,2,32,256]{3,2,1,0:T(8,128)(2,1)S(1)}, u32[]{:S(2)}, u32[]{:S(2)}) collective-permute-start(bf16[2,2,32,256]{3,2,1,0:T(8,128)(2,1)S(1)} %get-tuple-element.76), channel_id=1, source_target_pairs={{0,6},{1,7},{2,4},{3,5},{4,2},{5,3},{6,0},{7,1},{8,14},{9,15},{10,... | collective-permute-start | bytes 196616 | tf_op jit(solution)/shard_map/ppermute | solution.py:585

commit v7 on v6

--- a/solution.py
+++ b/solution.py
@@ -433,6 +433,31 @@
     )
 
 
+def pair_mix_kernel(
+    held_ref, returned_ref, near_slow, far_slow, bracket_ref, inverse_y, cross_ref, even, odd, *, depth
+):
+    piece = near_slow.shape[2]
+    tile = cross_ref.shape[-2]
+    for slow_ref, starts in zip((near_slow, far_slow), piece_starts(piece)):
+
+        def put_cross(block, side, values, starts=starts):
+            for part in range(piece // tile):
+                place = place_of(starts[block] // tile + part)
+                cross_ref[*place, side] = values[part * tile : (part + 1) * tile]
+
+        blend(
+            returned_ref,
+            slow_ref.at[:, depth],
+            bracket_ref,
+            inverse_y,
+            scalars_of(held_ref, depth),
+            (even, odd),
+            None,
+            put_cross,
+            starts,
+        )
+
+
 def march_kernel(
     held_ref,
     near_wave,
@@ -483,7 +508,7 @@
 
 
 IMAGE_ROWS = 8
-PAIR_ORDER = (2, 4, 5, 6, 7, 3, 1)
+PAIR_ORDER = (3, 4, 5, 6, 7, 2, 1)
 
 
 def lag_kernel(lag_ref, *weight_refs):
@@ -725,12 +750,26 @@
             pin(forward_y),
             pin(inverse_x),
         )
-        *near_wave, near_cross = mix(
-            depth, False, held_scalars, returned, near_slow, bracket, kept_inverse
-        )
-        *far_wave, cross = mix(
-            depth, True, held_scalars, returned, far_slow, bracket, kept_inverse, near_cross
-        )
+        if paired and depth == depths - 1:
+            cross = pl.pallas_call(
+                functools.partial(pair_mix_kernel, depth=depth),
+                in_specs=[vmem] * 6,
+                out_specs=vmem,
+                out_shape=jax.ShapeDtypeStruct((2, ranks // 2, 2, tile, cols), bf16),
+                scratch_shapes=blend_scratch,
+                compiler_params=pltpu.CompilerParams(vmem_limit_bytes=16 << 20),
+                cost_estimate=pl.CostEstimate(
+                    flops=flops // 2, bytes_accessed=1 << 20, transcendentals=0
+                ),
+                name="mix",
+            )(held_scalars, returned, near_slow, far_slow, bracket, kept_inverse)
+        else:
+            *near_wave, near_cross = mix(
+                depth, False, held_scalars, returned, near_slow, bracket, kept_inverse
+            )
+            *far_wave, cross = mix(
+                depth, True, held_scalars, returned, far_slow, bracket, kept_inverse, near_cross
+            )
         crosses.append(cross)
 
     scale = bins ** (-0.5)

time: 63.7 us -> 63.4 us (level)
    pallas_call x4 -> x2, Pallas kernels: 4.93 us -> 2.49 us  [mix(): pl.pallas_call(functools.partial(mix_kernel, depth=depth, far=far, last=l...]
    pallas_call x0 -> x1, Pallas kernels: none -> 2.27 us  [shards(): pl.pallas_call(functools.partial(pair_mix_kernel, depth=depth), in_specs=...]
  transfers between devices with their start and end apart: 18 -> 18, of which waited for: 9 -> 10; matrix products, arithmetic and copies ran while one was open for 2% -> 2% of each run, Pallas kernels for 32% -> 32%
where the time goes in v7:
time: 63.4 us; the launch traced here: 63.2 us
  starting transfers between devices  28.6 us (45%)
  Pallas kernels  26.6 us (42%)
  waiting for transfers between devices  6.19 us (10%)
  other arithmetic  1.46 us (2%)
    ppermute x17, starting transfers between devices, swap(): return lax.ppermute(value, 'freq', [(i, i ^ bit) for i in range(ranks)])  23 us
    pallas_call x2, Pallas kernels, shards(): pl.pallas_call(functools.partial(image_kernel, scale=scale, depth=depth,...  7.63 us
    ppermute x17, waiting for transfers between devices, swap(): return lax.ppermute(value, 'freq', [(i, i ^ bit) for i in range(ranks)])  6.19 us
    all_to_all x1, starting transfers between devices, exchange(): lax.all_to_all(value, 'freq', split_axis=0, concat_axis=0, tiled=True)  5.59 us
    pallas_call x1, Pallas kernels, shards(): pl.pallas_call(functools.partial(march_kernel, depth=depth), in_specs=[vm...  4.93 us
    pallas_call x1, Pallas kernels, shards(): pl.pallas_call(out_kernel, in_specs=[hbm] * 6, out_specs=[vmem] * 4, out_...  3.74 us
    pallas_call x1, Pallas kernels, shards(): pl.pallas_call(back_kernel, in_specs=[vmem] * 3 + [hbm] * 3, out_specs=[v...  2.98 us
    pallas_call x2, Pallas kernels, mix(): pl.pallas_call(functools.partial(mix_kernel, depth=depth, far=far, last=l...  2.49 us
  transfers between devices with their start and end apart: 18, of which 10 were waited for; matrix products, arithmetic and copies ran while one was open for 2% of the time, Pallas kernels for 32%

profile of v7, /device:TPU:0, one launch (start us, length us, event | category | flops | bytes accessed | tf_op | source)
XLA Modules:
  0.0 63.2 jit_solution(1757646482323982543)
XLA Ops:
  0.0 1.2 %window.1 = (bf16[4,2,64,256]{3,2,1,0:T(8,128)(2,1)S(1)}, bf16[4,2,64,256]{3,2,1,0:T(8,128)(2,1)S(1)}) custom-call(s32[2]{0:T(128)} %map_hbm.1, s32[2]{0:T(128)} %corner_hbm.1, bf16[1,768,512]{2,1,0:T(8,128)(2,1)} %slab_hbm.1), custom_call_target="tpu_custom_call" | custom-call | tf_op jit(solution)/shard_map/window/pallas_call | solution.py:594
  3.0 3.0 %collective-permute-start.2 = (bf16[2,64,256]{2,1,0:T(8,128)(2,1)S(1)}, bf16[2,64,256]{2,1,0:T(8,128)(2,1)S(1)}, u32[]{:S(2)}, u32[]{:S(2)}) collective-permute-start(bf16[2,64,256]{2,1,0:T(8,128)(2,1)S(1)} %get-tuple-element.79), channel_id=1, source_target_pairs={{0,4},{1,5},{2,6},{3,7},{4,0},{5,1},{6,2},{7,3},{8,12},{9,13},{10,... | collective-permute-start | bytes 196616 | tf_op jit(solution)/shard_map/ppermute | solution.py:610
  6.0 1.4 %collective-permute-start.3 = (bf16[2,64,256]{2,1,0:T(8,128)(2,1)S(1)}, bf16[2,64,256]{2,1,0:T(8,128)(2,1)S(1)}, u32[]{:S(2)}, u32[]{:S(2)}) collective-permute-start(bf16[2,64,256]{2,1,0:T(8,128)(2,1)S(1)} %get-tuple-element.80), channel_id=1, source_target_pairs={{0,6},{1,7},{2,4},{3,5},{4,2},{5,3},{6,0},{7,1},{8,14},{9,15},{10,... | collective-permute-start | bytes 196616 | tf_op jit(solution)/shard_map/ppermute | solution.py:610
  7.5 3.7 %out.1 = (f32[4,512,256]{2,1,0:T(8,128)S(1)}, f32[3,512,256]{2,1,0:T(8,128)S(1)}, f32[3,512,256]{2,1,0:T(8,128)S(1)}, f32[8,256]{1,0:T(8,128)S(1)}) custom-call(s32[16]{0:T(128)} %bins_hbm, f32[2,3]{1,0:T(2,128)} %gaps_hbm.1, bf16[2,1,512,256]{3,2,1,0:T(8,128)(2,1)} %source_hbm.1, bf16[2,1,512,256]{3,2,1,0:T(8,128)(2,1)} %receiver_hbm.1, ...), custom_call_target="tpu_custom_call" | custom-call | flops 1073741824 | bytes 4194304 | tf_op jit(solution)/shard_map/out/pallas_call | solution.py:621
  11.3 0.9 %collective-permute-done.1 = bf16[2,64,256]{2,1,0:T(8,128)(2,1)S(1)} collective-permute-done((bf16[2,64,256]{2,1,0:T(8,128)(2,1)S(1)}, bf16[2,64,256]{2,1,0:T(8,128)(2,1)S(1)}, u32[]{:S(2)}, u32[]{:S(2)}) %collective-permute-start.1) | collective-permute-done | bytes 65568 | tf_op jit(solution)/shard_map/ppermute | solution.py:610
  12.2 2.8 %collective-permute-start.4 = (bf16[2,64,256]{2,1,0:T(8,128)(2,1)S(1)}, bf16[2,64,256]{2,1,0:T(8,128)(2,1)S(1)}, u32[]{:S(2)}, u32[]{:S(2)}) collective-permute-start(bf16[2,64,256]{2,1,0:T(8,128)(2,1)S(1)} %bitcast_add_fusion), channel_id=1, source_target_pairs={{0,8},{1,9},{2,10},{3,11},{4,12},{5,13},{6,14},{7,15},{8,0},{9,1},... | collective-permute-start | bytes 196616 | tf_op jit(solution)/shard_map/ppermute | solution.py:610
  15.0 3.0 %back.1 = (bf16[3,4,512,256]{3,2,1,0:T(8,128)(2,1)S(1)}, s32[512,256]{1,0:T(8,128)S(1)}, bf16[256,256]{1,0:T(8,128)(2,1)S(1)}) custom-call(f32[4,512,256]{2,1,0:T(8,128)S(1)} %get-tuple-element.46.spec_ref, f32[3,512,256]{2,1,0:T(8,128)S(1)} %get-tuple-element.47.cos_ref, f32[3,512,256]{2,1,0:T(8,128)S(1)} %get-tuple-element.48.sin_ref, ...), custom_call_target="tpu_custom_call" | custom-call | flops 2147483648 | bytes 4194304 | tf_op jit(solution)/shard_map/back/pallas_call | solution.py:654
  18.3 1.7 %collective-permute-start.7 = (bf16[2,64,256]{2,1,0:T(8,128)(2,1)S(1)}, bf16[2,64,256]{2,1,0:T(8,128)(2,1)S(1)}, u32[]{:S(2)}, u32[]{:S(2)}) collective-permute-start(bf16[2,64,256]{2,1,0:T(8,128)(2,1)S(1)} %add.41), channel_id=1, source_target_pairs={{0,6},{1,7},{2,4},{3,5},{4,2},{5,3},{6,0},{7,1},{8,14},{9,15},{10,... | collective-permute-start | bytes 196616 | tf_op jit(solution)/shard_map/ppermute | solution.py:610
  20.4 1.5 %collective-permute-start.5 = (bf16[2,64,256]{2,1,0:T(8,128)(2,1)S(1)}, bf16[2,64,256]{2,1,0:T(8,128)(2,1)S(1)}, u32[]{:S(2)}, u32[]{:S(2)}) collective-permute-start(bf16[2,64,256]{2,1,0:T(8,128)(2,1)S(1)} %add.41), channel_id=1, source_target_pairs={{0,2},{1,3},{2,0},{3,1},{4,6},{5,7},{6,4},{7,5},{8,10},{9,11},{10,... | collective-permute-start | bytes 196616 | tf_op jit(solution)/shard_map/ppermute | solution.py:610
  21.9 1.0 %unfold.1.refs_1_ = f32[12,512,256]{2,1,0:T(8,128)S(1)} custom-call(bf16[3,4,512,256]{3,2,1,0:T(8,128)(2,1)S(1)} %get-tuple-element.51.returned_ref, bf16[256,256]{1,0:T(8,128)(2,1)S(1)} %get-tuple-element.52.inverse_y), custom_call_target="tpu_custom_call" | custom-call | flops 1073741824 | bytes 1048576 | tf_op jit(solution)/shard_map/unfold/pallas_call | solution.py:678
  26.3 1.6 %far.1 = (bf16[4,256,256]{2,1,0:T(8,128)(2,1)S(1)}, bf16[16,2,32,256]{3,2,1,0:T(8,128)(2,1)}) custom-call(f32[8,256]{1,0:T(8,128)S(1)} %get-tuple-element.40.refs_0_.held_ref, f32[12,512,256]{2,1,0:T(8,128)S(1)} %unfold.1.refs_1_, bf16[4,2,64,256]{3,2,1,0:T(8,128)(2,1)S(1)} %collective-permute-done.8.refs_2_.far_slow, ...), custom_call_target="tpu_custom_call" | custom-call | flops 536870912 | bytes 1048576 | tf_op jit(solution)/shard_map/far/pallas_call | solution.py:703
  28.0 5.6 %all-to-all-start = ((bf16[16,2,32,256]{3,2,1,0:T(8,128)(2,1)}), bf16[16,2,32,256]{3,2,1,0:T(8,128)(2,1)S(1)}, u32[]{:S(2)}, u32[]{:S(2)}) async-start(bf16[16,2,32,256]{3,2,1,0:T(8,128)(2,1)} %get-tuple-element.67), calls=%async_computation | async-start | bytes 1048576 | tf_op jit(solution)/shard_map/all_to_all | solution.py:777
  33.6 4.9 %march.1 = (bf16[3,4,512,256]{3,2,1,0:T(8,128)(2,1)S(1)}, s32[512,256]{1,0:T(8,128)S(1)}) custom-call(f32[8,256]{1,0:T(8,128)S(1)} %get-tuple-element.40.refs_0_.held_ref, bf16[4,256,256]{2,1,0:T(8,128)(2,1)S(1)} %get-tuple-element.59.near_wave, bf16[4,256,256]{2,1,0:T(8,128)(2,1)S(1)} %get-tuple-element.62.far_wave, s32[2,512,256]{2,1,0:T(8,128)} %bracket_hbm.3, ...), custom_call_target="tpu_custom_call" | custom-call | flops 3221225472 | bytes 8388608 | tf_op jit(solution)/shard_map/march/pallas_call | solution.py:725
  38.5 2.3 %mix.1 = bf16[2,8,2,32,256]{4,3,2,1,0:T(8,128)(2,1)S(1)} custom-call(f32[8,256]{1,0:T(8,128)S(1)} %get-tuple-element.40.refs_0_.held_ref, bf16[3,4,512,256]{3,2,1,0:T(8,128)(2,1)S(1)} %get-tuple-element.63.returned_ref, bf16[4,2,64,256]{3,2,1,0:T(8,128)(2,1)S(1)} %pad_maximum_fusion.refs_2_.near_slow, ...), custom_call_target="tpu_custom_call" | custom-call | flops 1073741824 | bytes 1048576 | tf_op jit(solution)/shard_map/mix/pallas_call | solution.py:754
  41.3 1.2 %collective-permute-done.9 = bf16[8,2,32,256]{3,2,1,0:T(8,128)(2,1)S(1)} collective-permute-done((bf16[8,2,32,256]{3,2,1,0:T(8,128)(2,1)S(1)}, bf16[8,2,32,256]{3,2,1,0:T(8,128)(2,1)S(1)}, u32[]{:S(2)}, u32[]{:S(2)}) %collective-permute-start.9) | collective-permute-done | bytes 262176 | tf_op jit(solution)/shard_map/ppermute | solution.py:610
  42.5 2.0 %collective-permute-start.16 = (bf16[2,2,32,256]{3,2,1,0:T(8,128)(2,1)S(1)}, bf16[2,2,32,256]{3,2,1,0:T(8,128)(2,1)S(1)}, u32[]{:S(2)}, u32[]{:S(2)}) collective-permute-start(bf16[2,2,32,256]{3,2,1,0:T(8,128)(2,1)S(1)} %get-tuple-element.69), channel_id=1, source_target_pairs={{0,2},{1,3},{2,0},{3,1},{4,6},{5,7},{6,4},{7,5},{8,10},{9,11},{10,... | collective-permute-start | bytes 196616 | tf_op jit(solution)/shard_map/ppermute | solution.py:610
  44.4 1.5 %collective-permute-start.10 = (bf16[2,2,32,256]{3,2,1,0:T(8,128)(2,1)S(1)}, bf16[2,2,32,256]{3,2,1,0:T(8,128)(2,1)S(1)}, u32[]{:S(2)}, u32[]{:S(2)}) collective-permute-start(bf16[2,2,32,256]{3,2,1,0:T(8,128)(2,1)S(1)} %get-tuple-element.71), channel_id=1, source_target_pairs={{0,6},{1,7},{2,4},{3,5},{4,2},{5,3},{6,0},{7,1},{8,14},{9,15},{10,... | collective-permute-start | bytes 196616 | tf_op jit(solution)/shard_map/ppermute | solution.py:610
  45.9 2.4 %collective-permute-start.11 = (bf16[2,2,32,256]{3,2,1,0:T(8,128)(2,1)S(1)}, bf16[2,2,32,256]{3,2,1,0:T(8,128)(2,1)S(1)}, u32[]{:S(2)}, u32[]{:S(2)}) collective-permute-start(bf16[2,2,32,256]{3,2,1,0:T(8,128)(2,1)S(1)} %get-tuple-element.72), channel_id=1, source_target_pairs={{0,8},{1,9},{2,10},{3,11},{4,12},{5,13},{6,14},{7,15},{8,0},{9,1},... | collective-permute-start | bytes 196616 | tf_op jit(solution)/shard_map/ppermute | solution.py:610
  48.3 1.5 %collective-permute-start.12 = (bf16[2,2,32,256]{3,2,1,0:T(8,128)(2,1)S(1)}, bf16[2,2,32,256]{3,2,1,0:T(8,128)(2,1)S(1)}, u32[]{:S(2)}, u32[]{:S(2)}) collective-permute-start(bf16[2,2,32,256]{3,2,1,0:T(8,128)(2,1)S(1)} %get-tuple-element.73), channel_id=1, source_target_pairs={{0,10},{1,11},{2,8},{3,9},{4,14},{5,15},{6,12},{7,13},{8,2},{9,3},... | collective-permute-start | bytes 196616 | tf_op jit(solution)/shard_map/ppermute | solution.py:610
  49.7 2.4 %collective-permute-start.13 = (bf16[2,2,32,256]{3,2,1,0:T(8,128)(2,1)S(1)}, bf16[2,2,32,256]{3,2,1,0:T(8,128)(2,1)S(1)}, u32[]{:S(2)}, u32[]{:S(2)}) collective-permute-start(bf16[2,2,32,256]{3,2,1,0:T(8,128)(2,1)S(1)} %get-tuple-element.74), channel_id=1, source_target_pairs={{0,12},{1,13},{2,14},{3,15},{4,8},{5,9},{6,10},{7,11},{8,4},{9,5},... | collective-permute-start | bytes 196616 | tf_op jit(solution)/shard_map/ppermute | solution.py:610
  52.1 1.5 %collective-permute-start.14 = (bf16[2,2,32,256]{3,2,1,0:T(8,128)(2,1)S(1)}, bf16[2,2,32,256]{3,2,1,0:T(8,128)(2,1)S(1)}, u32[]{:S(2)}, u32[]{:S(2)}) collective-permute-start(bf16[2,2,32,256]{3,2,1,0:T(8,128)(2,1)S(1)} %get-tuple-element.75), channel_id=1, source_target_pairs={{0,14},{1,15},{2,12},{3,13},{4,10},{5,11},{6,8},{7,9},{8,6},{9,7},... | collective-permute-start | bytes 196616 | tf_op jit(solution)/shard_map/ppermute | solution.py:610
  53.9 3.8 %image.2.refs_9_ = f32[2,32,256,256]{3,2,1,0:T(8,128)} custom-call(bf16[16,2,32,256]{3,2,1,0:T(8,128)(2,1)S(1)} %all-to-all-done.refs_0_, bf16[256,2048]{1,0:T(8,128)(2,1)S(1)} %get-tuple-element.68.refs_1_), custom_call_target="tpu_custom_call" | custom-call | tf_op jit(solution)/shard_map/image/pallas_call | solution.py:807
  58.0 1.2 %collective-permute-done.14.refs_5_ = bf16[2,2,32,256]{3,2,1,0:T(8,128)(2,1)S(1)} collective-permute-done((bf16[2,2,32,256]{3,2,1,0:T(8,128)(2,1)S(1)}, bf16[2,2,32,256]{3,2,1,0:T(8,128)(2,1)S(1)}, u32[]{:S(2)}, u32[]{:S(2)}) %collective-permute-start.14) | collective-permute-done | bytes 65568 | tf_op jit(solution)/shard_map/ppermute | solution.py:610
  59.2 3.8 %image.3 = f32[2,32,256,256]{3,2,1,0:T(8,128)} custom-call(bf16[2,2,32,256]{3,2,1,0:T(8,128)(2,1)S(1)} %get-tuple-element.70.refs_0_, bf16[2,2,32,256]{3,2,1,0:T(8,128)(2,1)S(1)} %collective-permute-done.10.refs_1_, bf16[2,2,32,256]{3,2,1,0:T(8,128)(2,1)S(1)} %collective-permute-done.11.refs_2_, ...), custom_call_target="tpu_custom_call", output_to_operand_aliasing={{}: (9, {})} | custom-call | tf_op jit(solution)/shard_map/image/pallas_call | solution.py:807
  (35 shorter events, 7.2 us)
Async XLA Ops:
  1.2 1.7 %collective-permute-start = (bf16[4,2,64,256]{3,2,1,0:T(8,128)(2,1)S(1)}, bf16[4,2,64,256]{3,2,1,0:T(8,128)(2,1)S(1)}, u32[]{:S(2)}, u32[]{:S(2)}) collective-permute-start(bf16[4,2,64,256]{3,2,1,0:T(8,128)(2,1)S(1)} %get-tuple-element.38), channel_id=1, source_target_pairs={{0,1},{1,0},{2,3},{3,2},{4,5},{5,4},{6,7},{7,6},{8,9},{9,8},{10,11... | collective-permute-start | bytes 786440 | tf_op jit(solution)/shard_map/ppermute | solution.py:610
  3.0 8.3 %collective-permute-start.2 = (bf16[2,64,256]{2,1,0:T(8,128)(2,1)S(1)}, bf16[2,64,256]{2,1,0:T(8,128)(2,1)S(1)}, u32[]{:S(2)}, u32[]{:S(2)}) collective-permute-start(bf16[2,64,256]{2,1,0:T(8,128)(2,1)S(1)} %get-tuple-element.79), channel_id=1, source_target_pairs={{0,4},{1,5},{2,6},{3,7},{4,0},{5,1},{6,2},{7,3},{8,12},{9,13},{10,... | collective-permute-start | bytes 196616 | tf_op jit(solution)/shard_map/ppermute | solution.py:610
  6.0 5.3 %collective-permute-start.3 = (bf16[2,64,256]{2,1,0:T(8,128)(2,1)S(1)}, bf16[2,64,256]{2,1,0:T(8,128)(2,1)S(1)}, u32[]{:S(2)}, u32[]{:S(2)}) collective-permute-start(bf16[2,64,256]{2,1,0:T(8,128)(2,1)S(1)} %get-tuple-element.80), channel_id=1, source_target_pairs={{0,6},{1,7},{2,4},{3,5},{4,2},{5,3},{6,0},{7,1},{8,14},{9,15},{10,... | collective-permute-start | bytes 196616 | tf_op jit(solution)/shard_map/ppermute | solution.py:610
  7.4 4.9 %collective-permute-start.1 = (bf16[2,64,256]{2,1,0:T(8,128)(2,1)S(1)}, bf16[2,64,256]{2,1,0:T(8,128)(2,1)S(1)}, u32[]{:S(2)}, u32[]{:S(2)}) collective-permute-start(bf16[2,64,256]{2,1,0:T(8,128)(2,1)S(1)} %get-tuple-element.81), channel_id=1, source_target_pairs={{0,2},{1,3},{2,0},{3,1},{4,6},{5,7},{6,4},{7,5},{8,10},{9,11},{10,... | collective-permute-start | bytes 196616 | tf_op jit(solution)/shard_map/ppermute | solution.py:610
  12.2 6.0 %collective-permute-start.4 = (bf16[2,64,256]{2,1,0:T(8,128)(2,1)S(1)}, bf16[2,64,256]{2,1,0:T(8,128)(2,1)S(1)}, u32[]{:S(2)}, u32[]{:S(2)}) collective-permute-start(bf16[2,64,256]{2,1,0:T(8,128)(2,1)S(1)} %bitcast_add_fusion), channel_id=1, source_target_pairs={{0,8},{1,9},{2,10},{3,11},{4,12},{5,13},{6,14},{7,15},{8,0},{9,1},... | collective-permute-start | bytes 196616 | tf_op jit(solution)/shard_map/ppermute | solution.py:610
  18.3 5.2 %collective-permute-start.7 = (bf16[2,64,256]{2,1,0:T(8,128)(2,1)S(1)}, bf16[2,64,256]{2,1,0:T(8,128)(2,1)S(1)}, u32[]{:S(2)}, u32[]{:S(2)}) collective-permute-start(bf16[2,64,256]{2,1,0:T(8,128)(2,1)S(1)} %add.41), channel_id=1, source_target_pairs={{0,6},{1,7},{2,4},{3,5},{4,2},{5,3},{6,0},{7,1},{8,14},{9,15},{10,... | collective-permute-start | bytes 196616 | tf_op jit(solution)/shard_map/ppermute | solution.py:610
  20.0 4.3 %collective-permute-start.6 = (bf16[2,64,256]{2,1,0:T(8,128)(2,1)S(1)}, bf16[2,64,256]{2,1,0:T(8,128)(2,1)S(1)}, u32[]{:S(2)}, u32[]{:S(2)}) collective-permute-start(bf16[2,64,256]{2,1,0:T(8,128)(2,1)S(1)} %add.41), channel_id=1, source_target_pairs={{0,4},{1,5},{2,6},{3,7},{4,0},{5,1},{6,2},{7,3},{8,12},{9,13},{10,... | collective-permute-start | bytes 196616 | tf_op jit(solution)/shard_map/ppermute | solution.py:610
  20.4 4.3 %collective-permute-start.5 = (bf16[2,64,256]{2,1,0:T(8,128)(2,1)S(1)}, bf16[2,64,256]{2,1,0:T(8,128)(2,1)S(1)}, u32[]{:S(2)}, u32[]{:S(2)}) collective-permute-start(bf16[2,64,256]{2,1,0:T(8,128)(2,1)S(1)} %add.41), channel_id=1, source_target_pairs={{0,2},{1,3},{2,0},{3,1},{4,6},{5,7},{6,4},{7,5},{8,10},{9,11},{10,... | collective-permute-start | bytes 196616 | tf_op jit(solution)/shard_map/ppermute | solution.py:610
  24.7 1.6 %collective-permute-start.8 = (bf16[4,2,64,256]{3,2,1,0:T(8,128)(2,1)S(1)}, bf16[4,2,64,256]{3,2,1,0:T(8,128)(2,1)S(1)}, u32[]{:S(2)}, u32[]{:S(2)}) collective-permute-start(bf16[4,2,64,256]{3,2,1,0:T(8,128)(2,1)S(1)} %pad_maximum_fusion.refs_2_.near_slow), channel_id=1, source_target_pairs={{0,1},{1,0},{2,3},{3,2},{4,5},{5,4},{6,7},{7,6},{8,9},{9,8},{10,11... | collective-permute-start | bytes 786440 | tf_op jit(solution)/shard_map/ppermute | solution.py:610
  28.0 26.0 %all-to-all-start = ((bf16[16,2,32,256]{3,2,1,0:T(8,128)(2,1)}), bf16[16,2,32,256]{3,2,1,0:T(8,128)(2,1)S(1)}, u32[]{:S(2)}, u32[]{:S(2)}) async-start(bf16[16,2,32,256]{3,2,1,0:T(8,128)(2,1)} %get-tuple-element.67), calls=%async_computation | async-start | bytes 1048576 | tf_op jit(solution)/shard_map/all_to_all | solution.py:777
  40.8 1.6 %collective-permute-start.9 = (bf16[8,2,32,256]{3,2,1,0:T(8,128)(2,1)S(1)}, bf16[8,2,32,256]{3,2,1,0:T(8,128)(2,1)S(1)}, u32[]{:S(2)}, u32[]{:S(2)}) collective-permute-start(bf16[8,2,32,256]{3,2,1,0:T(8,128)(2,1)S(1)} %get-tuple-element.78), channel_id=1, source_target_pairs={{0,1},{1,0},{2,3},{3,2},{4,5},{5,4},{6,7},{7,6},{8,9},{9,8},{10,11... | collective-permute-start | bytes 786440 | tf_op jit(solution)/shard_map/ppermute | solution.py:610
  42.5 9.6 %collective-permute-start.16 = (bf16[2,2,32,256]{3,2,1,0:T(8,128)(2,1)S(1)}, bf16[2,2,32,256]{3,2,1,0:T(8,128)(2,1)S(1)}, u32[]{:S(2)}, u32[]{:S(2)}) collective-permute-start(bf16[2,2,32,256]{3,2,1,0:T(8,128)(2,1)S(1)} %get-tuple-element.69), channel_id=1, source_target_pairs={{0,2},{1,3},{2,0},{3,1},{4,6},{5,7},{6,4},{7,5},{8,10},{9,11},{10,... | collective-permute-start | bytes 196616 | tf_op jit(solution)/shard_map/ppermute | solution.py:610
  44.4 9.1 %collective-permute-start.10 = (bf16[2,2,32,256]{3,2,1,0:T(8,128)(2,1)S(1)}, bf16[2,2,32,256]{3,2,1,0:T(8,128)(2,1)S(1)}, u32[]{:S(2)}, u32[]{:S(2)}) collective-permute-start(bf16[2,2,32,256]{3,2,1,0:T(8,128)(2,1)S(1)} %get-tuple-element.71), channel_id=1, source_target_pairs={{0,6},{1,7},{2,4},{3,5},{4,2},{5,3},{6,0},{7,1},{8,14},{9,15},{10,... | collective-permute-start | bytes 196616 | tf_op jit(solution)/shard_map/ppermute | solution.py:610
  45.9 11.9 %collective-permute-start.11 = (bf16[2,2,32,256]{3,2,1,0:T(8,128)(2,1)S(1)}, bf16[2,2,32,256]{3,2,1,0:T(8,128)(2,1)S(1)}, u32[]{:S(2)}, u32[]{:S(2)}) collective-permute-start(bf16[2,2,32,256]{3,2,1,0:T(8,128)(2,1)S(1)} %get-tuple-element.72), channel_id=1, source_target_pairs={{0,8},{1,9},{2,10},{3,11},{4,12},{5,13},{6,14},{7,15},{8,0},{9,1},... | collective-permute-start | bytes 196616 | tf_op jit(solution)/shard_map/ppermute | solution.py:610
  48.3 9.7 %collective-permute-start.12 = (bf16[2,2,32,256]{3,2,1,0:T(8,128)(2,1)S(1)}, bf16[2,2,32,256]{3,2,1,0:T(8,128)(2,1)S(1)}, u32[]{:S(2)}, u32[]{:S(2)}) collective-permute-start(bf16[2,2,32,256]{3,2,1,0:T(8,128)(2,1)S(1)} %get-tuple-element.73), channel_id=1, source_target_pairs={{0,10},{1,11},{2,8},{3,9},{4,14},{5,15},{6,12},{7,13},{8,2},{9,3},... | collective-permute-start | bytes 196616 | tf_op jit(solution)/shard_map/ppermute | solution.py:610
  49.7 8.2 %collective-permute-start.13 = (bf16[2,2,32,256]{3,2,1,0:T(8,128)(2,1)S(1)}, bf16[2,2,32,256]{3,2,1,0:T(8,128)(2,1)S(1)}, u32[]{:S(2)}, u32[]{:S(2)}) collective-permute-start(bf16[2,2,32,256]{3,2,1,0:T(8,128)(2,1)S(1)} %get-tuple-element.74), channel_id=1, source_target_pairs={{0,12},{1,13},{2,14},{3,15},{4,8},{5,9},{6,10},{7,11},{8,4},{9,5},... | collective-permute-start | bytes 196616 | tf_op jit(solution)/shard_map/ppermute | solution.py:610
  52.1 7.1 %collective-permute-start.14 = (bf16[2,2,32,256]{3,2,1,0:T(8,128)(2,1)S(1)}, bf16[2,2,32,256]{3,2,1,0:T(8,128)(2,1)S(1)}, u32[]{:S(2)}, u32[]{:S(2)}) collective-permute-start(bf16[2,2,32,256]{3,2,1,0:T(8,128)(2,1)S(1)} %get-tuple-element.75), channel_id=1, source_target_pairs={{0,14},{1,15},{2,12},{3,13},{4,10},{5,11},{6,8},{7,9},{8,6},{9,7},... | collective-permute-start | bytes 196616 | tf_op jit(solution)/shard_map/ppermute | solution.py:610
  53.6 5.7 %collective-permute-start.15 = (bf16[2,2,32,256]{3,2,1,0:T(8,128)(2,1)S(1)}, bf16[2,2,32,256]{3,2,1,0:T(8,128)(2,1)S(1)}, u32[]{:S(2)}, u32[]{:S(2)}) collective-permute-start(bf16[2,2,32,256]{3,2,1,0:T(8,128)(2,1)S(1)} %get-tuple-element.76), channel_id=1, source_target_pairs={{0,4},{1,5},{2,6},{3,7},{4,0},{5,1},{6,2},{7,3},{8,12},{9,13},{10,... | collective-permute-start | bytes 196616 | tf_op jit(solution)/shard_map/ppermute | solution.py:610

commit v8 on v7

--- a/solution.py
+++ b/solution.py
@@ -508,7 +508,7 @@
 
 
 IMAGE_ROWS = 8
-PAIR_ORDER = (3, 4, 5, 6, 7, 2, 1)
+PAIR_ORDER = (2, 4, 5, 6, 7, 3, 1)
 
 
 def lag_kernel(lag_ref, *weight_refs):

time: 63.4 us -> 63.8 us (level)
  transfers between devices with their start and end apart: 18 -> 18, of which waited for: 10 -> 9; matrix products, arithmetic and copies ran while one was open for 2% -> 2% of each run, Pallas kernels for 32% -> 31%
where the time goes in v8:
time: 63.8 us; the launch traced here: 63.4 us
  starting transfers between devices  28.6 us (45%)
  Pallas kernels  26.6 us (42%)
  waiting for transfers between devices  6.46 us (10%)
  other arithmetic  1.46 us (2%)
    ppermute x17, starting transfers between devices, swap(): return lax.ppermute(value, 'freq', [(i, i ^ bit) for i in range(ranks)])  23.1 us
    pallas_call x2, Pallas kernels, shards(): pl.pallas_call(functools.partial(image_kernel, scale=scale, depth=depth,...  7.63 us
    ppermute x17, waiting for transfers between devices, swap(): return lax.ppermute(value, 'freq', [(i, i ^ bit) for i in range(ranks)])  6.45 us
    all_to_all x1, starting transfers between devices, exchange(): lax.all_to_all(value, 'freq', split_axis=0, concat_axis=0, tiled=True)  5.5 us
    pallas_call x1, Pallas kernels, shards(): pl.pallas_call(functools.partial(march_kernel, depth=depth), in_specs=[vm...  4.93 us
    pallas_call x1, Pallas kernels, shards(): pl.pallas_call(out_kernel, in_specs=[hbm] * 6, out_specs=[vmem] * 4, out_...  3.74 us
    pallas_call x1, Pallas kernels, shards(): pl.pallas_call(back_kernel, in_specs=[vmem] * 3 + [hbm] * 3, out_specs=[v...  2.98 us
    pallas_call x2, Pallas kernels, mix(): pl.pallas_call(functools.partial(mix_kernel, depth=depth, far=far, last=l...  2.49 us
  transfers between devices with their start and end apart: 18, of which 9 were waited for; matrix products, arithmetic and copies ran while one was open for 2% of the time, Pallas kernels for 31%

profile of v8, /device:TPU:0, one launch (start us, length us, event | category | flops | bytes accessed | tf_op | source)
XLA Modules:
  0.0 63.4 jit_solution(15079269947499893299)
XLA Ops:
  0.0 1.2 %window.1 = (bf16[4,2,64,256]{3,2,1,0:T(8,128)(2,1)S(1)}, bf16[4,2,64,256]{3,2,1,0:T(8,128)(2,1)S(1)}) custom-call(s32[2]{0:T(128)} %map_hbm.1, s32[2]{0:T(128)} %corner_hbm.1, bf16[1,768,512]{2,1,0:T(8,128)(2,1)} %slab_hbm.1), custom_call_target="tpu_custom_call" | custom-call | tf_op jit(solution)/shard_map/window/pallas_call | solution.py:594
  3.3 3.0 %collective-permute-start.2 = (bf16[2,64,256]{2,1,0:T(8,128)(2,1)S(1)}, bf16[2,64,256]{2,1,0:T(8,128)(2,1)S(1)}, u32[]{:S(2)}, u32[]{:S(2)}) collective-permute-start(bf16[2,64,256]{2,1,0:T(8,128)(2,1)S(1)} %get-tuple-element.79), channel_id=1, source_target_pairs={{0,4},{1,5},{2,6},{3,7},{4,0},{5,1},{6,2},{7,3},{8,12},{9,13},{10,... | collective-permute-start | bytes 196616 | tf_op jit(solution)/shard_map/ppermute | solution.py:610
  6.3 1.0 %collective-permute-start.3 = (bf16[2,64,256]{2,1,0:T(8,128)(2,1)S(1)}, bf16[2,64,256]{2,1,0:T(8,128)(2,1)S(1)}, u32[]{:S(2)}, u32[]{:S(2)}) collective-permute-start(bf16[2,64,256]{2,1,0:T(8,128)(2,1)S(1)} %get-tuple-element.80), channel_id=1, source_target_pairs={{0,6},{1,7},{2,4},{3,5},{4,2},{5,3},{6,0},{7,1},{8,14},{9,15},{10,... | collective-permute-start | bytes 196616 | tf_op jit(solution)/shard_map/ppermute | solution.py:610
  7.9 3.7 %out.1 = (f32[4,512,256]{2,1,0:T(8,128)S(1)}, f32[3,512,256]{2,1,0:T(8,128)S(1)}, f32[3,512,256]{2,1,0:T(8,128)S(1)}, f32[8,256]{1,0:T(8,128)S(1)}) custom-call(s32[16]{0:T(128)} %bins_hbm, f32[2,3]{1,0:T(2,128)} %gaps_hbm.1, bf16[2,1,512,256]{3,2,1,0:T(8,128)(2,1)} %source_hbm.1, bf16[2,1,512,256]{3,2,1,0:T(8,128)(2,1)} %receiver_hbm.1, ...), custom_call_target="tpu_custom_call" | custom-call | flops 1073741824 | bytes 4194304 | tf_op jit(solution)/shard_map/out/pallas_call | solution.py:621
  12.4 2.5 %collective-permute-start.4 = (bf16[2,64,256]{2,1,0:T(8,128)(2,1)S(1)}, bf16[2,64,256]{2,1,0:T(8,128)(2,1)S(1)}, u32[]{:S(2)}, u32[]{:S(2)}) collective-permute-start(bf16[2,64,256]{2,1,0:T(8,128)(2,1)S(1)} %bitcast_add_fusion), channel_id=1, source_target_pairs={{0,8},{1,9},{2,10},{3,11},{4,12},{5,13},{6,14},{7,15},{8,0},{9,1},... | collective-permute-start | bytes 196616 | tf_op jit(solution)/shard_map/ppermute | solution.py:610
  14.9 3.0 %back.1 = (bf16[3,4,512,256]{3,2,1,0:T(8,128)(2,1)S(1)}, s32[512,256]{1,0:T(8,128)S(1)}, bf16[256,256]{1,0:T(8,128)(2,1)S(1)}) custom-call(f32[4,512,256]{2,1,0:T(8,128)S(1)} %get-tuple-element.46.spec_ref, f32[3,512,256]{2,1,0:T(8,128)S(1)} %get-tuple-element.47.cos_ref, f32[3,512,256]{2,1,0:T(8,128)S(1)} %get-tuple-element.48.sin_ref, ...), custom_call_target="tpu_custom_call" | custom-call | flops 2147483648 | bytes 4194304 | tf_op jit(solution)/shard_map/back/pallas_call | solution.py:654
  17.9 2.1 %collective-permute-start.7 = (bf16[2,64,256]{2,1,0:T(8,128)(2,1)S(1)}, bf16[2,64,256]{2,1,0:T(8,128)(2,1)S(1)}, u32[]{:S(2)}, u32[]{:S(2)}) collective-permute-start(bf16[2,64,256]{2,1,0:T(8,128)(2,1)S(1)} %add.41), channel_id=1, source_target_pairs={{0,6},{1,7},{2,4},{3,5},{4,2},{5,3},{6,0},{7,1},{8,14},{9,15},{10,... | collective-permute-start | bytes 196616 | tf_op jit(solution)/shard_map/ppermute | solution.py:610
  20.4 1.1 %collective-permute-start.5 = (bf16[2,64,256]{2,1,0:T(8,128)(2,1)S(1)}, bf16[2,64,256]{2,1,0:T(8,128)(2,1)S(1)}, u32[]{:S(2)}, u32[]{:S(2)}) collective-permute-start(bf16[2,64,256]{2,1,0:T(8,128)(2,1)S(1)} %add.41), channel_id=1, source_target_pairs={{0,2},{1,3},{2,0},{3,1},{4,6},{5,7},{6,4},{7,5},{8,10},{9,11},{10,... | collective-permute-start | bytes 196616 | tf_op jit(solution)/shard_map/ppermute | solution.py:610
  21.5 1.0 %unfold.1.refs_1_ = f32[12,512,256]{2,1,0:T(8,128)S(1)} custom-call(bf16[3,4,512,256]{3,2,1,0:T(8,128)(2,1)S(1)} %get-tuple-element.51.returned_ref, bf16[256,256]{1,0:T(8,128)(2,1)S(1)} %get-tuple-element.52.inverse_y), custom_call_target="tpu_custom_call" | custom-call | flops 1073741824 | bytes 1048576 | tf_op jit(solution)/shard_map/unfold/pallas_call | solution.py:678
  23.2 1.0 %collective-permute-done.6 = bf16[2,64,256]{2,1,0:T(8,128)(2,1)S(1)} collective-permute-done((bf16[2,64,256]{2,1,0:T(8,128)(2,1)S(1)}, bf16[2,64,256]{2,1,0:T(8,128)(2,1)S(1)}, u32[]{:S(2)}, u32[]{:S(2)}) %collective-permute-start.6) | collective-permute-done | bytes 65568 | tf_op jit(solution)/shard_map/ppermute | solution.py:610
  26.3 1.6 %far.1 = (bf16[4,256,256]{2,1,0:T(8,128)(2,1)S(1)}, bf16[16,2,32,256]{3,2,1,0:T(8,128)(2,1)}) custom-call(f32[8,256]{1,0:T(8,128)S(1)} %get-tuple-element.40.refs_0_.held_ref, f32[12,512,256]{2,1,0:T(8,128)S(1)} %unfold.1.refs_1_, bf16[4,2,64,256]{3,2,1,0:T(8,128)(2,1)S(1)} %collective-permute-done.8.refs_2_.far_slow, ...), custom_call_target="tpu_custom_call" | custom-call | flops 536870912 | bytes 1048576 | tf_op jit(solution)/shard_map/far/pallas_call | solution.py:703
  28.0 5.5 %all-to-all-start = ((bf16[16,2,32,256]{3,2,1,0:T(8,128)(2,1)}), bf16[16,2,32,256]{3,2,1,0:T(8,128)(2,1)S(1)}, u32[]{:S(2)}, u32[]{:S(2)}) async-start(bf16[16,2,32,256]{3,2,1,0:T(8,128)(2,1)} %get-tuple-element.67), calls=%async_computation | async-start | bytes 1048576 | tf_op jit(solution)/shard_map/all_to_all | solution.py:777
  33.5 4.9 %march.1 = (bf16[3,4,512,256]{3,2,1,0:T(8,128)(2,1)S(1)}, s32[512,256]{1,0:T(8,128)S(1)}) custom-call(f32[8,256]{1,0:T(8,128)S(1)} %get-tuple-element.40.refs_0_.held_ref, bf16[4,256,256]{2,1,0:T(8,128)(2,1)S(1)} %get-tuple-element.59.near_wave, bf16[4,256,256]{2,1,0:T(8,128)(2,1)S(1)} %get-tuple-element.62.far_wave, s32[2,512,256]{2,1,0:T(8,128)} %bracket_hbm.3, ...), custom_call_target="tpu_custom_call" | custom-call | flops 3221225472 | bytes 8388608 | tf_op jit(solution)/shard_map/march/pallas_call | solution.py:725
  38.4 2.3 %mix.1 = bf16[2,8,2,32,256]{4,3,2,1,0:T(8,128)(2,1)S(1)} custom-call(f32[8,256]{1,0:T(8,128)S(1)} %get-tuple-element.40.refs_0_.held_ref, bf16[3,4,512,256]{3,2,1,0:T(8,128)(2,1)S(1)} %get-tuple-element.63.returned_ref, bf16[4,2,64,256]{3,2,1,0:T(8,128)(2,1)S(1)} %pad_maximum_fusion.refs_2_.near_slow, ...), custom_call_target="tpu_custom_call" | custom-call | flops 1073741824 | bytes 1048576 | tf_op jit(solution)/shard_map/mix/pallas_call | solution.py:754
  41.2 1.2 %collective-permute-done.9 = bf16[8,2,32,256]{3,2,1,0:T(8,128)(2,1)S(1)} collective-permute-done((bf16[8,2,32,256]{3,2,1,0:T(8,128)(2,1)S(1)}, bf16[8,2,32,256]{3,2,1,0:T(8,128)(2,1)S(1)}, u32[]{:S(2)}, u32[]{:S(2)}) %collective-permute-start.9) | collective-permute-done | bytes 262176 | tf_op jit(solution)/shard_map/ppermute | solution.py:610
  42.4 1.9 %collective-permute-start.16 = (bf16[2,2,32,256]{3,2,1,0:T(8,128)(2,1)S(1)}, bf16[2,2,32,256]{3,2,1,0:T(8,128)(2,1)S(1)}, u32[]{:S(2)}, u32[]{:S(2)}) collective-permute-start(bf16[2,2,32,256]{3,2,1,0:T(8,128)(2,1)S(1)} %get-tuple-element.69), channel_id=1, source_target_pairs={{0,2},{1,3},{2,0},{3,1},{4,6},{5,7},{6,4},{7,5},{8,10},{9,11},{10,... | collective-permute-start | bytes 196616 | tf_op jit(solution)/shard_map/ppermute | solution.py:610
  44.3 1.5 %collective-permute-start.10 = (bf16[2,2,32,256]{3,2,1,0:T(8,128)(2,1)S(1)}, bf16[2,2,32,256]{3,2,1,0:T(8,128)(2,1)S(1)}, u32[]{:S(2)}, u32[]{:S(2)}) collective-permute-start(bf16[2,2,32,256]{3,2,1,0:T(8,128)(2,1)S(1)} %get-tuple-element.71), channel_id=1, source_target_pairs={{0,4},{1,5},{2,6},{3,7},{4,0},{5,1},{6,2},{7,3},{8,12},{9,13},{10,... | collective-permute-start | bytes 196616 | tf_op jit(solution)/shard_map/ppermute | solution.py:610
  45.8 2.4 %collective-permute-start.11 = (bf16[2,2,32,256]{3,2,1,0:T(8,128)(2,1)S(1)}, bf16[2,2,32,256]{3,2,1,0:T(8,128)(2,1)S(1)}, u32[]{:S(2)}, u32[]{:S(2)}) collective-permute-start(bf16[2,2,32,256]{3,2,1,0:T(8,128)(2,1)S(1)} %get-tuple-element.72), channel_id=1, source_target_pairs={{0,8},{1,9},{2,10},{3,11},{4,12},{5,13},{6,14},{7,15},{8,0},{9,1},... | collective-permute-start | bytes 196616 | tf_op jit(solution)/shard_map/ppermute | solution.py:610
  48.7 2.4 %collective-permute-start.13 = (bf16[2,2,32,256]{3,2,1,0:T(8,128)(2,1)S(1)}, bf16[2,2,32,256]{3,2,1,0:T(8,128)(2,1)S(1)}, u32[]{:S(2)}, u32[]{:S(2)}) collective-permute-start(bf16[2,2,32,256]{3,2,1,0:T(8,128)(2,1)S(1)} %get-tuple-element.74), channel_id=1, source_target_pairs={{0,12},{1,13},{2,14},{3,15},{4,8},{5,9},{6,10},{7,11},{8,4},{9,5},... | collective-permute-start | bytes 196616 | tf_op jit(solution)/shard_map/ppermute | solution.py:610
  51.1 2.4 %collective-permute-start.14 = (bf16[2,2,32,256]{3,2,1,0:T(8,128)(2,1)S(1)}, bf16[2,2,32,256]{3,2,1,0:T(8,128)(2,1)S(1)}, u32[]{:S(2)}, u32[]{:S(2)}) collective-permute-start(bf16[2,2,32,256]{3,2,1,0:T(8,128)(2,1)S(1)} %get-tuple-element.75), channel_id=1, source_target_pairs={{0,14},{1,15},{2,12},{3,13},{4,10},{5,11},{6,8},{7,9},{8,6},{9,7},... | collective-permute-start | bytes 196616 | tf_op jit(solution)/shard_map/ppermute | solution.py:610
  53.9 3.8 %image.2.refs_9_ = f32[2,32,256,256]{3,2,1,0:T(8,128)} custom-call(bf16[16,2,32,256]{3,2,1,0:T(8,128)(2,1)S(1)} %all-to-all-done.refs_0_, bf16[256,2048]{1,0:T(8,128)(2,1)S(1)} %get-tuple-element.68.refs_1_), custom_call_target="tpu_custom_call" | custom-call | tf_op jit(solution)/shard_map/image/pallas_call | solution.py:807
  57.7 0.9 %collective-permute-done.12.refs_3_ = bf16[2,2,32,256]{3,2,1,0:T(8,128)(2,1)S(1)} collective-permute-done((bf16[2,2,32,256]{3,2,1,0:T(8,128)(2,1)S(1)}, bf16[2,2,32,256]{3,2,1,0:T(8,128)(2,1)S(1)}, u32[]{:S(2)}, u32[]{:S(2)}) %collective-permute-start.12) | collective-permute-done | bytes 65568 | tf_op jit(solution)/shard_map/ppermute | solution.py:610
  58.5 0.9 %collective-permute-done.15.refs_6_ = bf16[2,2,32,256]{3,2,1,0:T(8,128)(2,1)S(1)} collective-permute-done((bf16[2,2,32,256]{3,2,1,0:T(8,128)(2,1)S(1)}, bf16[2,2,32,256]{3,2,1,0:T(8,128)(2,1)S(1)}, u32[]{:S(2)}, u32[]{:S(2)}) %collective-permute-start.15) | collective-permute-done | bytes 65568 | tf_op jit(solution)/shard_map/ppermute | solution.py:610
  59.5 3.8 %image.3 = f32[2,32,256,256]{3,2,1,0:T(8,128)} custom-call(bf16[2,2,32,256]{3,2,1,0:T(8,128)(2,1)S(1)} %get-tuple-element.70.refs_0_, bf16[2,2,32,256]{3,2,1,0:T(8,128)(2,1)S(1)} %collective-permute-done.10.refs_1_, bf16[2,2,32,256]{3,2,1,0:T(8,128)(2,1)S(1)} %collective-permute-done.11.refs_2_, ...), custom_call_target="tpu_custom_call", output_to_operand_aliasing={{}: (9, {})} | custom-call | tf_op jit(solution)/shard_map/image/pallas_call | solution.py:807
  (35 shorter events, 8.1 us)
Async XLA Ops:
  1.2 2.0 %collective-permute-start = (bf16[4,2,64,256]{3,2,1,0:T(8,128)(2,1)S(1)}, bf16[4,2,64,256]{3,2,1,0:T(8,128)(2,1)S(1)}, u32[]{:S(2)}, u32[]{:S(2)}) collective-permute-start(bf16[4,2,64,256]{3,2,1,0:T(8,128)(2,1)S(1)} %get-tuple-element.38), channel_id=1, source_target_pairs={{0,1},{1,0},{2,3},{3,2},{4,5},{5,4},{6,7},{7,6},{8,9},{9,8},{10,11... | collective-permute-start | bytes 786440 | tf_op jit(solution)/shard_map/ppermute | solution.py:610
  3.3 8.3 %collective-permute-start.2 = (bf16[2,64,256]{2,1,0:T(8,128)(2,1)S(1)}, bf16[2,64,256]{2,1,0:T(8,128)(2,1)S(1)}, u32[]{:S(2)}, u32[]{:S(2)}) collective-permute-start(bf16[2,64,256]{2,1,0:T(8,128)(2,1)S(1)} %get-tuple-element.79), channel_id=1, source_target_pairs={{0,4},{1,5},{2,6},{3,7},{4,0},{5,1},{6,2},{7,3},{8,12},{9,13},{10,... | collective-permute-start | bytes 196616 | tf_op jit(solution)/shard_map/ppermute | solution.py:610
  6.3 5.3 %collective-permute-start.3 = (bf16[2,64,256]{2,1,0:T(8,128)(2,1)S(1)}, bf16[2,64,256]{2,1,0:T(8,128)(2,1)S(1)}, u32[]{:S(2)}, u32[]{:S(2)}) collective-permute-start(bf16[2,64,256]{2,1,0:T(8,128)(2,1)S(1)} %get-tuple-element.80), channel_id=1, source_target_pairs={{0,6},{1,7},{2,4},{3,5},{4,2},{5,3},{6,0},{7,1},{8,14},{9,15},{10,... | collective-permute-start | bytes 196616 | tf_op jit(solution)/shard_map/ppermute | solution.py:610
  7.4 5.0 %collective-permute-start.1 = (bf16[2,64,256]{2,1,0:T(8,128)(2,1)S(1)}, bf16[2,64,256]{2,1,0:T(8,128)(2,1)S(1)}, u32[]{:S(2)}, u32[]{:S(2)}) collective-permute-start(bf16[2,64,256]{2,1,0:T(8,128)(2,1)S(1)} %get-tuple-element.81), channel_id=1, source_target_pairs={{0,2},{1,3},{2,0},{3,1},{4,6},{5,7},{6,4},{7,5},{8,10},{9,11},{10,... | collective-permute-start | bytes 196616 | tf_op jit(solution)/shard_map/ppermute | solution.py:610
  12.4 5.5 %collective-permute-start.4 = (bf16[2,64,256]{2,1,0:T(8,128)(2,1)S(1)}, bf16[2,64,256]{2,1,0:T(8,128)(2,1)S(1)}, u32[]{:S(2)}, u32[]{:S(2)}) collective-permute-start(bf16[2,64,256]{2,1,0:T(8,128)(2,1)S(1)} %bitcast_add_fusion), channel_id=1, source_target_pairs={{0,8},{1,9},{2,10},{3,11},{4,12},{5,13},{6,14},{7,15},{8,0},{9,1},... | collective-permute-start | bytes 196616 | tf_op jit(solution)/shard_map/ppermute | solution.py:610
  17.9 5.3 %collective-permute-start.7 = (bf16[2,64,256]{2,1,0:T(8,128)(2,1)S(1)}, bf16[2,64,256]{2,1,0:T(8,128)(2,1)S(1)}, u32[]{:S(2)}, u32[]{:S(2)}) collective-permute-start(bf16[2,64,256]{2,1,0:T(8,128)(2,1)S(1)} %add.41), channel_id=1, source_target_pairs={{0,6},{1,7},{2,4},{3,5},{4,2},{5,3},{6,0},{7,1},{8,14},{9,15},{10,... | collective-permute-start | bytes 196616 | tf_op jit(solution)/shard_map/ppermute | solution.py:610
  20.0 4.3 %collective-permute-start.6 = (bf16[2,64,256]{2,1,0:T(8,128)(2,1)S(1)}, bf16[2,64,256]{2,1,0:T(8,128)(2,1)S(1)}, u32[]{:S(2)}, u32[]{:S(2)}) collective-permute-start(bf16[2,64,256]{2,1,0:T(8,128)(2,1)S(1)} %add.41), channel_id=1, source_target_pairs={{0,4},{1,5},{2,6},{3,7},{4,0},{5,1},{6,2},{7,3},{8,12},{9,13},{10,... | collective-permute-start | bytes 196616 | tf_op jit(solution)/shard_map/ppermute | solution.py:610
  20.4 4.3 %collective-permute-start.5 = (bf16[2,64,256]{2,1,0:T(8,128)(2,1)S(1)}, bf16[2,64,256]{2,1,0:T(8,128)(2,1)S(1)}, u32[]{:S(2)}, u32[]{:S(2)}) collective-permute-start(bf16[2,64,256]{2,1,0:T(8,128)(2,1)S(1)} %add.41), channel_id=1, source_target_pairs={{0,2},{1,3},{2,0},{3,1},{4,6},{5,7},{6,4},{7,5},{8,10},{9,11},{10,... | collective-permute-start | bytes 196616 | tf_op jit(solution)/shard_map/ppermute | solution.py:610
  24.7 1.6 %collective-permute-start.8 = (bf16[4,2,64,256]{3,2,1,0:T(8,128)(2,1)S(1)}, bf16[4,2,64,256]{3,2,1,0:T(8,128)(2,1)S(1)}, u32[]{:S(2)}, u32[]{:S(2)}) collective-permute-start(bf16[4,2,64,256]{3,2,1,0:T(8,128)(2,1)S(1)} %pad_maximum_fusion.refs_2_.near_slow), channel_id=1, source_target_pairs={{0,1},{1,0},{2,3},{3,2},{4,5},{5,4},{6,7},{7,6},{8,9},{9,8},{10,11... | collective-permute-start | bytes 786440 | tf_op jit(solution)/shard_map/ppermute | solution.py:610
  28.0 25.9 %all-to-all-start = ((bf16[16,2,32,256]{3,2,1,0:T(8,128)(2,1)}), bf16[16,2,32,256]{3,2,1,0:T(8,128)(2,1)S(1)}, u32[]{:S(2)}, u32[]{:S(2)}) async-start(bf16[16,2,32,256]{3,2,1,0:T(8,128)(2,1)} %get-tuple-element.67), calls=%async_computation | async-start | bytes 1048576 | tf_op jit(solution)/shard_map/all_to_all | solution.py:777
  40.7 1.6 %collective-permute-start.9 = (bf16[8,2,32,256]{3,2,1,0:T(8,128)(2,1)S(1)}, bf16[8,2,32,256]{3,2,1,0:T(8,128)(2,1)S(1)}, u32[]{:S(2)}, u32[]{:S(2)}) collective-permute-start(bf16[8,2,32,256]{3,2,1,0:T(8,128)(2,1)S(1)} %get-tuple-element.78), channel_id=1, source_target_pairs={{0,1},{1,0},{2,3},{3,2},{4,5},{5,4},{6,7},{7,6},{8,9},{9,8},{10,11... | collective-permute-start | bytes 786440 | tf_op jit(solution)/shard_map/ppermute | solution.py:610
  42.4 8.7 %collective-permute-start.16 = (bf16[2,2,32,256]{3,2,1,0:T(8,128)(2,1)S(1)}, bf16[2,2,32,256]{3,2,1,0:T(8,128)(2,1)S(1)}, u32[]{:S(2)}, u32[]{:S(2)}) collective-permute-start(bf16[2,2,32,256]{3,2,1,0:T(8,128)(2,1)S(1)} %get-tuple-element.69), channel_id=1, source_target_pairs={{0,2},{1,3},{2,0},{3,1},{4,6},{5,7},{6,4},{7,5},{8,10},{9,11},{10,... | collective-permute-start | bytes 196616 | tf_op jit(solution)/shard_map/ppermute | solution.py:610
  44.3 9.1 %collective-permute-start.10 = (bf16[2,2,32,256]{3,2,1,0:T(8,128)(2,1)S(1)}, bf16[2,2,32,256]{3,2,1,0:T(8,128)(2,1)S(1)}, u32[]{:S(2)}, u32[]{:S(2)}) collective-permute-start(bf16[2,2,32,256]{3,2,1,0:T(8,128)(2,1)S(1)} %get-tuple-element.71), channel_id=1, source_target_pairs={{0,4},{1,5},{2,6},{3,7},{4,0},{5,1},{6,2},{7,3},{8,12},{9,13},{10,... | collective-permute-start | bytes 196616 | tf_op jit(solution)/shard_map/ppermute | solution.py:610
  45.8 11.9 %collective-permute-start.11 = (bf16[2,2,32,256]{3,2,1,0:T(8,128)(2,1)S(1)}, bf16[2,2,32,256]{3,2,1,0:T(8,128)(2,1)S(1)}, u32[]{:S(2)}, u32[]{:S(2)}) collective-permute-start(bf16[2,2,32,256]{3,2,1,0:T(8,128)(2,1)S(1)} %get-tuple-element.72), channel_id=1, source_target_pairs={{0,8},{1,9},{2,10},{3,11},{4,12},{5,13},{6,14},{7,15},{8,0},{9,1},... | collective-permute-start | bytes 196616 | tf_op jit(solution)/shard_map/ppermute | solution.py:610
  48.2 10.4 %collective-permute-start.12 = (bf16[2,2,32,256]{3,2,1,0:T(8,128)(2,1)S(1)}, bf16[2,2,32,256]{3,2,1,0:T(8,128)(2,1)S(1)}, u32[]{:S(2)}, u32[]{:S(2)}) collective-permute-start(bf16[2,2,32,256]{3,2,1,0:T(8,128)(2,1)S(1)} %get-tuple-element.73), channel_id=1, source_target_pairs={{0,10},{1,11},{2,8},{3,9},{4,14},{5,15},{6,12},{7,13},{8,2},{9,3},... | collective-permute-start | bytes 196616 | tf_op jit(solution)/shard_map/ppermute | solution.py:610
  48.7 9.8 %collective-permute-start.13 = (bf16[2,2,32,256]{3,2,1,0:T(8,128)(2,1)S(1)}, bf16[2,2,32,256]{3,2,1,0:T(8,128)(2,1)S(1)}, u32[]{:S(2)}, u32[]{:S(2)}) collective-permute-start(bf16[2,2,32,256]{3,2,1,0:T(8,128)(2,1)S(1)} %get-tuple-element.74), channel_id=1, source_target_pairs={{0,12},{1,13},{2,14},{3,15},{4,8},{5,9},{6,10},{7,11},{8,4},{9,5},... | collective-permute-start | bytes 196616 | tf_op jit(solution)/shard_map/ppermute | solution.py:610
  51.1 7.4 %collective-permute-start.14 = (bf16[2,2,32,256]{3,2,1,0:T(8,128)(2,1)S(1)}, bf16[2,2,32,256]{3,2,1,0:T(8,128)(2,1)S(1)}, u32[]{:S(2)}, u32[]{:S(2)}) collective-permute-start(bf16[2,2,32,256]{3,2,1,0:T(8,128)(2,1)S(1)} %get-tuple-element.75), channel_id=1, source_target_pairs={{0,14},{1,15},{2,12},{3,13},{4,10},{5,11},{6,8},{7,9},{8,6},{9,7},... | collective-permute-start | bytes 196616 | tf_op jit(solution)/shard_map/ppermute | solution.py:610
  53.5 6.0 %collective-permute-start.15 = (bf16[2,2,32,256]{3,2,1,0:T(8,128)(2,1)S(1)}, bf16[2,2,32,256]{3,2,1,0:T(8,128)(2,1)S(1)}, u32[]{:S(2)}, u32[]{:S(2)}) collective-permute-start(bf16[2,2,32,256]{3,2,1,0:T(8,128)(2,1)S(1)} %get-tuple-element.76), channel_id=1, source_target_pairs={{0,6},{1,7},{2,4},{3,5},{4,2},{5,3},{6,0},{7,1},{8,14},{9,15},{10,... | collective-permute-start | bytes 196616 | tf_op jit(solution)/shard_map/ppermute | solution.py:610
